TPU v7x, 128 devices: a whole 4x4x4 slice. The times are simulated.
128 devices in a mesh: fsdp: 16 (over y, x_lo, core), seq: 8 (over z, x_hi).
Axes of the slice: x: 4 (x_hi: 2, x_lo: 2; x = x_hi * 2 + x_lo), y: 4, z: 4, core: 2. Of those that a mesh axis runs over, the one named last changes fastest.
Arguments:
- hidden: float32 [16, 1024, 1536], P('fsdp', 'seq'), may hold values from -6 to 6
- cotangent: float32 [16, 1024, 1536], P('fsdp', 'seq'), may hold values from -6 to 6
- routes: int32 [16, 1024, 6], P('fsdp', 'seq'), may hold values from 0 to 7, all different within a row
- head_params: float32 [3, 48], replicated, may hold values from -5 to 3.41
- head_first: float32 [3, 48], replicated
- head_second: float32 [3, 48], replicated
- small_params: float32 [22784], P(('fsdp', 'seq')), may hold values from -1.5 to 1.5
- small_first: float32 [22784], P(('fsdp', 'seq'))
- small_second: float32 [22784], P(('fsdp', 'seq'))
- proj_weight: float32 [1536, 6448], P(('fsdp', 'seq')), may hold values from -0.15625 to 0.15625
- proj_first: float32 [1536, 6448], P(('fsdp', 'seq'))
- proj_second: float32 [1536, 6448], P(('fsdp', 'seq'))
- out_weight: float32 [3072, 1536], P(('fsdp', 'seq')), may hold values from -0.109375 to 0.109375
- out_first: float32 [3072, 1536], P(('fsdp', 'seq'))
- out_second: float32 [3072, 1536], P(('fsdp', 'seq'))
- router_weight: float32 [1536, 8], P(('fsdp', 'seq')), may hold values from -0.078125 to 0.078125
- router_first: float32 [1536, 8], P(('fsdp', 'seq'))
- router_second: float32 [1536, 8], P(('fsdp', 'seq'))
- experts_up: float32 [1536, 8, 1024], P('fsdp', 'seq'), may hold values from -0.15625 to 0.15625
- experts_up_first: float32 [1536, 8, 1024], P('fsdp', 'seq')
- experts_up_second: float32 [1536, 8, 1024], P('fsdp', 'seq')
- experts_down: float32 [512, 8, 1536], P('fsdp', 'seq'), may hold values from -1 to 1
- experts_down_first: float32 [512, 8, 1536], P('fsdp', 'seq')
- experts_down_second: float32 [512, 8, 1536], P('fsdp', 'seq')
- shared_up: float32 [1536, 2048], P(('fsdp', 'seq')), may hold values from -0.15625 to 0.15625
- shared_up_first: float32 [1536, 2048], P(('fsdp', 'seq'))
- shared_up_second: float32 [1536, 2048], P(('fsdp', 'seq'))
- shared_down: float32 [1024, 1536], P(('fsdp', 'seq')), may hold values from -0.375 to 0.375
- shared_down_first: float32 [1024, 1536], P(('fsdp', 'seq'))
- shared_down_second: float32 [1024, 1536], P(('fsdp', 'seq'))
Outputs:
- block_out: float32 [16, 1024, 1536], P('fsdp', 'seq')
- hidden_grad: float32 [16, 1024, 1536], P('fsdp', 'seq')
- head_params_new: float32 [3, 48], replicated
- head_first_new: float32 [3, 48], replicated
- head_second_new: float32 [3, 48], replicated
- small_params_new: float32 [22784], P(('fsdp', 'seq'))
- small_first_new: float32 [22784], P(('fsdp', 'seq'))
- small_second_new: float32 [22784], P(('fsdp', 'seq'))
- proj_weight_new: float32 [1536, 6448], P(('fsdp', 'seq'))
- proj_first_new: float32 [1536, 6448], P(('fsdp', 'seq'))
- proj_second_new: float32 [1536, 6448], P(('fsdp', 'seq'))
- out_weight_new: float32 [3072, 1536], P(('fsdp', 'seq'))
- out_first_new: float32 [3072, 1536], P(('fsdp', 'seq'))
- out_second_new: float32 [3072, 1536], P(('fsdp', 'seq'))
- router_weight_new: float32 [1536, 8], P(('fsdp', 'seq'))
- router_first_new: float32 [1536, 8], P(('fsdp', 'seq'))
- router_second_new: float32 [1536, 8], P(('fsdp', 'seq'))
- experts_up_new: float32 [1536, 8, 1024], P('fsdp', 'seq')
- experts_up_first_new: float32 [1536, 8, 1024], P('fsdp', 'seq')
- experts_up_second_new: float32 [1536, 8, 1024], P('fsdp', 'seq')
- experts_down_new: float32 [512, 8, 1536], P('fsdp', 'seq')
- experts_down_first_new: float32 [512, 8, 1536], P('fsdp', 'seq')
- experts_down_second_new: float32 [512, 8, 1536], P('fsdp', 'seq')
- shared_up_new: float32 [1536, 2048], P(('fsdp', 'seq'))
- shared_up_first_new: float32 [1536, 2048], P(('fsdp', 'seq'))
- shared_up_second_new: float32 [1536, 2048], P(('fsdp', 'seq'))
- shared_down_new: float32 [1024, 1536], P(('fsdp', 'seq'))
- shared_down_first_new: float32 [1024, 1536], P(('fsdp', 'seq'))
- shared_down_second_new: float32 [1024, 1536], P(('fsdp', 'seq'))
Inputs may be any that keep to these rules, and one draw needn't show every extreme that they name: `routes`: each position names 6 different experts, and every expert is named somewhere.
All inputs are finite; a program needn't handle non-finite values.
Results may differ from a plain program's by a relative error of at most 0.02.
Values may be sent and summed in bfloat16 or wider, within the bound.
A program may use at most 256 MiB of HBM per device.

v0:
```python
import jax
import jax.numpy as jnp
from jax import lax
from jax.sharding import PartitionSpec as P

D = 1536
HEADS = 48
HDIM = 64
STATE = 128
CONV = 4
FF_EXP = 512
FF_SH = 1024
TOPK = 6
EXPERTS = 8
STEP = 5
INNER = 3072
CHANNELS = 3328


NORM_EPSILON = 1e-05
BETA_FIRST = 0.9
BETA_SECOND = 0.95
ADAM_EPSILON = 1e-08
RATE_MATRIX = 0.04
RATE_DOWN = 0.1
RATE_SMALL = 0.3
RATE_HEAD = 1.0
WEIGHT_DECAY = 0.1
HIGHEST = lax.Precision.HIGHEST


def rms_scale(values, gain_vec):
    return (
        values
        * lax.rsqrt(jnp.mean(values * values, axis=-1, keepdims=True) + NORM_EPSILON)
        * gain_vec
    )


def conv_silu(inputs, kernel, offsets):
    length = inputs.shape[-2]
    kernel_size = kernel.shape[0]
    padded = jnp.pad(inputs, [(0, 0)] * (inputs.ndim - 2) + [(kernel_size - 1, 0), (0, 0)])
    running = offsets
    for offset_index in range(kernel_size):
        running = running + kernel[offset_index] * lax.slice_in_dim(
            padded, offset_index, offset_index + length, axis=inputs.ndim - 2
        )
    return jax.nn.silu(running)


def silu_gate(values, half_width):
    return jax.nn.silu(values[..., :half_width]) * values[..., half_width:]


def route_combine(logit_values, onehot):
    picked = jnp.sum(logit_values[:, None, :] * onehot, axis=-1)
    route_probs = jax.nn.softmax(picked, axis=-1)
    return jnp.sum(route_probs[:, :, None] * onehot, axis=1)


def split_small(small_vec):
    cut_three = 2 * D + INNER
    cut_four = cut_three + CHANNELS
    return (
        small_vec[:D],
        small_vec[D : 2 * D],
        small_vec[2 * D : cut_three],
        small_vec[cut_three:cut_four],
        small_vec[cut_four:].reshape(CONV, CHANNELS),
    )


def adam_update(weight, old_first, old_second, gradient, step_rate, decay_rate):
    first_new = BETA_FIRST * old_first + (1.0 - BETA_FIRST) * gradient
    second_new = BETA_SECOND * old_second + (1.0 - BETA_SECOND) * gradient * gradient
    first_hat = first_new / (1.0 - BETA_FIRST**STEP)
    second_hat = second_new / (1.0 - BETA_SECOND**STEP)
    weight_new = weight - step_rate * (
        first_hat / (jnp.sqrt(second_hat) + ADAM_EPSILON) + decay_rate * weight
    )
    return (weight_new, first_new, second_new)


def local(
    hidden,
    cotangent,
    routes,
    head_params,
    head_first,
    head_second,
    small_params,
    small_first,
    small_second,
    proj_weight,
    proj_first,
    proj_second,
    out_weight,
    out_first,
    out_second,
    router_weight,
    router_first,
    router_second,
    experts_up,
    experts_up_first,
    experts_up_second,
    experts_down,
    experts_down_first,
    experts_down_second,
    shared_up,
    shared_up_first,
    shared_up_second,
    shared_down,
    shared_down_first,
    shared_down_second,
):
    groups = lax.axis_size("seq")
    group_index = lax.axis_index("seq")
    seq_count, piece_len, model_width = hidden.shape
    row_count = seq_count * piece_len
    full_len = piece_len * groups
    heads_here = HEADS // groups
    inner_here = heads_here * HDIM
    experts_here = EXPERTS // groups
    dense_low = (
        proj_weight.astype(jnp.bfloat16),
        out_weight.astype(jnp.bfloat16),
        small_params.astype(jnp.bfloat16),
        router_weight.astype(jnp.bfloat16),
        shared_up.astype(jnp.bfloat16),
        shared_down.astype(jnp.bfloat16),
    )
    proj_full, out_full, small_full, router_full, shared_up_full, shared_down_full = (
        lax.all_gather(dense_low[0], ("fsdp", "seq"), axis=0, tiled=True),
        lax.all_gather(dense_low[1], ("fsdp", "seq"), axis=0, tiled=True),
        lax.all_gather(dense_low[2], ("fsdp", "seq"), axis=0, tiled=True),
        lax.all_gather(dense_low[3], ("fsdp", "seq"), axis=0, tiled=True),
        lax.all_gather(dense_low[4], ("fsdp", "seq"), axis=0, tiled=True),
        lax.all_gather(dense_low[5], ("fsdp", "seq"), axis=0, tiled=True),
    )
    small_vec = small_full.astype(jnp.float32)
    gain_first, gain_second, gain_mixer, conv_bias, conv_kernel = split_small(small_vec)
    inputs = hidden.reshape(row_count, model_width)
    normed = rms_scale(inputs, gain_first).astype(jnp.bfloat16)
    projected = jnp.dot(normed, proj_full, preferred_element_type=jnp.float32).astype(jnp.bfloat16)
    projected = projected.reshape(seq_count, piece_len, -1)
    gate_and_x = projected[:, :, : 2 * INNER].reshape(seq_count, piece_len, 2, INNER)
    rate_raw = projected[:, :, INNER + CHANNELS :].reshape(seq_count, piece_len, 1, HEADS)
    state_cols = projected[:, :, 2 * INNER : INNER + CHANNELS]
    state_copies = jnp.tile(state_cols[:, :, None, :], (1, 1, 1, groups))
    heads_zx, heads_rate, full_state = (
        lax.all_to_all(gate_and_x, "seq", split_axis=3, concat_axis=1, tiled=True),
        lax.all_to_all(rate_raw, "seq", split_axis=3, concat_axis=1, tiled=True),
        lax.all_to_all(state_copies, "seq", split_axis=3, concat_axis=1, tiled=True),
    )
    full_state = full_state[:, :, 0, :]
    head_local = lax.dynamic_slice_in_dim(head_params, group_index * heads_here, heads_here, 1)
    x_kernel = lax.dynamic_slice_in_dim(conv_kernel, group_index * inner_here, inner_here, 1)
    x_bias = lax.dynamic_slice_in_dim(conv_bias, group_index * inner_here, inner_here, 0)
    state_kernel = conv_kernel[:, INNER:]
    state_bias = conv_bias[INNER:]
    gate_z = heads_zx[:, :, 0, :].astype(jnp.float32)
    x_raw = heads_zx[:, :, 1, :].astype(jnp.float32)
    x_act = conv_silu(x_raw, x_kernel, x_bias).astype(jnp.bfloat16)
    state_raw = full_state.astype(jnp.float32)
    state_act = conv_silu(state_raw, state_kernel, state_bias).astype(jnp.bfloat16)
    b_state = state_act[..., :STATE]
    c_state = state_act[..., STATE:]
    rate_in = heads_rate[:, :, 0, :].astype(jnp.float32)
    step_sizes = jax.nn.softplus(rate_in + head_local[0])
    decay_head = -jnp.exp(head_local[1])
    cumulative = jnp.cumsum(step_sizes * decay_head, axis=1)
    lower_mask = jnp.tril(jnp.ones((full_len, full_len), dtype=bool))
    x_split = x_act.reshape(seq_count, full_len, heads_here, HDIM)

    def decay_weights(scores, cum_seq, sizes_seq):
        cum_heads = cum_seq.T
        decay_matrix = jnp.exp(
            jnp.where(lower_mask, cum_heads[:, :, None] - cum_heads[:, None, :], 0.0)
        )
        weight_matrix = jnp.where(lower_mask, scores * decay_matrix, 0.0) * sizes_seq.T[:, None, :]
        return (decay_matrix, weight_matrix)

    def forward_seq(operands):
        b_seq, c_seq, cum_seq, sizes_seq, x_seq = operands
        scores = jnp.einsum("tn,sn->ts", c_seq, b_seq, preferred_element_type=jnp.float32)
        decay_matrix, weight_matrix = decay_weights(scores, cum_seq, sizes_seq)
        return jnp.einsum(
            "hts,shp->thp",
            weight_matrix.astype(jnp.bfloat16),
            x_seq,
            preferred_element_type=jnp.float32,
        )

    mixed_mat = lax.map(forward_seq, (b_state, c_state, cumulative, step_sizes, x_split))
    mixed_out = mixed_mat + x_split.astype(jnp.float32) * head_local[2][:, None]
    mixed_out = mixed_out.reshape(seq_count, full_len, inner_here)
    gated_out = (mixed_out * jax.nn.silu(gate_z)).astype(jnp.bfloat16)
    gated_pieces = lax.all_to_all(gated_out, "seq", split_axis=1, concat_axis=2, tiled=True)
    gated_rows = gated_pieces.reshape(row_count, INNER).astype(jnp.float32)
    gated_normed = rms_scale(gated_rows, gain_mixer).astype(jnp.bfloat16)
    mixer_out = jnp.dot(gated_normed, out_full, preferred_element_type=jnp.float32)
    middle = inputs + mixer_out
    up_cols, down_cols = (
        lax.all_gather(experts_up.astype(jnp.bfloat16), "fsdp", axis=0, tiled=True),
        lax.all_gather(experts_down.astype(jnp.bfloat16), "fsdp", axis=0, tiled=True),
    )
    normed_two = rms_scale(middle, gain_second).astype(jnp.bfloat16)
    logits = jnp.dot(normed_two, router_full, preferred_element_type=jnp.float32)
    onehot = (
        routes.reshape(row_count, TOPK)[:, :, None] == jnp.arange(EXPERTS, dtype=jnp.int32)
    ).astype(jnp.float32)
    combine = route_combine(logits, onehot)
    out_grad = cotangent.reshape(row_count, model_width)
    up_use, down_use = (up_cols, down_cols)
    rows_normed = lax.all_gather(
        normed_two.reshape(seq_count, piece_len, model_width), "seq", axis=1, tiled=True
    ).reshape(-1, model_width)
    group_combine, group_cot = (
        lax.all_gather(
            combine.reshape(seq_count, piece_len, EXPERTS).astype(jnp.bfloat16),
            "seq",
            axis=1,
            tiled=True,
        ).astype(jnp.float32),
        lax.all_gather(cotangent.astype(jnp.bfloat16), "seq", axis=1, tiled=True).astype(
            cotangent.dtype
        ),
    )
    rows_combine = lax.dynamic_slice_in_dim(
        group_combine.reshape(-1, EXPERTS), group_index * experts_here, experts_here, 1
    )
    rows_cot = group_cot.reshape(-1, model_width)
    expert_gu = jnp.einsum("td,def->etf", rows_normed, up_use, preferred_element_type=jnp.float32)
    expert_act = silu_gate(expert_gu, FF_EXP).astype(jnp.bfloat16)
    expert_out = jnp.einsum(
        "etf,fed->etd", expert_act, down_use, preferred_element_type=jnp.float32
    )
    routed_part = jnp.sum(rows_combine.T[:, :, None] * expert_out, axis=0)
    routed = (
        lax.psum_scatter(
            routed_part.reshape(seq_count, full_len, model_width).astype(jnp.bfloat16),
            "seq",
            scatter_dimension=1,
            tiled=True,
        )
        .astype(jnp.float32)
        .reshape(row_count, model_width)
    )
    shared_gu = jnp.dot(normed_two, shared_up_full, preferred_element_type=jnp.float32)
    shared_act = silu_gate(shared_gu, FF_SH).astype(jnp.bfloat16)
    shared_out = jnp.dot(shared_act, shared_down_full, preferred_element_type=jnp.float32)
    block_out = middle + routed + shared_out
    shared_out_grad = out_grad.astype(jnp.bfloat16)
    shared_act_grad = jnp.einsum(
        "td,fd->tf", shared_out_grad, shared_down_full, preferred_element_type=jnp.float32
    )
    shared_down_grad = jnp.einsum(
        "tf,td->fd", shared_act, shared_out_grad, preferred_element_type=jnp.float32
    )
    shared_pull = jax.vjp(lambda values: silu_gate(values, FF_SH), shared_gu)[1]
    shared_gu_grad = shared_pull(shared_act_grad)[0].astype(jnp.bfloat16)
    normed_two_grad = jnp.einsum(
        "tf,df->td", shared_gu_grad, shared_up_full, preferred_element_type=jnp.float32
    )
    shared_up_grad = jnp.einsum(
        "td,tf->df", normed_two, shared_gu_grad, preferred_element_type=jnp.float32
    )
    expert_out_grad = (rows_combine.T[:, :, None] * rows_cot[None]).astype(jnp.bfloat16)
    expert_act_grad = jnp.einsum(
        "etd,fed->etf", expert_out_grad, down_use, preferred_element_type=jnp.float32
    )
    experts_down_grad = jnp.einsum(
        "etf,etd->fed", expert_act, expert_out_grad, preferred_element_type=jnp.float32
    )
    expert_pull = jax.vjp(lambda values: silu_gate(values, FF_EXP), expert_gu)[1]
    expert_gu_grad = expert_pull(expert_act_grad)[0].astype(jnp.bfloat16)
    rows_input_grad = jnp.einsum(
        "etf,def->td", expert_gu_grad, up_use, preferred_element_type=jnp.float32
    )
    experts_up_grad = jnp.einsum(
        "td,etf->def", rows_normed, expert_gu_grad, preferred_element_type=jnp.float32
    )
    combine_part = jnp.sum(expert_out * rows_cot[None], axis=2).T
    combine_wide = lax.dynamic_update_slice_in_dim(
        jnp.zeros((combine_part.shape[0], EXPERTS), jnp.float32),
        combine_part,
        group_index * experts_here,
        1,
    )
    back_input, back_combine = (
        lax.psum_scatter(
            rows_input_grad.reshape(seq_count, full_len, model_width).astype(jnp.bfloat16),
            "seq",
            scatter_dimension=1,
            tiled=True,
        ).astype(jnp.float32),
        lax.psum_scatter(
            combine_wide.reshape(seq_count, full_len, EXPERTS).astype(jnp.bfloat16),
            "seq",
            scatter_dimension=1,
            tiled=True,
        ).astype(jnp.float32),
    )
    normed_two_grad = normed_two_grad + back_input.reshape(row_count, model_width)
    combine_grad = back_combine.reshape(row_count, EXPERTS)
    up_part, down_part = (experts_up_grad, experts_down_grad)
    up_sum, down_sum = (
        lax.psum_scatter(
            up_part.astype(jnp.bfloat16), "fsdp", scatter_dimension=0, tiled=True
        ).astype(jnp.float32),
        lax.psum_scatter(
            down_part.astype(jnp.bfloat16), "fsdp", scatter_dimension=0, tiled=True
        ).astype(jnp.float32),
    )
    route_pull = jax.vjp(lambda values: route_combine(values, onehot), logits)[1]
    logits_grad = route_pull(combine_grad)[0].astype(jnp.bfloat16)
    normed_two_grad = normed_two_grad + jnp.einsum(
        "te,de->td", logits_grad, router_full, preferred_element_type=jnp.float32
    )
    router_grad = jnp.einsum(
        "td,te->de", normed_two, logits_grad, preferred_element_type=jnp.float32
    )
    norm_two_pull = jax.vjp(rms_scale, middle, gain_second)[1]
    middle_from_norm, gain_second_grad = norm_two_pull(normed_two_grad)
    middle_grad = out_grad + middle_from_norm
    mixer_out_grad = middle_grad.astype(jnp.bfloat16)
    gated_normed_grad = jnp.einsum(
        "td,id->ti", mixer_out_grad, out_full, preferred_element_type=jnp.float32
    )
    out_weight_grad = jnp.einsum(
        "ti,td->id", gated_normed, mixer_out_grad, preferred_element_type=jnp.float32
    )
    mixer_norm_pull = jax.vjp(rms_scale, gated_rows, gain_mixer)[1]
    gated_grad, gain_mixer_grad = mixer_norm_pull(gated_normed_grad)
    gated_grad = gated_grad.astype(jnp.bfloat16).reshape(seq_count, piece_len, INNER)
    heads_gated_grad = lax.all_to_all(
        gated_grad, "seq", split_axis=2, concat_axis=1, tiled=True
    ).astype(jnp.float32)
    gate_pull = jax.vjp(
        lambda mixed_in, gate_in: mixed_in * jax.nn.silu(gate_in), mixed_out, gate_z
    )[1]
    mixed_grad, gate_z_grad = gate_pull(heads_gated_grad)
    mixed_grad = mixed_grad.reshape(seq_count, full_len, heads_here, HDIM)
    skip_grad = jnp.sum(mixed_grad * x_split.astype(jnp.float32), axis=(0, 1, 3))
    mixed_low = mixed_grad.astype(jnp.bfloat16)

    def backward_seq(operands):
        b_seq, c_seq, cum_seq, sizes_seq, x_seq, grad_seq = operands
        scores = jnp.einsum("tn,sn->ts", c_seq, b_seq, preferred_element_type=jnp.float32)
        decay_matrix, weight_matrix = decay_weights(scores, cum_seq, sizes_seq)
        x_grad = jnp.einsum(
            "hts,thp->shp",
            weight_matrix.astype(jnp.bfloat16),
            grad_seq,
            preferred_element_type=jnp.float32,
        )
        weight_grad = jnp.where(
            lower_mask,
            jnp.einsum("thp,shp->hts", grad_seq, x_seq, preferred_element_type=jnp.float32),
            0.0,
        )
        scaled = weight_grad * decay_matrix
        product = scaled * scores
        size_direct = jnp.sum(product, axis=1)
        cum_terms = product * sizes_seq.T[:, None, :]
        cum_grad = jnp.sum(cum_terms, axis=2) - jnp.sum(cum_terms, axis=1)
        scores_grad = jnp.sum(scaled * sizes_seq.T[:, None, :], axis=0)
        c_grad = jnp.einsum("ts,sn->tn", scores_grad, b_seq.astype(jnp.float32), precision=HIGHEST)
        b_grad = jnp.einsum("ts,tn->sn", scores_grad, c_seq.astype(jnp.float32), precision=HIGHEST)
        return (x_grad, size_direct.T, cum_grad.T, jnp.concatenate([b_grad, c_grad], axis=-1))

    x_mix_grad, size_direct, cum_grad, state_grad = lax.map(
        backward_seq, (b_state, c_state, cumulative, step_sizes, x_split, mixed_low)
    )
    x_total_grad = x_mix_grad + mixed_grad * head_local[2][:, None]
    cum_back = jnp.flip(jnp.cumsum(jnp.flip(cum_grad, 1), axis=1), 1)
    size_grad = size_direct + cum_back * decay_head
    log_decay_grad = jnp.sum(cum_back * step_sizes * decay_head, axis=(0, 1))
    softplus_pull = jax.vjp(
        lambda raw_rate, offset: jax.nn.softplus(raw_rate + offset), rate_in, head_local[0]
    )[1]
    rate_raw_grad, bias_grad = softplus_pull(size_grad)
    x_conv_pull = jax.vjp(conv_silu, x_raw, x_kernel, x_bias)[1]
    x_raw_grad, x_kernel_grad, x_bias_grad = x_conv_pull(
        x_total_grad.reshape(seq_count, full_len, inner_here)
    )
    state_conv_pull = jax.vjp(conv_silu, state_raw, state_kernel, state_bias)[1]
    state_raw_grad, state_kernel_grad, state_bias_grad = state_conv_pull(state_grad)
    zx_grad = jnp.stack([gate_z_grad, x_raw_grad], axis=2).astype(jnp.bfloat16)
    rate_back = rate_raw_grad.astype(jnp.bfloat16)[:, :, None, :]
    piece_zx_grad, piece_rate_grad = (
        lax.all_to_all(zx_grad, "seq", split_axis=1, concat_axis=3, tiled=True),
        lax.all_to_all(rate_back, "seq", split_axis=1, concat_axis=3, tiled=True),
    )
    piece_state_grad = lax.psum_scatter(
        state_raw_grad.astype(jnp.bfloat16), "seq", scatter_dimension=1, tiled=True
    )
    proj_grad = jnp.concatenate(
        [
            piece_zx_grad.reshape(seq_count, piece_len, 2 * INNER),
            piece_state_grad,
            piece_rate_grad.reshape(seq_count, piece_len, HEADS),
        ],
        axis=-1,
    ).reshape(row_count, -1)
    normed_grad = jnp.einsum("tc,dc->td", proj_grad, proj_full, preferred_element_type=jnp.float32)
    proj_weight_grad = jnp.einsum(
        "td,tc->dc", normed, proj_grad, preferred_element_type=jnp.float32
    )
    norm_one_pull = jax.vjp(rms_scale, inputs, gain_first)[1]
    input_from_norm, gain_first_grad = norm_one_pull(normed_grad)
    hidden_grad = (middle_grad + input_from_norm).reshape(hidden.shape)
    kernel_full = jnp.concatenate(
        [jnp.zeros((CONV, INNER), jnp.float32), state_kernel_grad], axis=1
    )
    kernel_full = lax.dynamic_update_slice_in_dim(
        kernel_full, x_kernel_grad, group_index * inner_here, 1
    )
    bias_full = jnp.concatenate([jnp.zeros((INNER,), jnp.float32), state_bias_grad])
    bias_full = lax.dynamic_update_slice_in_dim(bias_full, x_bias_grad, group_index * inner_here, 0)
    small_grad = jnp.concatenate(
        [gain_first_grad, gain_second_grad, gain_mixer_grad, bias_full, kernel_full.reshape(-1)]
    )
    proj_sum, out_sum, small_sum, router_sum, shared_up_sum, shared_down_sum = (
        lax.psum_scatter(proj_weight_grad, ("fsdp", "seq"), scatter_dimension=0, tiled=True),
        lax.psum_scatter(out_weight_grad, ("fsdp", "seq"), scatter_dimension=0, tiled=True),
        lax.psum_scatter(small_grad, ("fsdp", "seq"), scatter_dimension=0, tiled=True),
        lax.psum_scatter(router_grad, ("fsdp", "seq"), scatter_dimension=0, tiled=True),
        lax.psum_scatter(shared_up_grad, ("fsdp", "seq"), scatter_dimension=0, tiled=True),
        lax.psum_scatter(shared_down_grad, ("fsdp", "seq"), scatter_dimension=0, tiled=True),
    )
    head_grad_local = jnp.stack([bias_grad, log_decay_grad, skip_grad])
    head_grad = lax.dynamic_update_slice_in_dim(
        jnp.zeros((3, HEADS), jnp.float32), head_grad_local, group_index * heads_here, 1
    )
    head_sum = lax.psum(head_grad, ("fsdp", "seq"))
    head_new = adam_update(head_params, head_first, head_second, head_sum, RATE_HEAD, 0.0)
    small_new = adam_update(small_params, small_first, small_second, small_sum, RATE_SMALL, 0.0)
    proj_new = adam_update(
        proj_weight, proj_first, proj_second, proj_sum, RATE_MATRIX, WEIGHT_DECAY
    )
    out_new = adam_update(out_weight, out_first, out_second, out_sum, RATE_MATRIX, WEIGHT_DECAY)
    router_new = adam_update(
        router_weight, router_first, router_second, router_sum, RATE_MATRIX, WEIGHT_DECAY
    )
    up_new = adam_update(
        experts_up, experts_up_first, experts_up_second, up_sum, RATE_MATRIX, WEIGHT_DECAY
    )
    down_new = adam_update(
        experts_down, experts_down_first, experts_down_second, down_sum, RATE_DOWN, WEIGHT_DECAY
    )
    shared_up_new = adam_update(
        shared_up, shared_up_first, shared_up_second, shared_up_sum, RATE_MATRIX, WEIGHT_DECAY
    )
    shared_down_new = adam_update(
        shared_down,
        shared_down_first,
        shared_down_second,
        shared_down_sum,
        RATE_MATRIX,
        WEIGHT_DECAY,
    )
    return (
        block_out.reshape(hidden.shape),
        hidden_grad,
        head_new[0],
        head_new[1],
        head_new[2],
        small_new[0],
        small_new[1],
        small_new[2],
        proj_new[0],
        proj_new[1],
        proj_new[2],
        out_new[0],
        out_new[1],
        out_new[2],
        router_new[0],
        router_new[1],
        router_new[2],
        up_new[0],
        up_new[1],
        up_new[2],
        down_new[0],
        down_new[1],
        down_new[2],
        shared_up_new[0],
        shared_up_new[1],
        shared_up_new[2],
        shared_down_new[0],
        shared_down_new[1],
        shared_down_new[2],
    )


def solution(mesh):
    return jax.shard_map(
        local,
        mesh=mesh,
        in_specs=(
            P("fsdp", "seq", None),
            P("fsdp", "seq", None),
            P("fsdp", "seq", None),
            P(),
            P(),
            P(),
            P(("fsdp", "seq")),
            P(("fsdp", "seq")),
            P(("fsdp", "seq")),
            P(("fsdp", "seq"), None),
            P(("fsdp", "seq"), None),
            P(("fsdp", "seq"), None),
            P(("fsdp", "seq"), None),
            P(("fsdp", "seq"), None),
            P(("fsdp", "seq"), None),
            P(("fsdp", "seq"), None),
            P(("fsdp", "seq"), None),
            P(("fsdp", "seq"), None),
            P("fsdp", "seq", None),
            P("fsdp", "seq", None),
            P("fsdp", "seq", None),
            P("fsdp", "seq", None),
            P("fsdp", "seq", None),
            P("fsdp", "seq", None),
            P(("fsdp", "seq"), None),
            P(("fsdp", "seq"), None),
            P(("fsdp", "seq"), None),
            P(("fsdp", "seq"), None),
            P(("fsdp", "seq"), None),
            P(("fsdp", "seq"), None),
        ),
        out_specs=(
            P("fsdp", "seq", None),
            P("fsdp", "seq", None),
            P(),
            P(),
            P(),
            P(("fsdp", "seq")),
            P(("fsdp", "seq")),
            P(("fsdp", "seq")),
            P(("fsdp", "seq"), None),
            P(("fsdp", "seq"), None),
            P(("fsdp", "seq"), None),
            P(("fsdp", "seq"), None),
            P(("fsdp", "seq"), None),
            P(("fsdp", "seq"), None),
            P(("fsdp", "seq"), None),
            P(("fsdp", "seq"), None),
            P(("fsdp", "seq"), None),
            P("fsdp", "seq", None),
            P("fsdp", "seq", None),
            P("fsdp", "seq", None),
            P("fsdp", "seq", None),
            P("fsdp", "seq", None),
            P("fsdp", "seq", None),
            P(("fsdp", "seq"), None),
            P(("fsdp", "seq"), None),
            P(("fsdp", "seq"), None),
            P(("fsdp", "seq"), None),
            P(("fsdp", "seq"), None),
            P(("fsdp", "seq"), None),
        ),
        check_vma=False,
    )
```

profile of v0, /device:TPU:1, one launch (start us, length us, event | category | flops | bytes accessed | tf_op | source)
XLA Modules:
  0.0 4897.6 jit_solution(10716099614205532987)
XLA Ops:
  12.8 69.4 %all-reduce.24 = bf16[22784]{0:T(1024)(128)(2,1)S(1)} all-reduce(bf16[22784]{0:T(1024)(128)(2,1)S(1)} %dynamic-update-slice), channel_id=1, replica_groups=mesh['fsdp'=16,'seq'=8] {'fsdp','seq'}, use_global_device_ids=true, to_apply=%add.24 | all-reduce | flops 22784 | bytes 91136
  86.8 268.0 %all-gather.26.cloned.1.call-done = bf16[128,12,6448]{2,1,0:T(8,128)(2,1)} async-done(((bf16[1,12,6448]{2,1,0:T(8,128)(2,1)}), bf16[128,12,6448]{2,1,0:T(8,128)(2,1)}) %all-gather.26.cloned.1.call-update) | async-done | bytes 19808272 | tf_op jit(solution)/shard_map/all_gather | solution.py:134
  354.8 29.5 reshape.1078
  384.3 12.1 fusion.4
  407.8 13.8 copy.282
  421.6 8.1 copy.420
  429.8 11.8 reduce.32
  442.5 6.6 all-to-all-start.1
  453.0 8.0 all-to-all-done.1
  473.2 15.5 all-to-all-done
  497.4 11.5 bitcast_add_fusion.1
  525.3 12.8 all-to-all-done.3
  544.8 149.2 %all-gather.14.cloned.1.call-done = bf16[3072,1536]{1,0:T(8,128)(2,1)} async-done(((bf16[24,1536]{1,0:T(8,128)(2,1)}), bf16[3072,1536]{1,0:T(8,128)(2,1)}) %all-gather.14.cloned.1.call-update) | async-done | bytes 9437200 | tf_op jit(solution)/shard_map/all_gather | solution.py:135
  702.0 33.4 all-gather.16.cloned.1.call-done
  735.4 64.8 %all-gather.24.cloned.1.call-done = bf16[1024,1536]{1,0:T(8,128)(2,1)} async-done(((bf16[128,1536]{1,0:T(8,128)(2,1)}), bf16[1024,1536]{1,0:T(8,128)(2,1)}) %all-gather.24.cloned.1.call-update) | async-done | bytes 3145744 | tf_op jit(solution)/shard_map/all_gather | solution.py:216
  810.2 24.0 all-gather.18.cloned.1.call-done
  834.2 64.9 %all-gather.22.cloned.1.call-done = bf16[1,1024,1536]{2,1,0:T(8,128)(2,1)} async-done(((bf16[1,128,1536]{2,1,0:T(8,128)(2,1)}), bf16[1,1024,1536]{2,1,0:T(8,128)(2,1)}) %all-gather.22.cloned.1.call-update) | async-done | bytes 3145744 | tf_op jit(solution)/shard_map/all_gather | solution.py:226
  899.1 7.7 fusion.6
  916.7 304.7 %all-gather.3 = bf16[128,12,8]{1,2,0:T(8,128)(2,1)S(1)} all-gather(bf16[1,12,8]{1,2,0:T(8,128)(2,1)S(1)} %convert_bitcast_fusion.4), channel_id=1, replica_groups=mesh['fsdp'=16,'seq'=8] {'fsdp','seq'}, dimensions={0}, use_global_device_ids=true | all-gather | bytes 24768 | tf_op jit(solution)/shard_map/all_gather | solution.py:137
  1232.6 37.7 all-gather
  1283.6 12.9 all-gather.28.cloned.1.call-done
  1296.6 10.7 reshape.1082
  1312.1 292.0 %all-gather.20.cloned.1.call-done = bf16[1024,1536]{1,0:T(8,128)(2,1)} async-done(((bf16[8,1536]{1,0:T(8,128)(2,1)}), bf16[1024,1536]{1,0:T(8,128)(2,1)}) %all-gather.20.cloned.1.call-update) | async-done | bytes 3145744 | tf_op jit(solution)/shard_map/all_gather | solution.py:139
  1608.5 78.6 %reduce-scatter.19.cloned.1.call-done = bf16[1,128,1536]{2,1,0:T(8,128)(2,1)} async-done(((bf16[1,1024,1536]{2,1,0:T(8,128)(2,1)}), bf16[1,128,1536]{2,1,0:T(8,128)(2,1)}) %reduce-scatter.19.cloned.1.call-update) | async-done | bytes 393232 | tf_op jit(solution)/shard_map/reduce_scatter | solution.py:292
  1694.2 7.8 multiply_reduce_fusion.8
  1707.1 17.9 reduce.34
  1733.8 10.9 all-to-all-done.4
  1758.3 17.6 multiply_reduce_fusion.1
  1792.5 8.5 copy.322
  1801.1 8.4 fusion.8
  1842.0 13.9 bitcast_add_fusion
  1870.2 6.6 all-to-all-start.5
  1895.4 12.8 all-to-all-done.5
  1912.2 11.9 multiply_reduce_fusion.17
  1930.2 8.0 fusion.78
  1945.8 557.9 %fusion.1 = f32[16,2048]{1,0:T(8,128)} fusion(f32[1536,2048]{1,0:T(8,128)} %fusion.84), kind=kCustom, calls=%all-reduce-scatter.1 | all-reduce-scatter fusion | flops 4194305 | bytes 12713984
  2508.6 8.3 collective-permute-start.61
  2521.9 15.7 collective-permute-start.59
  2550.3 8.9 collective-permute-done.57
  2580.6 7.2 collective-permute-start.44
  2587.8 9.4 collective-permute-start.43
  2597.2 8.5 collective-permute-start.42
  2620.3 7.7 collective-permute-start.35
  2643.3 55.3 %concatenate.31 = f32[524,2048]{1,0:T(8,128)} concatenate(f32[12,2048]{1,0:T(8,128)} %collective-permute-done.63, f32[16,2048]{1,0:T(8,128)} %collective-permute-done.62, f32[16,2048]{1,0:T(8,128)} %collective-permute-done.61, f32[16,2048]{1,0:T(8,128)} %collective-permute-done.60, f32[16,2048]{1,0:T(8,128)} %collective-permute-done.59, f32[16,2048]{1,0:T(8,128)} %collective-permute-done.58, ...), dimensions={0} | concatenate | bytes 8585216
  2700.6 16.6 fusion.53
  2717.2 1163.7 %fusion = f32[16,6448]{1,0:T(8,128)S(1)} fusion(f32[1536,6448]{1,0:T(8,128)} %fusion.53), kind=kCustom, calls=%all-reduce-scatter | all-reduce-scatter fusion | flops 13205505 | bytes 40029184
  3881.6 13.4 collective-permute-start.30
  3898.5 14.1 collective-permute-start.29
  3912.6 13.7 collective-permute-start.28
  3926.2 24.9 collective-permute-start.27
  3951.1 17.2 collective-permute-start.26
  3973.6 21.5 collective-permute-start.24
  4013.1 23.3 collective-permute-start.19
  4038.5 26.1 collective-permute-start.17
  4070.6 92.2 %all-reduce.32 = (f32[3,48]{1,0:T(4,128)S(1)}, f32[1536,8]{0,1:T(8,128)S(1)}) all-reduce(f32[3,48]{1,0:T(4,128)S(1)} %dynamic_update_slice.27, f32[1536,8]{0,1:T(8,128)S(1)} %fusion.139), channel_id=1, replica_groups=mesh['fsdp'=16,'seq'=8] {'fsdp','seq'}, use_global_device_ids=true, to_apply=%region_31.32 | all-reduce | flops 12432 | bytes 99456 | tf_op jit(solution)/shard_map/psum | solution.py:437
  4181.2 13.5 collective-permute-done.14
  4196.8 23.0 collective-permute-start.8
  4231.4 6.7 collective-permute-start.4
  4238.1 27.9 collective-permute-done.8
  4269.9 8.9 collective-permute-start.1
  4283.3 7.0 collective-permute-done.2
  4290.3 7.2 collective-permute-done.1
  4298.3 140.5 %concatenate.30 = f32[524,6448]{1,0:T(8,128)} concatenate(f32[12,6448]{1,0:T(8,128)} %collective-permute-done.31, f32[16,6448]{1,0:T(8,128)} %collective-permute-done.30, f32[16,6448]{1,0:T(8,128)} %copy-done.47, f32[16,6448]{1,0:T(8,128)} %copy-done.48, f32[16,6448]{1,0:T(8,128)} %copy-done.49, f32[16,6448]{1,0:T(8,128)} %copy-done.50, f32[16,6448]{1,0:T(8,128)} %copy-done.51, ...), dimensions={0} | concatenate | bytes 27030016
  4441.3 447.7 %reduce-scatter.21.cloned.1.call-done = f32[24,1536]{1,0:T(8,128)} async-done(((f32[3072,1536]{1,0:T(8,128)}), f32[24,1536]{1,0:T(8,128)}) %reduce-scatter.21.cloned.1.call-update) | async-done | bytes 147472 | tf_op jit(solution)/shard_map/reduce_scatter | solution.py:427
  (615 shorter events, 420.8 us)
Async XLA Ops:
  7.2 347.6 %all-gather.26.cloned.1.call-start = ((), (), s32[]{:S(2)}) async-start(), calls=%async_computation.25 | async-start | bytes 26947584 | tf_op jit(solution)/shard_map/all_gather | solution.py:134
  9.1 684.9 %all-gather.14.cloned.1.call-start = ((), (), s32[]{:S(2)}) async-start(), calls=%async_computation.14 | async-start | bytes 9510912 | tf_op jit(solution)/shard_map/all_gather | solution.py:135
  10.7 724.7 %all-gather.16.cloned.1.call-start = ((), (), s32[]{:S(2)}) async-start(), calls=%async_computation.15 | async-start | bytes 3342336 | tf_op jit(solution)/shard_map/all_gather | solution.py:205
  399.5 43.0 all-to-all-start.2
  461.0 27.7 all-to-all-start
  525.2 275.0 %all-gather.24.cloned.1.call-start = ((), (), s32[]{:S(2)}) async-start(), calls=%async_computation.24 | async-start | bytes 3538944 | tf_op jit(solution)/shard_map/all_gather | solution.py:216
  700.2 134.0 %all-gather.18.cloned.1.call-start = ((), (), s32[]{:S(2)}) async-start(), calls=%async_computation.16 | async-start | bytes 1671168 | tf_op jit(solution)/shard_map/all_gather | solution.py:206
  701.1 198.0 %all-gather.22.cloned.1.call-start = ((), (), s32[]{:S(2)}) async-start(), calls=%async_computation.19 | async-start | bytes 3538944 | tf_op jit(solution)/shard_map/all_gather | solution.py:226
  701.9 523.6 %reduce-scatter.27.cloned.1.call-start = ((), (), s32[]{:S(2)}) async-start(), calls=%async_computation.27 | async-start | bytes 294912
  912.3 384.3 %all-gather.28.cloned.1.call-start = ((), (), s32[]{:S(2)}) async-start(), calls=%async_computation.26 | async-start | bytes 8454144 | tf_op jit(solution)/shard_map/all_gather | solution.py:138
  913.9 690.2 %all-gather.20.cloned.1.call-start = ((), (), s32[]{:S(2)}) async-start(), calls=%async_computation.18 | async-start | bytes 3170304 | tf_op jit(solution)/shard_map/all_gather | solution.py:139
  915.4 771.7 %reduce-scatter.19.cloned.1.call-start = ((), (), s32[]{:S(2)}) async-start(), calls=%async_computation.20 | async-start | bytes 3538944 | tf_op jit(solution)/shard_map/reduce_scatter | solution.py:292
  1732.2 160.0 %reduce-scatter.29.cloned.1.call-start = ((), (), s32[]{:S(2)}) async-start(), calls=%async_computation.28 | async-start | bytes 589824
  1787.4 2109.8 %all-reduce.38.cloned.1.call-start = ((), (), s32[]{:S(2)}) async-start(), calls=%async_computation.30 | async-start | bytes 6291456
  1801.0 2203.4 %reduce-scatter.23.cloned.1.call-start = ((), (), s32[]{:S(2)}) async-start(), calls=%async_computation.22 | async-start | bytes 3342336 | tf_op jit(solution)/shard_map/reduce_scatter | solution.py:309
  1809.5 2199.9 %reduce-scatter.17.cloned.1.call-start = ((), (), s32[]{:S(2)}) async-start(), calls=%async_computation.17 | async-start | bytes 3538944 | tf_op jit(solution)/shard_map/reduce_scatter | solution.py:241
  1814.5 2415.4 %reduce-scatter.25.cloned.1.call-start = ((), (), s32[]{:S(2)}) async-start(), calls=%async_computation.23 | async-start | bytes 6340608 | tf_op jit(solution)/shard_map/reduce_scatter | solution.py:431
  1837.7 32.5 all-to-all-start.6
  1870.2 38.0 all-to-all-start.5
  1876.8 2405.1 %all-reduce.36.cloned.1.call-start = ((), (), s32[]{:S(2)}) async-start(), calls=%async_computation.29 | async-start | bytes 188416
  1930.2 2958.8 %reduce-scatter.21.cloned.1.call-start = ((), (), s32[]{:S(2)}) async-start(), calls=%async_computation.21 | async-start | bytes 19021824 | tf_op jit(solution)/shard_map/reduce_scatter | solution.py:427
  2503.7 36.9 collective-permute-start.62
  2506.7 31.0 collective-permute-start.63
  2508.6 33.9 collective-permute-start.61
  2516.9 27.6 collective-permute-start.60
  2521.9 24.5 collective-permute-start.59
  2548.3 19.8 collective-permute-start.53
  2571.6 25.7 collective-permute-start.47
  2573.5 32.2 collective-permute-start.46
  2578.7 29.0 collective-permute-start.45
  2580.6 29.0 collective-permute-start.44
  2587.8 23.7 collective-permute-start.43
  2617.2 25.2 collective-permute-start.36
  2620.3 22.1 collective-permute-start.35
  3881.6 86.8 %collective-permute-start.30 = (f32[16,6448]{1,0:T(8,128)S(1)}, f32[16,6448]{1,0:T(8,128)}, u32[]{:S(2)}, u32[]{:S(2)}) collective-permute-start(f32[16,6448]{1,0:T(8,128)S(1)} %fusion), channel_id=1, source_target_pairs={{0,31},{1,32},{2,33},{3,34},{4,35},{5,36},{6,37},{7,38},{8,39},{9,... | collective-permute-start | bytes 1238024
  3895.0 56.1 %collective-permute-start.31 = (f32[12,6448]{1,0:T(8,128)}, f32[12,6448]{1,0:T(8,128)}, u32[]{:S(2)}, u32[]{:S(2)}) collective-permute-start(f32[12,6448]{1,0:T(8,128)} %slice.211), channel_id=1, source_target_pairs={{0,32},{1,33},{2,34},{3,35},{4,36},{5,37},{6,38},{7,39},{8,40},{9,... | collective-permute-start | bytes 928520
  3898.5 75.1 %collective-permute-start.29 = (f32[16,6448]{1,0:T(8,128)S(1)}, f32[16,6448]{1,0:T(8,128)S(1)}, u32[]{:S(2)}, u32[]{:S(2)}) collective-permute-start(f32[16,6448]{1,0:T(8,128)S(1)} %fusion), channel_id=1, source_target_pairs={{0,30},{1,31},{2,32},{3,33},{4,34},{5,35},{6,36},{7,37},{8,38},{9,... | collective-permute-start | bytes 1238024
  3912.6 82.5 %collective-permute-start.28 = (f32[16,6448]{1,0:T(8,128)S(1)}, f32[16,6448]{1,0:T(8,128)S(1)}, u32[]{:S(2)}, u32[]{:S(2)}) collective-permute-start(f32[16,6448]{1,0:T(8,128)S(1)} %fusion), channel_id=1, source_target_pairs={{0,29},{1,30},{2,31},{3,32},{4,33},{5,34},{6,35},{7,36},{8,37},{9,... | collective-permute-start | bytes 1238024
  3926.2 70.9 %collective-permute-start.27 = (f32[16,6448]{1,0:T(8,128)S(1)}, f32[16,6448]{1,0:T(8,128)S(1)}, u32[]{:S(2)}, u32[]{:S(2)}) collective-permute-start(f32[16,6448]{1,0:T(8,128)S(1)} %fusion), channel_id=1, source_target_pairs={{0,28},{1,29},{2,30},{3,31},{4,32},{5,33},{6,34},{7,35},{8,36},{9,... | collective-permute-start | bytes 1238024
  3951.1 48.0 collective-permute-start.26
  3968.4 32.9 collective-permute-start.25
  3973.6 39.5 collective-permute-start.24
  3995.1 41.3 collective-permute-start.23
  3997.1 41.4 collective-permute-start.22
  3999.2 65.4 %collective-permute-start.21 = (f32[16,6448]{1,0:T(8,128)S(1)}, f32[16,6448]{1,0:T(8,128)}, u32[]{:S(2)}, u32[]{:S(2)}) collective-permute-start(f32[16,6448]{1,0:T(8,128)S(1)} %fusion), channel_id=1, source_target_pairs={{0,22},{1,23},{2,24},{3,25},{4,26},{5,27},{6,28},{7,29},{8,30},{9,... | collective-permute-start | bytes 1238024
  4002.1 64.6 %collective-permute-start.20 = (f32[16,6448]{1,0:T(8,128)S(1)}, f32[16,6448]{1,0:T(8,128)}, u32[]{:S(2)}, u32[]{:S(2)}) collective-permute-start(f32[16,6448]{1,0:T(8,128)S(1)} %fusion), channel_id=1, source_target_pairs={{0,21},{1,22},{2,23},{3,24},{4,25},{5,26},{6,27},{7,28},{8,29},{9,... | collective-permute-start | bytes 1238024
  4013.1 149.7 %collective-permute-start.19 = (f32[16,6448]{1,0:T(8,128)S(1)}, f32[16,6448]{1,0:T(8,128)}, u32[]{:S(2)}, u32[]{:S(2)}) collective-permute-start(f32[16,6448]{1,0:T(8,128)S(1)} %fusion), channel_id=1, source_target_pairs={{0,20},{1,21},{2,22},{3,23},{4,24},{5,25},{6,26},{7,27},{8,28},{9,... | collective-permute-start | bytes 1238024
  4036.4 133.0 %collective-permute-start.18 = (f32[16,6448]{1,0:T(8,128)S(1)}, f32[16,6448]{1,0:T(8,128)}, u32[]{:S(2)}, u32[]{:S(2)}) collective-permute-start(f32[16,6448]{1,0:T(8,128)S(1)} %fusion), channel_id=1, source_target_pairs={{0,19},{1,20},{2,21},{3,22},{4,23},{5,24},{6,25},{7,26},{8,27},{9,... | collective-permute-start | bytes 1238024
  4038.5 132.3 %collective-permute-start.17 = (f32[16,6448]{1,0:T(8,128)S(1)}, f32[16,6448]{1,0:T(8,128)}, u32[]{:S(2)}, u32[]{:S(2)}) collective-permute-start(f32[16,6448]{1,0:T(8,128)S(1)} %fusion), channel_id=1, source_target_pairs={{0,18},{1,19},{2,20},{3,21},{4,22},{5,23},{6,24},{7,25},{8,26},{9,... | collective-permute-start | bytes 1238024
  4064.6 112.0 %collective-permute-start.16 = (f32[16,6448]{1,0:T(8,128)S(1)}, f32[16,6448]{1,0:T(8,128)}, u32[]{:S(2)}, u32[]{:S(2)}) collective-permute-start(f32[16,6448]{1,0:T(8,128)S(1)} %fusion), channel_id=1, source_target_pairs={{0,17},{1,18},{2,19},{3,20},{4,21},{5,22},{6,23},{7,24},{8,25},{9,... | collective-permute-start | bytes 1238024
  4066.6 111.7 %collective-permute-start.15 = (f32[16,6448]{1,0:T(8,128)S(1)}, f32[16,6448]{1,0:T(8,128)}, u32[]{:S(2)}, u32[]{:S(2)}) collective-permute-start(f32[16,6448]{1,0:T(8,128)S(1)} %fusion), channel_id=1, source_target_pairs={{0,16},{1,17},{2,18},{3,19},{4,20},{5,21},{6,22},{7,23},{8,24},{9,... | collective-permute-start | bytes 1238024
  4162.8 31.9 collective-permute-start.14
  4169.5 27.3 collective-permute-start.13
  4170.8 48.9 collective-permute-start.12
  4176.5 45.1 collective-permute-start.11
  4178.3 46.2 collective-permute-start.10
  4194.7 36.7 collective-permute-start.9
  4196.8 69.3 %collective-permute-start.8 = (f32[16,6448]{1,0:T(8,128)S(1)}, f32[16,6448]{1,0:T(8,128)}, u32[]{:S(2)}, u32[]{:S(2)}) collective-permute-start(f32[16,6448]{1,0:T(8,128)S(1)} %fusion), channel_id=1, source_target_pairs={{0,9},{1,10},{2,11},{3,12},{4,13},{5,14},{6,15},{7,16},{8,17},{9,1... | collective-permute-start | bytes 1238024
  4219.7 48.2 collective-permute-start.7
  4221.7 48.2 collective-permute-start.6
  4225.3 53.5 %collective-permute-start.5 = (f32[16,6448]{1,0:T(8,128)S(1)}, f32[16,6448]{1,0:T(8,128)}, u32[]{:S(2)}, u32[]{:S(2)}) collective-permute-start(f32[16,6448]{1,0:T(8,128)S(1)} %fusion), channel_id=1, source_target_pairs={{0,6},{1,7},{2,8},{3,9},{4,10},{5,11},{6,12},{7,13},{8,14},{9,15},... | collective-permute-start | bytes 1238024
  4231.4 51.9 %collective-permute-start.4 = (f32[16,6448]{1,0:T(8,128)S(1)}, f32[16,6448]{1,0:T(8,128)}, u32[]{:S(2)}, u32[]{:S(2)}) collective-permute-start(f32[16,6448]{1,0:T(8,128)S(1)} %fusion), channel_id=1, source_target_pairs={{0,5},{1,6},{2,7},{3,8},{4,9},{5,10},{6,11},{7,12},{8,13},{9,14},{... | collective-permute-start | bytes 1238024
  4267.9 22.3 collective-permute-start.2
  4269.9 27.5 collective-permute-start.1
  (153 other events, 14567.3 us)
Sparse Core Ops, SparseCore 0:
  10.3 344.4 all-gather.25
  357.1 336.8 all-gather.13
  696.3 39.1 all-gather.15
  738.2 62.0 all-gather.23
  802.4 31.7 all-gather.17
  836.9 62.1 all-gather.21
  912.4 66.2 reduce-scatter.26
  981.0 315.5 all-gather.27
  1298.8 305.1 all-gather.19
  1607.7 79.3 reduce-scatter.18
  1787.6 67.9 reduce-scatter.28
  1858.1 141.0 all-reduce.37
  2001.7 77.2 reduce-scatter.22
  2083.1 106.5 reduce-scatter.16
  2192.0 879.7 reduce-scatter.24
  3077.0 1060.2 all-reduce.35
  4139.7 749.1 reduce-scatter.20
where the time goes:
time: 4930 us; the launch traced here: 4900 us
  blocking collectives  2230 us (45%)
  waiting for transfers between devices  1560 us (32%)
  starting transfers between devices  404 us (8%)
  local copies, waits for them, and re-layouts  395 us (8%)
  matrix products  181 us (4%)
  other arithmetic  112 us (2%)
    unnamed x3, blocking collectives  1790 us
    reduce_scatter x1, waiting for transfers between devices, local(): lax.psum_scatter(out_weight_grad, ('fsdp', 'seq'), scatter_dimension=0, t...  448 us
    unnamed x68, starting transfers between devices  367 us
    all_gather x1, blocking collectives, local(): lax.all_gather(dense_low[3], ('fsdp', 'seq'), axis=0, tiled=True)  305 us
    unnamed x305, local copies, waits for them, and re-layouts  302 us
    all_gather x1, waiting for transfers between devices, local(): lax.all_gather(dense_low[5], ('fsdp', 'seq'), axis=0, tiled=True)  292 us
    all_gather x1, waiting for transfers between devices, local(): lax.all_gather(dense_low[0], ('fsdp', 'seq'), axis=0, tiled=True)  268 us
    all_gather x1, waiting for transfers between devices, local(): lax.all_gather(dense_low[1], ('fsdp', 'seq'), axis=0, tiled=True)  149 us
  transfers between devices with their start and end apart: 88, of which 23 were waited for; matrix products, arithmetic and copies ran while one was open for 47% of the time, Pallas kernels for 0%

commit v1 on v0

v1 whole, which is shorter than its diff:
```python
import functools

import jax
import jax.numpy as jnp
from jax import lax
from jax.experimental import pallas as pl
from jax.experimental.pallas import tpu as pltpu
from jax.sharding import PartitionSpec as P

D = 1536
HEADS = 48
HDIM = 64
STATE = 128
CONV = 4
FF_EXP = 512
FF_SH = 1024
TOPK = 6
EXPERTS = 8
STEP = 5
INNER = 3072
CHANNELS = 3328
SMALL = 22784
GROUPS = 8
SHARDS = 16
HEADS_HERE = HEADS // GROUPS
INNER_HERE = INNER // GROUPS
SH_HERE = FF_SH // GROUPS
SEQ_LEN = 1024
PIECE = SEQ_LEN // GROUPS
CONV_HERE = INNER_HERE + 2 * STATE
PROJ_HERE = INNER_HERE + CONV_HERE + 128
SMALL_COLS = 15


NORM_EPSILON = 1e-05
BETA_FIRST = 0.9
BETA_SECOND = 0.95
ADAM_EPSILON = 1e-08
RATE_MATRIX = 0.04
RATE_DOWN = 0.1
RATE_SMALL = 0.3
RATE_HEAD = 1.0
WEIGHT_DECAY = 0.1
HIGHEST = lax.Precision.HIGHEST
LOW = jnp.bfloat16
FULL = jnp.float32
MESH = pl.DeviceIdType.MESH


def hi_lo(values):
    high = values.astype(LOW)
    return high, (values - high.astype(FULL)).astype(LOW)


BUSY = pl.CostEstimate(flops=30_000_000_000, bytes_accessed=4_000_000, transcendentals=0)


def seq_axis():
    me = lax.axis_index("seq")
    side, level = lax.rem(me, 2), lax.div(me, 2)

    def slot(up, other):
        return lax.rem(level + up + 4, 4) * 2 + (1 - side if other else side)

    return me, slot, lambda up, other: {"seq": slot(up, other)}


def fsdp_axis():
    me = lax.axis_index("fsdp")
    core, rest = lax.rem(me, 2), lax.div(me, 2)
    side, level = lax.rem(rest, 2), lax.div(rest, 2)

    def slot(up, other):
        return lax.rem(level + up + 4, 4) * 2 + (1 - side if other else side)

    return core, slot, lambda up, other: {"fsdp": slot(up, other) * 2 + core}, {"fsdp": rest * 2 + 1 - core}


def meet(devices):
    barrier = pltpu.get_barrier_semaphore()
    for device in devices:
        pl.semaphore_signal(barrier, inc=1, device_id=device, device_id_type=MESH)
    pl.semaphore_wait(barrier, len(devices))


def ring_peers(device):
    return [device(0, True), device(1, False), device(-1, False)]


def sender(send_sem, recv_sem, started):
    def send(source, target, device):
        index = len(started)
        copy = pltpu.make_async_remote_copy(
            src_ref=source,
            dst_ref=target,
            send_sem=send_sem.at[index],
            recv_sem=recv_sem.at[index],
            device_id=device,
            device_id_type=MESH,
        )
        copy.start()
        started.append(copy)
        return copy

    return send


def take_turns(*programs):
    waiting = list(programs)
    while waiting:
        for program in list(waiting):
            if next(program, None) is None:
                waiting.remove(program)


def follow(order, ring, shards):
    for which in order:
        for program in [ring] if which == "z" else shards:
            next(program, None)


def ring_gather(source, place, slot, device, send, arrived, split=True):
    rows = source.shape[0]
    halves = ((pl.ds(0, rows // 2),), (pl.ds(rows // 2, rows // 2),)) if split else ((), None)
    own = place(slot(0, False), ())
    to_side = send(source, own, device(0, True))
    up = send(source, own, device(1, False))
    down = send(source, own, device(-1, False))
    arrived(source, own)
    yield True
    far, two = [], []

    def pass_on(copy, up, other, index):
        copy.wait_recv()
        if halves[index] is not None:
            part = place(slot(-up, other), halves[index])
            far.append(send(part, part, device(up, False)))
        block = place(slot(-up, other), ())
        arrived(block, block)

    def far_here(index, other):
        if halves[index % 2] is not None:
            far.pop(0).wait_recv()
            part = place(slot(2, other), halves[index % 2])
            arrived(part, part)

    pass_on(up, 1, False, 0)
    yield True
    pass_on(down, -1, False, 1)
    yield True
    to_side.wait_recv()
    block = place(slot(0, True), ())
    two.append(send(block, block, device(1, False)))
    two.append(send(block, block, device(-1, False)))
    arrived(block, block)
    yield True
    for index in range(2):
        far_here(index, False)
        yield True
    pass_on(two[0], 1, True, 0)
    yield True
    pass_on(two[1], -1, True, 1)
    yield True
    for index in range(2):
        far_here(index, True)
        yield True


def nothing(source, target):
    return None


def side_start(side_ref, side_out, per_peer, send_sem, recv_sem, local_sem):
    me = lax.axis_index("seq")
    copies = []
    for step in range(1, GROUPS):
        other = lax.rem(me + step, GROUPS)
        copy = pltpu.make_async_remote_copy(
            src_ref=side_ref.at[other] if per_peer else side_ref,
            dst_ref=side_out.at[me],
            send_sem=send_sem.at[step],
            recv_sem=recv_sem.at[step],
            device_id={"seq": other},
            device_id_type=MESH,
        )
        copy.start()
        copies.append(copy)
    keep = pltpu.make_async_copy(side_ref.at[me] if per_peer else side_ref, side_out.at[me], local_sem)
    keep.start()
    return copies, keep


def side_end(copies, keep):
    for copy in copies:
        copy.wait_recv()
    for copy in copies:
        copy.wait_send()
    keep.wait()


def all_peers():
    me = lax.axis_index("seq")
    return [{"seq": lax.rem(me + step, GROUPS)} for step in range(1, GROUPS)]


def gather_kernel(x_ref, side_ref, out_ref, side_out, send_sem, recv_sem, local_sem, s_send, s_recv, s_local):
    me, slot, device = seq_axis()
    meet(all_peers())
    started = []
    send = sender(send_sem, recv_sem, started)
    program = ring_gather(x_ref, lambda at, cut: out_ref.at[(at, *cut)], slot, device, send, nothing)
    next(program)
    sides = side_start(side_ref, side_out, False, s_send, s_recv, s_local)
    keep = pltpu.make_async_copy(x_ref, out_ref.at[me], local_sem)
    keep.start()
    take_turns(program)
    side_end(*sides)
    for copy in started:
        copy.wait_send()
    keep.wait()


def any_spec():
    return pl.BlockSpec(memory_space=pl.ANY)


def vmem_spec():
    return pl.BlockSpec(memory_space=pltpu.VMEM)


def dma_sems(count):
    return pltpu.SemaphoreType.DMA((count,))


def seq_gather(piece, side, name, collective_id):
    rows, width = piece.shape
    gathered, sides = pl.pallas_call(
        gather_kernel,
        out_shape=(
            jax.ShapeDtypeStruct((GROUPS, rows, width), piece.dtype),
            jax.ShapeDtypeStruct((GROUPS, 8, 128), FULL),
        ),
        in_specs=[any_spec()] * 2,
        out_specs=(any_spec(), any_spec()),
        scratch_shapes=[
            dma_sems(9),
            dma_sems(9),
            pltpu.SemaphoreType.DMA,
            dma_sems(GROUPS),
            dma_sems(GROUPS),
            pltpu.SemaphoreType.DMA,
        ],
        compiler_params=pltpu.CompilerParams(collective_id=collective_id, has_side_effects=True),
        cost_estimate=BUSY,
        name=name,
    )(piece, side)
    return gathered.reshape(GROUPS * rows, width), sides


def shard_gather(source, target, send_sem, recv_sem, started, crossing, split=True):
    core, slot, device, twin = fsdp_axis()
    send = sender(send_sem, recv_sem, started)

    def place(at, cut):
        return target.at[(at * 2 + core, *cut)]

    def arrived(origin, block):
        crossing.append(send(origin, block, twin))

    return ring_gather(source, place, slot, device, send, arrived, split)


START_COUNT = 2


def start_kernel(x_ref, *rest):
    sources, x_out, targets = rest[:START_COUNT], rest[START_COUNT], rest[START_COUNT + 1 : 2 * START_COUNT + 1]
    x_send, x_recv, keeps, *sems = rest[2 * START_COUNT + 1 :]
    me, slot, device = seq_axis()
    core, f_slot, f_device, twin = fsdp_axis()
    meet(ring_peers(device) + ring_peers(f_device) + [twin])
    mine = f_slot(0, False) * 2 + core
    x_started, started, crossing, kept = [], [], [], []
    x_sender = sender(x_send, x_recv, x_started)
    program = ring_gather(x_ref, lambda at, cut: x_out.at[(at, *cut)], slot, device, x_sender, nothing)
    shards = []
    for index, (source, target) in enumerate(zip(sources, targets)):
        copies = []
        started.append(copies)
        shards.append(
            shard_gather(
                source, target, sems[2 * index], sems[2 * index + 1], copies, crossing, source.shape[0] % 32 == 0
            )
        )
        keep = pltpu.make_async_copy(source, target.at[mine], keeps.at[index])
        keep.start()
        kept.append(keep)
    keep = pltpu.make_async_copy(x_ref, x_out.at[me], keeps.at[START_COUNT])
    keep.start()
    kept.append(keep)
    follow("yzyyyzzyyzyyyyzzzzzz", program, shards)
    take_turns(program, *shards)
    for copy in crossing:
        copy.wait_recv()
    for copies in (x_started, *started):
        for copy in copies:
            copy.wait_send()
    for keep in kept:
        keep.wait()


def start_gather(piece, *shards):
    rows, width = piece.shape
    out = pl.pallas_call(
        start_kernel,
        out_shape=(jax.ShapeDtypeStruct((GROUPS, rows, width), LOW),)
        + tuple(jax.ShapeDtypeStruct((SHARDS, *shard.shape), LOW) for shard in shards),
        in_specs=[any_spec()] * (1 + START_COUNT),
        out_specs=(any_spec(),) * (1 + START_COUNT),
        scratch_shapes=[dma_sems(9)] * 2 + [dma_sems(START_COUNT + 1)] + [dma_sems(19)] * (2 * START_COUNT),
        compiler_params=pltpu.CompilerParams(collective_id=2, has_side_effects=True),
        cost_estimate=BUSY,
        name="rows_first",
    )(piece, *shards)
    return [out[0].reshape(GROUPS * rows, width)] + [
        full.reshape(SHARDS * shard.shape[0], -1) for full, shard in zip(out[1:], shards)
    ]


def ring_scatter(block, slot, device, send, result, buffers):
    in_low, in_high, sum_up, sum_down, land_low, land_high, part_out, part_in = buffers
    rows = part_out.shape[0]
    half = rows // 2
    first, second = pl.ds(0, half), pl.ds(half, half)
    everything = pl.ds(0, rows)
    landing = {}

    def begin(turn, other):
        far = block(2, other)
        copies = [
            send(far(first), in_low.at[turn], device(1, False)),
            send(far(second), in_high.at[turn], device(-1, False)),
        ]
        landing[turn] = [
            send(block(1, other)(second), land_low.at[turn, second], device(1, False)),
            send(block(-1, other)(first), land_high.at[turn, first], device(-1, False)),
        ]
        return copies

    def middle(turn, other, copies):
        copies[0].wait_recv()
        sum_up[turn] = (in_low[turn].astype(FULL) + block(1, other)(first)[...].astype(FULL)).astype(LOW)
        landing[turn].append(send(sum_up.at[turn], land_low.at[turn, first], device(1, False)))
        copies[1].wait_recv()
        sum_down[turn] = (in_high[turn].astype(FULL) + block(-1, other)(second)[...].astype(FULL)).astype(LOW)
        landing[turn].append(send(sum_down.at[turn], land_high.at[turn, second], device(-1, False)))

    def total(turn, other):
        for copy in landing[turn]:
            copy.wait_recv()
        return (
            block(0, other)(everything)[...].astype(FULL)
            + land_low[turn].astype(FULL)
            + land_high[turn].astype(FULL)
        )

    copies = begin(0, True)
    yield True
    middle(0, True, copies)
    yield True
    copies = begin(1, False)
    yield True
    part_out[...] = total(0, True).astype(LOW)
    to_side = send(part_out, part_in, device(0, True))
    yield True
    middle(1, False, copies)
    yield True
    result[...] = total(1, False)
    yield True
    to_side.wait_recv()
    result[...] += part_in[...].astype(FULL)


def scatter_buffers(rows, width):
    half = rows // 2
    return (
        [pltpu.VMEM((2, half, width), LOW)] * 4
        + [pltpu.VMEM((2, rows, width), LOW)] * 2
        + [pltpu.VMEM((rows, width), LOW)] * 2
    )


def block_of(x_ref, slot):
    def block(up, other):
        return lambda cut: x_ref.at[slot(up, other), cut]

    return block


def mixed_kernel(x_ref, side_ref, u_ref, d_ref, out_ref, side_out, u_out, d_out, *rest):
    buffers, (send_sem, recv_sem, s_send, s_recv, s_local) = rest[:8], rest[8:13]
    u_send, u_recv, d_send, d_recv, keeps = rest[13:]
    me, slot, device = seq_axis()
    core, f_slot, f_device, twin = fsdp_axis()
    meet(all_peers() + ring_peers(f_device) + [twin])
    started, u_started, d_started, crossing = [], [], [], []
    send = sender(send_sem, recv_sem, started)
    program = ring_scatter(block_of(x_ref, slot), slot, device, send, out_ref, buffers)
    next(program)
    sides = side_start(side_ref, side_out, True, s_send, s_recv, s_local)
    mine = f_slot(0, False) * 2 + core
    kept = []
    for index, (source, block) in enumerate(((u_ref, u_out.at[mine]), (d_ref, d_out.at[mine]))):
        keep = pltpu.make_async_copy(source, block, keeps.at[index])
        keep.start()
        kept.append(keep)
    shards = [
        shard_gather(u_ref, u_out, u_send, u_recv, u_started, crossing),
        shard_gather(d_ref, d_out, d_send, d_recv, d_started, crossing),
    ]
    follow("yzyyzyyyzyyzyyzz", program, shards)
    take_turns(program, *shards)
    side_end(*sides)
    for copy in crossing:
        copy.wait_recv()
    for copy in started + u_started + d_started:
        copy.wait_send()
    for keep in kept:
        keep.wait()


def mixed_scatter(parts, side, up_piece, down_piece):
    groups, rows, width = parts.shape
    summed, sides, up_all, down_all = pl.pallas_call(
        mixed_kernel,
        out_shape=(
            jax.ShapeDtypeStruct((rows, width), FULL),
            jax.ShapeDtypeStruct((GROUPS, 8, 128), FULL),
            jax.ShapeDtypeStruct((SHARDS, *up_piece.shape), LOW),
            jax.ShapeDtypeStruct((SHARDS, *down_piece.shape), LOW),
        ),
        in_specs=[vmem_spec(), vmem_spec(), any_spec(), any_spec()],
        out_specs=(vmem_spec(), vmem_spec(), any_spec(), any_spec()),
        scratch_shapes=scatter_buffers(rows, width)
        + [dma_sems(13), dma_sems(13), dma_sems(GROUPS), dma_sems(GROUPS), pltpu.SemaphoreType.DMA]
        + [dma_sems(19)] * 4
        + [dma_sems(2)],
        compiler_params=pltpu.CompilerParams(
            collective_id=4, has_side_effects=True, vmem_limit_bytes=40 << 20
        ),
        cost_estimate=BUSY,
        name="mixer_out",
    )(parts, side, up_piece, down_piece)
    return summed, sides, up_all.reshape(-1, up_piece.shape[1]), down_all.reshape(-1, down_piece.shape[1])


def shard_scratch(grads):
    depth, columns = grads.shape[1:]
    return (
        scatter_buffers(depth, columns)
        + [pltpu.VMEM((GROUPS, depth, columns), LOW)]
        + [dma_sems(13), dma_sems(13), dma_sems(8), dma_sems(8)]
    )


SHARD_SCRATCH = 13


def shard_scatters(arrays, started):
    core, slot, device, twin = fsdp_axis()
    order = [(2, True), (1, True), (-1, True), (2, False), (1, False), (-1, False), (0, True), (0, False)]
    programs, senders = [], []
    for pick, target, scratch in arrays:
        buffers, (core_in, send_sem, recv_sem, c_send, c_recv) = scratch[:8], scratch[8:]
        crossing, copies, arriving = [], [], {}
        started.extend([crossing, copies])
        senders.append((pick, core_in, sender(c_send, c_recv, crossing), arriving))

        def block(up, other, pick=pick, core_in=core_in, arriving=arriving):
            at = slot(up, other)
            if (up, other) in arriving:
                arriving.pop((up, other)).wait_recv()
                core_in[at] = (core_in[at].astype(FULL) + pick(at * 2 + core)[...].astype(FULL)).astype(LOW)
            return lambda cut: core_in.at[at, cut]

        programs.append(ring_scatter(block, slot, device, sender(send_sem, recv_sem, copies), target, buffers))
    for key in order:
        for pick, core_in, send_core, arriving in senders:
            at = slot(*key)
            arriving[key] = send_core(pick(at * 2 + 1 - core), core_in.at[at], twin)
    return programs


def blocks_of(ref):
    return lambda at: ref.at[at]


def shard_peers():
    core, slot, device, twin = fsdp_axis()
    return ring_peers(device) + [twin]


def last_kernel(g_ref, p_ref, w_ref, a_ref, x_out, w_out, a_out, x_ref, *rest):
    x_buffers, (x_send, x_recv) = rest[:8], rest[8:10]
    me, slot, device = seq_axis()
    done = set()

    def part_of(up, other):
        at = slot(up, other)
        if (up, other) not in done:
            done.add((up, other))
            here = pl.ds(pl.multiple_of(at * PIECE, PIECE), PIECE)
            for part in range(D // 512):
                cols = slice(part * 512, (part + 1) * 512)
                x_ref[at, :, cols] = dot_rhs_t(g_ref[here, :], p_ref[cols, :]).astype(LOW)
        return lambda cut: x_ref.at[at, cut]

    meet(ring_peers(device) + shard_peers())
    x_started, started = [], []
    program = ring_scatter(part_of, slot, device, sender(x_send, x_recv, x_started), x_out, x_buffers)
    main, small = shard_scatters(
        [
            (blocks_of(w_ref), w_out, rest[10 : 10 + SHARD_SCRATCH]),
            (blocks_of(a_ref), a_out, rest[10 + SHARD_SCRATCH :]),
        ],
        started,
    )
    follow("zyzyzyyzyzyzyz", program, [main, small])
    take_turns(program, main, small)
    for copies in (x_started, *started):
        for copy in copies:
            copy.wait_send()


def last_scatter(proj_grad, weights, grads, small):
    rows, width = PIECE, D
    return pl.pallas_call(
        last_kernel,
        out_shape=(
            jax.ShapeDtypeStruct((rows, width), FULL),
            jax.ShapeDtypeStruct(grads.shape[1:], FULL),
            jax.ShapeDtypeStruct(small.shape[1:], FULL),
        ),
        in_specs=[vmem_spec()] * 4,
        out_specs=(vmem_spec(),) * 3,
        scratch_shapes=[pltpu.VMEM((GROUPS, rows, width), LOW)]
        + scatter_buffers(rows, width)
        + [dma_sems(13), dma_sems(13)]
        + shard_scratch(grads)
        + shard_scratch(small),
        compiler_params=pltpu.CompilerParams(
            collective_id=8, has_side_effects=True, vmem_limit_bytes=40 << 20
        ),
        cost_estimate=BUSY,
        name="rows_last",
    )(proj_grad, weights, grads, small)


def middle_kernel(x_ref, side_ref, u_ref, x_out, side_out, u_out, *rest):
    x_send, x_recv, x_local, s_send, s_recv, s_local = rest[:6]
    me, slot, device = seq_axis()
    meet(all_peers() + shard_peers())
    x_started, started = [], []
    send = sender(x_send, x_recv, x_started)
    program = ring_gather(x_ref, lambda at, cut: x_out.at[(at, *cut)], slot, device, send, nothing)
    next(program)
    [shard] = shard_scatters([(blocks_of(u_ref), u_out, rest[6:])], started)
    sides = side_start(side_ref, side_out, False, s_send, s_recv, s_local)
    keep = pltpu.make_async_copy(x_ref, x_out.at[me], x_local)
    keep.start()
    follow("yyyzzyzyzzyyzzzz", program, [shard])
    take_turns(program, shard)
    side_end(*sides)
    for copies in (x_started, *started):
        for copy in copies:
            copy.wait_send()
    keep.wait()


def middle_gather(piece, side, up_grads):
    rows, width = piece.shape
    gathered, sides, up_sum = pl.pallas_call(
        middle_kernel,
        out_shape=(
            jax.ShapeDtypeStruct((GROUPS, rows, width), piece.dtype),
            jax.ShapeDtypeStruct((GROUPS, 8, 128), FULL),
            jax.ShapeDtypeStruct(up_grads.shape[1:], FULL),
        ),
        in_specs=[any_spec(), any_spec(), vmem_spec()],
        out_specs=(any_spec(), any_spec(), vmem_spec()),
        scratch_shapes=[
            dma_sems(9),
            dma_sems(9),
            pltpu.SemaphoreType.DMA,
            dma_sems(GROUPS),
            dma_sems(GROUPS),
            pltpu.SemaphoreType.DMA,
        ]
        + shard_scratch(up_grads),
        compiler_params=pltpu.CompilerParams(
            collective_id=7, has_side_effects=True, vmem_limit_bytes=48 << 20
        ),
        cost_estimate=BUSY,
        name="rows_mixer",
    )(piece, side, up_grads)
    return gathered.reshape(GROUPS * rows, width), sides, up_sum


UNITS = FF_EXP + SH_HERE
HIDDEN_COLS = 2 * UNITS


def experts_kernel(
    x_ref,
    side_ref,
    cot_any,
    up_any,
    shared_any,
    down_any,
    shared_down_any,
    back_out,
    side_back,
    block_any,
    up_grad_any,
    down_grad_any,
    shared_grad_any,
    cot_ref,
    up_ref,
    shared_ref,
    down_ref,
    shared_down_ref,
    block_ref,
    up_grad_ref,
    down_grad_ref,
    shared_grad_ref,
    rows_ref,
    sides_in,
    parts_ref,
    gu_ref,
    act_ref,
    side_send,
    *rest,
):
    buffers, rest = rest[:8], rest[8:]
    g_send, g_recv, g_local, s_send, s_recv, s_local, r_send, r_recv, b_send, b_recv, b_local, moves = rest
    me, slot, device = seq_axis()
    moving = []

    def move(source, target):
        copy = pltpu.make_async_copy(source, target, moves.at[len(moving)])
        copy.start()
        moving.append(copy)

    for source, target in (
        (up_any, up_ref),
        (down_any, down_ref),
        (cot_any, cot_ref),
        (shared_any, shared_ref),
        (shared_down_any, shared_down_ref),
    ):
        move(source, target)
    meet(all_peers())
    started = []
    gather = ring_gather(
        x_ref, lambda at, cut: rows_ref.at[(at, *cut)], slot, device, sender(g_send, g_recv, started), nothing
    )
    next(gather)
    sides = side_start(side_ref, sides_in, False, s_send, s_recv, s_local)
    keep = pltpu.make_async_copy(x_ref, rows_ref.at[me], g_local)
    keep.start()
    keep.wait()
    for copy in moving:
        copy.wait()
    side_end(*sides)

    def unit_step(hidden, cot, weights, downs, width, gu_at, half, scale):
        gate = dot(hidden, weights[:, gu_at : gu_at + width])
        lift = dot(hidden, weights[:, gu_at + half : gu_at + half + width])
        back = dot_rhs_t(cot, downs)
        gate_sig = sigmoid(gate)
        gate_silu = gate * gate_sig
        act = (gate_silu * lift).astype(LOW).astype(FULL)
        product = back * act
        if scale is not None:
            scale = jnp.concatenate([scale] * (width // 128), axis=1)
            act = act * scale
            back = back * scale
        gate_grad = back * lift * (gate_sig * (1.0 + gate * (1.0 - gate_sig)))
        return product, act.astype(LOW), gate_grad.astype(LOW), (back * gate_silu).astype(LOW)

    def joined(blocks):
        return blocks[0] if len(blocks) == 1 else jnp.concatenate(blocks, axis=0)

    def process(*keys):
        slots = [slot(*key) for key in keys]
        rows = [pl.ds(pl.multiple_of(at * PIECE, PIECE), PIECE) for at in slots]

        def put(ref, cols, values):
            for index, here in enumerate(rows):
                ref[here, cols] = values[index * PIECE : (index + 1) * PIECE]

        hidden = joined([rows_ref[at] for at in slots])
        cot = joined([cot_ref[at] for at in slots])
        scale = joined([jnp.broadcast_to(sides_in[at, pl.ds(me, 1), :], (128, 128)).T for at in slots])
        folded = None
        for begin in range(0, FF_EXP, 256):
            cols = slice(begin, begin + 256)
            product, act, gate_grad, lift_grad = unit_step(
                hidden, cot, up_ref, down_ref[cols, :], 256, begin, FF_EXP, scale
            )
            put(act_ref, cols, act)
            put(gu_ref, cols, gate_grad)
            put(gu_ref, slice(FF_EXP + begin, FF_EXP + begin + 256), lift_grad)
            product = product[:, :128] + product[:, 128:]
            folded = product if folded is None else folded + product
        unused, act, gate_grad, lift_grad = unit_step(
            hidden, cot, shared_ref, shared_down_ref[...], SH_HERE, 0, SH_HERE, None
        )
        put(act_ref, slice(FF_EXP, UNITS), act)
        put(gu_ref, slice(2 * FF_EXP, 2 * FF_EXP + SH_HERE), gate_grad)
        put(gu_ref, slice(2 * FF_EXP + SH_HERE, HIDDEN_COLS), lift_grad)
        sums = lax.dot_general(
            jnp.ones((8, 128), FULL),
            folded,
            (((1,), (1,)), ((), ())),
            precision=HIGHEST,
            preferred_element_type=FULL,
        )
        for index, at in enumerate(slots):
            side_send[at] = sums[:, index * PIECE : (index + 1) * PIECE]
        grads = joined([gu_ref[here, :] for here in rows])
        for begin in range(0, D, 512):
            cols = slice(begin, begin + 512)
            total = dot_rhs_t(grads[:, : 2 * FF_EXP], up_ref[cols, :])
            total = (total + dot_rhs_t(grads[:, 2 * FF_EXP :], shared_ref[cols, :])).astype(LOW)
            for index, at in enumerate(slots):
                parts_ref[at, :, cols] = total[index * PIECE : (index + 1) * PIECE]

    process((0, False))
    next(gather)
    next(gather)
    process((-1, False), (1, False))
    next(gather)
    next(gather)
    next(gather)
    process((0, True), (2, False))
    next(gather)
    next(gather)
    process((-1, True), (1, True))
    take_turns(gather)
    process((2, True))

    summed = []
    scatter = ring_scatter(
        block_of(parts_ref, slot), slot, device, sender(r_send, r_recv, summed), back_out, buffers
    )
    next(scatter)
    backs = side_start(side_send, side_back, True, b_send, b_recv, b_local)

    def block_step(at, carry):
        rows = pl.ds(pl.multiple_of(at * PIECE, PIECE), PIECE)
        for begin in range(0, D, 512):
            cols = slice(begin, begin + 512)
            total = dot(act_ref[rows, :FF_EXP], down_ref[:, cols])
            total = total + dot(act_ref[rows, FF_EXP:], shared_down_ref[:, cols])
            block_ref[at, :, cols] = total.astype(LOW)
        return carry

    def up_step(part, carry):
        rows = pl.ds(pl.multiple_of(part * 256, 256), 256)
        left = rows_ref[:, :, rows].reshape(SEQ_LEN, 256).T
        for begin in range(0, HIDDEN_COLS, 640):
            cols = slice(begin, begin + 640)
            up_grad_ref[rows, cols] = dot(left, gu_ref[:, cols]).astype(LOW)
        return carry

    lax.fori_loop(0, 4, block_step, 0)
    next(scatter)
    next(scatter)
    lax.fori_loop(4, 8, block_step, 0)
    moving.clear()
    move(block_ref, block_any)
    next(scatter)
    lax.fori_loop(0, 3, up_step, 0)
    next(scatter)
    lax.fori_loop(3, 6, up_step, 0)
    move(up_grad_ref, up_grad_any)
    next(scatter)
    for row in range(0, UNITS, 128):
        left = act_ref[:, row : row + 128].T
        for begin in range(0, D, 512):
            cols = slice(begin, begin + 512)
            grads = dot(left, cot_ref[:, :, cols].reshape(SEQ_LEN, 512)).astype(LOW)
            if row < FF_EXP:
                down_grad_ref[row : row + 128, cols] = grads
            else:
                shared_grad_ref[:, cols] = grads
    move(down_grad_ref, down_grad_any)
    move(shared_grad_ref, shared_grad_any)
    take_turns(scatter)
    for copy in moving:
        copy.wait()
    side_end(*backs)
    for copy in started + summed:
        copy.wait_send()


def experts(piece, side, rows_cot, up, shared, down, shared_down):
    return pl.pallas_call(
        experts_kernel,
        out_shape=(
            jax.ShapeDtypeStruct((PIECE, D), FULL),
            jax.ShapeDtypeStruct((GROUPS, 8, 128), FULL),
            jax.ShapeDtypeStruct((GROUPS, PIECE, D), LOW),
            jax.ShapeDtypeStruct((D, HIDDEN_COLS), LOW),
            jax.ShapeDtypeStruct((FF_EXP, D), LOW),
            jax.ShapeDtypeStruct((SH_HERE, D), LOW),
        ),
        in_specs=[vmem_spec()] * 2 + [any_spec()] * 5,
        out_specs=(vmem_spec(),) * 2 + (any_spec(),) * 4,
        scratch_shapes=[
            pltpu.VMEM((GROUPS, PIECE, D), LOW),
            pltpu.VMEM((D, 2 * FF_EXP), LOW),
            pltpu.VMEM((D, 2 * SH_HERE), LOW),
            pltpu.VMEM((FF_EXP, D), LOW),
            pltpu.VMEM((SH_HERE, D), LOW),
            pltpu.VMEM((GROUPS, PIECE, D), LOW),
            pltpu.VMEM((D, HIDDEN_COLS), LOW),
            pltpu.VMEM((FF_EXP, D), LOW),
            pltpu.VMEM((SH_HERE, D), LOW),
            pltpu.VMEM((GROUPS, PIECE, D), LOW),
            pltpu.VMEM((GROUPS, 8, 128), FULL),
            pltpu.VMEM((GROUPS, PIECE, D), LOW),
            pltpu.VMEM((SEQ_LEN, HIDDEN_COLS), LOW),
            pltpu.VMEM((SEQ_LEN, UNITS), LOW),
            pltpu.VMEM((GROUPS, 8, 128), FULL),
        ]
        + scatter_buffers(PIECE, D)
        + [dma_sems(9), dma_sems(9), pltpu.SemaphoreType.DMA]
        + [dma_sems(GROUPS), dma_sems(GROUPS), pltpu.SemaphoreType.DMA]
        + [dma_sems(13), dma_sems(13)]
        + [dma_sems(GROUPS), dma_sems(GROUPS), pltpu.SemaphoreType.DMA]
        + [dma_sems(5)],
        compiler_params=pltpu.CompilerParams(
            collective_id=5, has_side_effects=True, vmem_limit_bytes=56 << 20
        ),
        cost_estimate=BUSY,
        name="experts",
    )(piece, side, rows_cot, up, shared, down, shared_down)


def swap_start(x_ref, out_ref, send_sem, recv_sem, local_sem):
    return side_start(x_ref, out_ref, True, send_sem, recv_sem, local_sem)


def columns_kernel(x_ref, x_out, x_send, x_recv, x_local):
    meet(all_peers())
    side_end(*swap_start(x_ref, x_out, x_send, x_recv, x_local))


def columns_out(blocks):
    return pl.pallas_call(
        columns_kernel,
        out_shape=jax.ShapeDtypeStruct(blocks.shape, blocks.dtype),
        in_specs=[any_spec()],
        out_specs=any_spec(),
        scratch_shapes=[dma_sems(GROUPS), dma_sems(GROUPS), pltpu.SemaphoreType.DMA],
        compiler_params=pltpu.CompilerParams(collective_id=1, has_side_effects=True),
        cost_estimate=BUSY,
        name="columns_out",
    )(blocks)


def back_kernel(x_ref, u_ref, side_ref, x_out, u_out, side_out, *sems):
    meet(all_peers())
    swaps = [
        swap_start(x_ref, x_out, *sems[:3]),
        swap_start(u_ref, u_out, *sems[3:6]),
        swap_start(side_ref, side_out, *sems[6:]),
    ]
    for swap in swaps:
        side_end(*swap)


def columns_back(blocks, shared, side):
    return pl.pallas_call(
        back_kernel,
        out_shape=(
            jax.ShapeDtypeStruct(blocks.shape, blocks.dtype),
            jax.ShapeDtypeStruct(shared.shape, shared.dtype),
            jax.ShapeDtypeStruct(side.shape, side.dtype),
        ),
        in_specs=[any_spec()] * 3,
        out_specs=(any_spec(),) * 3,
        scratch_shapes=[dma_sems(GROUPS), dma_sems(GROUPS), pltpu.SemaphoreType.DMA] * 3,
        compiler_params=pltpu.CompilerParams(collective_id=10, has_side_effects=True),
        cost_estimate=BUSY,
        name="columns_back",
    )(blocks, shared, side)


TILE = 256
TILES = SEQ_LEN // TILE
PAIRS = HEADS_HERE // 2


def scan_lanes(values, backward):
    length = values.shape[1]
    lane = lax.broadcasted_iota(jnp.int32, values.shape, 1)
    step = 1
    while step < length:
        if backward:
            values = values + jnp.where(lane < length - step, pltpu.roll(values, length - step, 1), 0.0)
        else:
            values = values + jnp.where(lane >= step, pltpu.roll(values, step, 1), 0.0)
        step *= 2
    return values


def sigmoid(values):
    return 1.0 / (1.0 + jnp.exp(-values))


def conv_taps(padded, taps, at):
    total = taps[0:1, at] * padded[5 : 5 + SEQ_LEN]
    for tap in range(1, CONV):
        total = total + taps[tap : tap + 1, at] * padded[5 + tap : 5 + tap + SEQ_LEN]
    return total


def scores_and_columns(b_state, c_state, cum_rows, scores, columns):
    for low in range(TILES):
        for far in range(low + 1):
            scores[low * TILE : (low + 1) * TILE, far * TILE : (far + 1) * TILE] = dot_rhs_t(
                c_state[low * TILE : (low + 1) * TILE], b_state[far * TILE : (far + 1) * TILE]
            )
    turned = jnp.concatenate([cum_rows, jnp.zeros((120, SEQ_LEN), FULL)], axis=0).T
    for head in range(HEADS_HERE):
        columns[head] = jnp.broadcast_to(turned[:, head : head + 1], (SEQ_LEN, 128))


def decay_tile(columns, cum_ref, head, low, far):
    column = columns[head, low * TILE : (low + 1) * TILE]
    row = cum_ref[pl.ds(head, 1), far * TILE : (far + 1) * TILE]
    return jnp.exp(jnp.minimum(jnp.concatenate([column] * (TILE // 128), axis=1) - row, 0.0))


def lower_tile():
    shape = (TILE, TILE)
    return lax.broadcasted_iota(jnp.int32, shape, 0) >= lax.broadcasted_iota(jnp.int32, shape, 1)


def mixer_forward_kernel(
    unit_any,
    first_ref,
    weight_any,
    out_weight_ref,
    taps_ref,
    bias_ref,
    head_ref,
    gain_ref,
    skip_ref,
    cot_ref,
    shared_ref,
    shared_down_ref,
    proj_any,
    act_any,
    mixed_any,
    gated_any,
    part_any,
    side_ref,
    cum_ref,
    step_ref,
    cot_out,
    shared_out,
    shared_down_out,
    unit_ref,
    weight_ref,
    proj_ref,
    act_ref,
    mixed_ref,
    gated_ref,
    part_ref,
    padded,
    scores,
    columns,
    scaled_ref,
    c_send,
    c_recv,
    c_local,
    moves,
    u_send,
    u_recv,
    d_send,
    d_recv,
    keeps,
):
    moving = []

    def move(source, target):
        copy = pltpu.make_async_copy(source, target, moves.at[len(moving)])
        copy.start()
        moving.append(copy)

    move(weight_any, weight_ref)
    move(unit_any, unit_ref)
    me, slot, device = seq_axis()
    core, f_slot, f_device, twin = fsdp_axis()
    meet(ring_peers(device) + ring_peers(f_device) + [twin])
    mine = f_slot(0, False) * 2 + core
    started, u_started, d_started, crossing, kept = [], [], [], [], []
    program = ring_gather(
        cot_ref, lambda at, cut: cot_out.at[(at, *cut)], slot, device, sender(c_send, c_recv, started), nothing
    )
    next(program)
    keep = pltpu.make_async_copy(cot_ref, cot_out.at[me], c_local)
    keep.start()
    shards = [
        shard_gather(shared_ref, shared_out, u_send, u_recv, u_started, crossing),
        shard_gather(shared_down_ref, shared_down_out, d_send, d_recv, d_started, crossing, False),
    ]
    for index, (source, block) in enumerate(
        ((shared_ref, shared_out.at[mine]), (shared_down_ref, shared_down_out.at[mine]))
    ):
        kept.append(pltpu.make_async_copy(source, block, keeps.at[index]))
        kept[-1].start()
    follow("y", program, shards)
    for copy in moving:
        copy.wait()
    moving.clear()

    def rows_step(tile, carry):
        here = pl.ds(pl.multiple_of(tile * TILE, TILE), TILE)
        normed = (unit_ref[here, :].astype(FULL) * first_ref[...]).astype(LOW)
        for part in range(PROJ_HERE // 384):
            at = slice(part * 384, (part + 1) * 384)
            proj_ref[here, at] = dot(normed, weight_ref[:, at]).astype(LOW)
        return carry

    lax.fori_loop(0, TILES, rows_step, 0)
    move(proj_ref, proj_any)
    follow("yyyzz", program, shards)
    padded[0:8] = jnp.zeros((8, 128), FULL)
    for part in range(CONV_HERE // 128):
        at = slice(part * 128, (part + 1) * 128)
        padded[8:] = proj_ref[:, INNER_HERE + part * 128 : INNER_HERE + (part + 1) * 128].astype(FULL)
        before = bias_ref[0:1, at] + conv_taps(padded, taps_ref, at)
        act_ref[:, at] = (before * sigmoid(before)).astype(LOW)
    rates = proj_ref[:, INNER_HERE + CONV_HERE :].astype(FULL).T[:8] + head_ref[0][:, :1]
    step_ref[...] = jnp.maximum(rates, 0.0) + jnp.log1p(jnp.exp(-jnp.abs(rates)))
    cum_ref[...] = scan_lanes(step_ref[...] * head_ref[1][:, :1], False)
    scores_and_columns(
        act_ref[:, INNER_HERE : INNER_HERE + STATE],
        act_ref[:, INNER_HERE + STATE :],
        cum_ref[...],
        scores,
        columns,
    )
    move(act_ref, act_any)
    follow("yyz", program, shards)

    def pair_step(pair, carry):
        at = pl.ds(pl.multiple_of(pair * 128, 128), 128)
        for low in range(TILES):
            here = slice(low * TILE, (low + 1) * TILE)
            sums = [None, None]
            for far in range(low + 1):
                there = slice(far * TILE, (far + 1) * TILE)
                for half in range(2):
                    head = pair * 2 + half
                    weight = scores[here, there] * decay_tile(columns, cum_ref, head, low, far)
                    weight = weight * step_ref[pl.ds(head, 1), there]
                    if far == low:
                        weight = jnp.where(lower_tile(), weight, 0.0)
                    term = dot(weight.astype(LOW), act_ref[there, at])
                    sums[half] = term if far == 0 else sums[half] + term
            first = lax.broadcasted_iota(jnp.int32, (TILE, 128), 1) < HDIM
            x_tile = act_ref[here, at].astype(FULL)
            mixed = jnp.where(first, sums[0], sums[1]) + skip_ref[0:1, at] * x_tile
            gate = proj_ref[here, at].astype(FULL)
            gated = (mixed * (gate * sigmoid(gate))).astype(LOW)
            mixed_ref[here, at] = mixed
            gated_ref[here, at] = gated
            scaled_ref[here, at] = (gated.astype(FULL) * gain_ref[0:1, at]).astype(LOW)
        return carry

    lax.fori_loop(0, PAIRS, pair_step, 0)
    move(mixed_ref, mixed_any)
    move(gated_ref, gated_any)
    follow("yyyyzzzz", program, shards)

    def out_step(tile, carry):
        here = pl.ds(pl.multiple_of(tile * TILE, TILE), TILE)
        for part in range(D // 512):
            at = slice(part * 512, (part + 1) * 512)
            part_ref[here, at] = dot(scaled_ref[here, :], out_weight_ref[:, at]).astype(LOW)
        return carry

    lax.fori_loop(0, TILES, out_step, 0)
    move(part_ref, part_any)
    wide = gated_ref[...].astype(FULL)
    squares = lax.dot_general(
        jnp.ones((8, INNER_HERE), FULL),
        wide * wide,
        (((1,), (1,)), ((), ())),
        precision=HIGHEST,
        preferred_element_type=FULL,
    )
    for piece in range(GROUPS):
        side_ref[piece] = squares[:, piece * PIECE : (piece + 1) * PIECE]
    take_turns(program, *shards)
    for copy in moving + kept:
        copy.wait()
    for copy in crossing:
        copy.wait_recv()
    for copy in started + u_started + d_started:
        copy.wait_send()
    keep.wait()


def mixer_forward(unit_rows, gain_first, weights, out_weights, taps, bias, head_cols, gain, skip, piece, shared, shared_down):
    return pl.pallas_call(
        mixer_forward_kernel,
        out_shape=(
            jax.ShapeDtypeStruct((SEQ_LEN, PROJ_HERE), LOW),
            jax.ShapeDtypeStruct((SEQ_LEN, CONV_HERE), LOW),
            jax.ShapeDtypeStruct((SEQ_LEN, INNER_HERE), FULL),
            jax.ShapeDtypeStruct((SEQ_LEN, INNER_HERE), LOW),
            jax.ShapeDtypeStruct((SEQ_LEN, D), LOW),
            jax.ShapeDtypeStruct((GROUPS, 8, PIECE), FULL),
            jax.ShapeDtypeStruct((8, SEQ_LEN), FULL),
            jax.ShapeDtypeStruct((8, SEQ_LEN), FULL),
            jax.ShapeDtypeStruct((GROUPS, PIECE, D), LOW),
            jax.ShapeDtypeStruct((SHARDS, *shared.shape), LOW),
            jax.ShapeDtypeStruct((SHARDS, *shared_down.shape), LOW),
        ),
        in_specs=[any_spec(), vmem_spec(), any_spec()] + [vmem_spec()] * 6 + [any_spec()] * 3,
        out_specs=(any_spec(),) * 5 + (vmem_spec(),) * 3 + (any_spec(),) * 3,
        scratch_shapes=[
            pltpu.VMEM((SEQ_LEN, D), LOW),
            pltpu.VMEM((D, PROJ_HERE), LOW),
            pltpu.VMEM((SEQ_LEN, PROJ_HERE), LOW),
            pltpu.VMEM((SEQ_LEN, CONV_HERE), LOW),
            pltpu.VMEM((SEQ_LEN, INNER_HERE), FULL),
            pltpu.VMEM((SEQ_LEN, INNER_HERE), LOW),
            pltpu.VMEM((SEQ_LEN, D), LOW),
            pltpu.VMEM((SEQ_LEN + 8, 128), FULL),
            pltpu.VMEM((SEQ_LEN, SEQ_LEN), FULL),
            pltpu.VMEM((HEADS_HERE, SEQ_LEN, 128), FULL),
            pltpu.VMEM((SEQ_LEN, INNER_HERE), LOW),
            dma_sems(9),
            dma_sems(9),
            pltpu.SemaphoreType.DMA,
            dma_sems(6),
        ]
        + [dma_sems(19)] * 4
        + [dma_sems(2)],
        compiler_params=pltpu.CompilerParams(
            collective_id=3, has_side_effects=True, vmem_limit_bytes=52 << 20
        ),
        cost_estimate=BUSY,
        name="mixer_forward",
    )(unit_rows, gain_first, weights, out_weights, taps, bias, head_cols, gain, skip, piece, shared, shared_down)


def mixer_backward_kernel(
    grad_ref,
    proj_ref,
    act_ref,
    mixed_ref,
    cum_ref,
    step_ref,
    taps_ref,
    bias_ref,
    head_ref,
    skip_ref,
    block_ref,
    down_ref,
    owned_ref,
    out_ref,
    conv_ref,
    skip_grad_ref,
    head_grad_ref,
    block_out,
    down_out,
    owned_out,
    padded,
    trailing,
    scores,
    score_grad,
    columns,
    mixed_low,
    act_grad,
    size_rows,
    flow_rows,
    row_sums,
    mixed_back,
    *rest,
):
    me, slot, device = seq_axis()
    meet(ring_peers(device) + shard_peers())
    started = [[]]
    shards = shard_scatters(
        [
            (blocks_of(down_ref), down_out, rest[10 : 10 + SHARD_SCRATCH]),
            (blocks_of(owned_ref), owned_out, rest[10 + SHARD_SCRATCH :]),
        ],
        started,
    )
    send = sender(rest[8], rest[9], started[0])
    program = ring_scatter(block_of(block_ref, slot), slot, device, send, block_out, rest[:8])
    next(program)
    scores_and_columns(
        act_ref[:, INNER_HERE : INNER_HERE + STATE],
        act_ref[:, INNER_HERE + STATE :],
        cum_ref[...],
        scores,
        columns,
    )
    size_rows[...] = jnp.zeros((8, SEQ_LEN), FULL)
    flow_rows[...] = jnp.zeros((8, SEQ_LEN), FULL)
    for part in range(PAIRS):
        at = slice(part * 128, (part + 1) * 128)
        gate = proj_ref[:, at].astype(FULL)
        gate_sig = sigmoid(gate)
        grad = grad_ref[:, at].astype(FULL)
        mixed_grad = grad * (gate * gate_sig)
        out_ref[:, at] = (grad * mixed_ref[:, at] * (gate_sig * (1.0 + gate * (1.0 - gate_sig)))).astype(LOW)
        x_tile = act_ref[:, at].astype(FULL)
        skip_grad_ref[:, at] = jnp.broadcast_to(jnp.sum(mixed_grad * x_tile, axis=0, keepdims=True), (8, 128))
        mixed_low[:, at] = mixed_grad.astype(LOW)
        act_grad[:, at] = skip_ref[0:1, at] * mixed_grad
    follow("zzy", program, shards)

    def pair_step(pair):
        at = slice(pair * 128, (pair + 1) * 128)
        first = lax.broadcasted_iota(jnp.int32, (TILE, 128), 1) < HDIM
        for half in range(2):
            head = pair * 2 + half
            mine = first if half == 0 else jnp.logical_not(first)
            for low in range(TILES):
                here = slice(low * TILE, (low + 1) * TILE)
                grad = jnp.where(mine, mixed_low[here, at], jnp.zeros((TILE, 128), LOW))
                turned = mixed_low[here, at].T[half * HDIM : (half + 1) * HDIM]
                sums = jnp.zeros((TILE, 128), FULL)
                for far in range(low + 1):
                    there = slice(far * TILE, (far + 1) * TILE)
                    decay = decay_tile(columns, cum_ref, head, low, far)
                    if far == low:
                        decay = jnp.where(lower_tile(), decay, 0.0)
                    step = step_ref[pl.ds(head, 1), there]
                    scaled = dot_rhs_t(grad, act_ref[there, at]) * decay
                    product = scaled * scores[here, there]
                    size_rows[pl.ds(head, 1), there] += jnp.sum(product, axis=0, keepdims=True)
                    flow = product * step
                    for part in range(TILE // 128):
                        sums = sums + flow[:, part * 128 : (part + 1) * 128]
                    add = scaled * step
                    if half == 0 and pair == 0:
                        score_grad[here, there] = add
                    else:
                        score_grad[here, there] += add
                    weight = (scores[here, there] * decay * step).astype(LOW)
                    mixed_back[half * HDIM : (half + 1) * HDIM, there] += dot(turned, weight)
                row_sums[...] = sums
                flow_rows[pl.ds(head, 1), here] = lax.dot_general(
                    jnp.ones((8, 128), FULL),
                    row_sums[...],
                    (((1,), (1,)), ((), ())),
                    precision=HIGHEST,
                    preferred_element_type=FULL,
                )[:1]

    for pair in range(PAIRS):
        mixed_back[...] = jnp.zeros((128, SEQ_LEN), FULL)
        pair_step(pair)
        act_grad[:, pair * 128 : (pair + 1) * 128] += mixed_back[...].T
        follow(("yyz", "yz", "y")[pair], program, shards)

    b_at, c_at = INNER_HERE, INNER_HERE + STATE
    mixed_back[...] = jnp.zeros((128, SEQ_LEN), FULL)
    for low in range(TILES):
        here = slice(low * TILE, (low + 1) * TILE)
        for far in range(low + 1):
            there = slice(far * TILE, (far + 1) * TILE)
            high, rest = hi_lo(score_grad[here, there])
            b_tile, c_tile = act_ref[there, b_at:c_at], act_ref[here, c_at:]
            c_term = dot(high, b_tile) + dot(rest, b_tile)
            if far == 0:
                c_turned = c_tile.T
            mixed_back[:, there] += dot(c_turned, high) + dot(c_turned, rest)
            if far == 0:
                act_grad[here, c_at:] = c_term
            else:
                act_grad[here, c_at:] += c_term
    act_grad[:, b_at:c_at] = mixed_back[...].T

    step, size = step_ref[...], size_rows[...]
    decay_rate = head_ref[1][:, :1]
    back = scan_lanes(flow_rows[...] - step * size, True)
    rates = proj_ref[:, INNER_HERE + CONV_HERE :].astype(FULL).T[:8] + head_ref[0][:, :1]
    rate_grad = (size + back * decay_rate) * sigmoid(rates)
    real = lax.broadcasted_iota(jnp.int32, (8, SEQ_LEN), 0) < HEADS_HERE
    rate_grad = jnp.where(real, rate_grad, 0.0)
    head_grad_ref[0] = jnp.broadcast_to(jnp.sum(rate_grad, axis=1, keepdims=True), (8, 128))
    head_grad_ref[1] = jnp.broadcast_to(jnp.sum(back * step * decay_rate, axis=1, keepdims=True), (8, 128))
    turned = jnp.concatenate([rate_grad, jnp.zeros((120, SEQ_LEN), FULL)], axis=0).T
    out_ref[:, INNER_HERE + CONV_HERE :] = turned.astype(LOW)

    padded[0:8] = jnp.zeros((8, 128), FULL)
    trailing[SEQ_LEN:] = jnp.zeros((8, 128), FULL)
    for part in range(CONV_HERE // 128):
        at = slice(part * 128, (part + 1) * 128)
        wide = slice(INNER_HERE + part * 128, INNER_HERE + (part + 1) * 128)
        padded[8:] = proj_ref[:, wide].astype(FULL)
        before = bias_ref[0:1, at] + conv_taps(padded, taps_ref, at)
        gate = sigmoid(before)
        grad = act_grad[:, at] * (gate * (1.0 + before * (1.0 - gate)))
        trailing[:SEQ_LEN] = grad
        conv_ref[CONV : CONV + 1, at] = jnp.sum(grad, axis=0, keepdims=True)
        total = None
        for tap in range(CONV):
            conv_ref[tap : tap + 1, at] = jnp.sum(
                trailing[:SEQ_LEN] * padded[5 + tap : 5 + tap + SEQ_LEN], axis=0, keepdims=True
            )
            shift = CONV - 1 - tap
            term = taps_ref[tap : tap + 1, at] * trailing[shift : shift + SEQ_LEN]
            total = term if total is None else total + term
        out_ref[:, wide] = total.astype(LOW)
    conv_ref[CONV + 1 :] = jnp.zeros((3, CONV_HERE), FULL)
    take_turns(program, *shards)
    for copies in started:
        for copy in copies:
            copy.wait_send()


def mixer_backward(grad, projected, act, mixed, cum, step, taps, bias, head_cols, skip, blocks, downs, owned):
    return pl.pallas_call(
        mixer_backward_kernel,
        out_shape=(
            jax.ShapeDtypeStruct((SEQ_LEN, PROJ_HERE), LOW),
            jax.ShapeDtypeStruct((8, CONV_HERE), FULL),
            jax.ShapeDtypeStruct((8, INNER_HERE), FULL),
            jax.ShapeDtypeStruct((2, 8, 128), FULL),
            jax.ShapeDtypeStruct((PIECE, D), FULL),
            jax.ShapeDtypeStruct((32, D), FULL),
            jax.ShapeDtypeStruct((32, D), FULL),
        ),
        in_specs=[vmem_spec()] * 13,
        out_specs=(vmem_spec(),) * 7,
        scratch_shapes=[
            pltpu.VMEM((SEQ_LEN + 8, 128), FULL),
            pltpu.VMEM((SEQ_LEN + 8, 128), FULL),
            pltpu.VMEM((SEQ_LEN, SEQ_LEN), FULL),
            pltpu.VMEM((SEQ_LEN, SEQ_LEN), FULL),
            pltpu.VMEM((HEADS_HERE, SEQ_LEN, 128), FULL),
            pltpu.VMEM((SEQ_LEN, INNER_HERE), LOW),
            pltpu.VMEM((SEQ_LEN, CONV_HERE), FULL),
            pltpu.VMEM((8, SEQ_LEN), FULL),
            pltpu.VMEM((8, SEQ_LEN), FULL),
            pltpu.VMEM((TILE, 128), FULL),
            pltpu.VMEM((128, SEQ_LEN), FULL),
        ]
        + scatter_buffers(PIECE, D)
        + [dma_sems(13), dma_sems(13)]
        + shard_scratch(downs)
        + shard_scratch(owned),
        compiler_params=pltpu.CompilerParams(
            collective_id=9, has_side_effects=True, vmem_limit_bytes=52 << 20
        ),
        cost_estimate=BUSY,
        name="mixer_backward",
    )(grad, projected, act, mixed, cum, step, taps, bias, head_cols, skip, blocks, downs, owned)


def adam_update(weight, old_first, old_second, gradient, step_rate, decay_rate):
    first_new = BETA_FIRST * old_first + (1.0 - BETA_FIRST) * gradient
    second_new = BETA_SECOND * old_second + (1.0 - BETA_SECOND) * gradient * gradient
    first_hat = first_new / (1.0 - BETA_FIRST**STEP)
    second_hat = second_new / (1.0 - BETA_SECOND**STEP)
    weight_new = weight - step_rate * (
        first_hat / (jnp.sqrt(second_hat) + ADAM_EPSILON) + decay_rate * weight
    )
    return (weight_new, first_new, second_new)


def update_kernel(dense_ref, shared_ref, aux_ref, owned_ref, up_ref, down_ref, gain_ref, *refs):
    olds = [refs[3 * index : 3 * index + 3] for index in range(9)]
    news = [refs[27 + 3 * index : 27 + 3 * index + 3] for index in range(9)]

    def step(index, gradient, rate, decay, at=()):
        old, new = olds[index], news[index]
        values = adam_update(old[0][at], old[1][at], old[2][at], gradient, rate, decay)
        for ref, value in zip(new, values):
            ref[at] = value

    rows = slice(None)
    state, rates = None, None
    place_row = lax.broadcasted_iota(jnp.int32, (128, 128), 0)
    place_col = lax.broadcasted_iota(jnp.int32, (128, 128), 1)
    for group in range(GROUPS):
        block = dense_ref[group].astype(FULL)
        for half in range(2):
            begin = half * INNER + group * INNER_HERE
            gradient = block[:, half * INNER_HERE : (half + 1) * INNER_HERE] * gain_ref[...]
            step(0, gradient, RATE_MATRIX, WEIGHT_DECAY, (rows, slice(begin, begin + INNER_HERE)))
            begin = half * FF_SH + group * SH_HERE
            gradient = shared_ref[group, :, half * SH_HERE : (half + 1) * SH_HERE].astype(FULL)
            step(1, gradient, RATE_MATRIX, WEIGHT_DECAY, (rows, slice(begin, begin + SH_HERE)))
        part = block[:, 2 * INNER_HERE : 2 * INNER_HERE + 2 * STATE]
        state = part if group == 0 else state + part
        moved = jnp.logical_and(place_row < HEADS_HERE, place_col == place_row + group * HEADS_HERE)
        part = dot(dense_ref[group, :, INNER_HERE + CONV_HERE : PROJ_HERE], moved.astype(LOW))
        rates = part if group == 0 else rates + part
    state, rates = state * gain_ref[...], rates * gain_ref[...]
    step(0, state, RATE_MATRIX, WEIGHT_DECAY, (rows, slice(2 * INNER, 2 * INNER + 2 * STATE)))
    step(0, rates[:, :HEADS], RATE_MATRIX, WEIGHT_DECAY, (rows, slice(INNER + CHANNELS, INNER + CHANNELS + HEADS)))
    step(2, owned_ref[:24], RATE_MATRIX, WEIGHT_DECAY, (slice(0, 24),))
    step(3, owned_ref[24:], RATE_MATRIX, WEIGHT_DECAY, (slice(0, 8),))

    def expert_step(index, sums, width, rate):
        def turn(count, carry):
            for row in range(8):
                at = count * 8 + row
                step(index, sums[pl.ds(at, 1), :width], rate, WEIGHT_DECAY, (at,))
            return carry

        lax.fori_loop(0, sums.shape[0] // 8, turn, 0)

    expert_step(4, up_ref, 2 * FF_EXP, RATE_MATRIX)
    expert_step(5, down_ref, D, RATE_DOWN)
    aux = aux_ref[0]
    for group in range(1, GROUPS):
        aux = aux + aux_ref[group]
    small = jnp.concatenate([aux[0:1], aux[1:2]], axis=1)[:, :178]
    step(6, small, RATE_SMALL, 0.0, (slice(0, 1),))
    step(7, aux[2:3, :96], RATE_MATRIX, WEIGHT_DECAY, (slice(0, 1),))
    step(8, aux[3:6, :HEADS], RATE_HEAD, 0.0, (slice(0, 3),))


def update(sums, triples):
    olds = [values for triple in triples for values in triple]
    news = pl.pallas_call(
        update_kernel,
        out_shape=tuple(jax.ShapeDtypeStruct(values.shape, FULL) for values in olds),
        in_specs=[vmem_spec()] * (7 + len(olds)),
        out_specs=(vmem_spec(),) * len(olds),
        compiler_params=pltpu.CompilerParams(vmem_limit_bytes=52 << 20),
        name="update",
    )(*sums, *olds)
    return [news[3 * index : 3 * index + 3] for index in range(len(triples))]


def route_combine(logit_values, onehot):
    picked = jnp.sum(logit_values[:, None, :] * onehot, axis=-1)
    route_probs = jax.nn.softmax(picked, axis=-1)
    return jnp.sum(route_probs[:, :, None] * onehot, axis=1)


def inverse_rms(values):
    return lax.rsqrt(jnp.mean(values * values, axis=-1, keepdims=True) + NORM_EPSILON)


def norm_back(values, inverse, gain, grad):
    shared = grad * gain
    inner = jnp.mean(values * shared, axis=-1, keepdims=True)
    grad_in = inverse * shared - values * (inverse * inverse * inverse * inner)
    return grad_in, jnp.sum(values * inverse * grad, axis=0)


def silu_slope(values, gate):
    return gate * (1.0 + values * (1.0 - gate))


def dot(left, right):
    return jnp.dot(left, right, preferred_element_type=FULL)


def dot_lhs_t(left, right):
    return lax.dot_general(left, right, (((0,), (0,)), ((), ())), preferred_element_type=FULL)


def dot_rhs_t(left, right):
    return lax.dot_general(left, right, (((1,), (1,)), ((), ())), preferred_element_type=FULL)


def side_rows(values):
    return jnp.pad(values, ((0, 0), (0, 7), (0, 0)))


def piece_order(forward):
    order = []
    for shard in range(SHARDS):
        for group in range(GROUPS):
            owner = shard * GROUPS + group
            user = ((shard % 2) * GROUPS + group) * GROUPS + shard // 2
            order.append((owner, user) if forward else (user, owner))
    return order


def local(
    hidden,
    cotangent,
    routes,
    head_params,
    head_first,
    head_second,
    small_params,
    small_first,
    small_second,
    proj_weight,
    proj_first,
    proj_second,
    out_weight,
    out_first,
    out_second,
    router_weight,
    router_first,
    router_second,
    experts_up,
    experts_up_first,
    experts_up_second,
    experts_down,
    experts_down_first,
    experts_down_second,
    shared_up,
    shared_up_first,
    shared_up_second,
    shared_down,
    shared_down_first,
    shared_down_second,
):
    group_index = lax.axis_index("seq")
    both = ("fsdp", "seq")
    inputs = hidden[0]
    out_grad = cotangent[0]

    proj_low = proj_weight.astype(LOW)
    misc = jnp.concatenate(
        [router_weight.astype(LOW), jnp.pad(small_params.astype(LOW), (0, 2)).reshape(12, SMALL_COLS)],
        axis=1,
    )
    columns = jnp.concatenate(
        [
            proj_low[:, :INNER].reshape(12, GROUPS, INNER_HERE),
            proj_low[:, INNER : 2 * INNER].reshape(12, GROUPS, INNER_HERE),
            jnp.broadcast_to(proj_low[:, None, 2 * INNER : INNER + CHANNELS], (12, GROUPS, 2 * STATE)),
            proj_low[:, INNER + CHANNELS :].reshape(12, GROUPS, HEADS_HERE),
            jnp.broadcast_to(misc[:, None], (12, GROUPS, 8 + SMALL_COLS)),
            jnp.zeros((12, GROUPS, 128 - HEADS_HERE - 8 - SMALL_COLS), LOW),
            shared_up.astype(LOW).reshape(12, 2, GROUPS, SH_HERE)[:, 0],
            shared_up.astype(LOW).reshape(12, 2, GROUPS, SH_HERE)[:, 1],
        ],
        axis=2,
    )
    columns = columns_out(columns.transpose(1, 0, 2)).reshape(96, -1)
    owned = jnp.concatenate([out_weight.astype(LOW), shared_down.astype(LOW)], axis=0)
    owned = lax.ppermute(owned, both, piece_order(True))

    first_inverse = inverse_rms(inputs)
    unit_rows, weights, out_here = start_gather(
        (inputs * first_inverse).astype(LOW), columns[:, :PROJ_HERE], owned[:24]
    )

    misc_at = INNER_HERE + CONV_HERE + HEADS_HERE
    misc = weights[:, misc_at : misc_at + EXPERTS + SMALL_COLS]
    router_full = misc[:, :EXPERTS]
    small_vec = (
        misc[:, EXPERTS:].reshape(SHARDS * GROUPS, 12 * SMALL_COLS)[:, :178].reshape(SMALL).astype(FULL)
    )
    gain_first, gain_second = small_vec[:D], small_vec[D : 2 * D]
    gain_mixer = lax.dynamic_slice_in_dim(small_vec, 2 * D + group_index * INNER_HERE, INNER_HERE)
    bias_all = small_vec[2 * D + INNER : 2 * D + INNER + CHANNELS]
    kernel_all = small_vec[2 * D + INNER + CHANNELS :].reshape(CONV, CHANNELS)
    conv_bias = jnp.concatenate(
        [lax.dynamic_slice_in_dim(bias_all, group_index * INNER_HERE, INNER_HERE), bias_all[INNER:]]
    )
    conv_kernel = jnp.concatenate(
        [
            lax.dynamic_slice_in_dim(kernel_all, group_index * INNER_HERE, INNER_HERE, 1),
            kernel_all[:, INNER:],
        ],
        axis=1,
    )
    head_local = lax.dynamic_slice_in_dim(head_params, group_index * HEADS_HERE, HEADS_HERE, 1)

    head_cols = jnp.stack([head_local[0], -jnp.exp(head_local[1])])
    head_cols = jnp.broadcast_to(jnp.pad(head_cols, ((0, 0), (0, 2)))[:, :, None], (2, 8, 128))
    skip_wide = jnp.repeat(head_local[2], HDIM)[None]
    projected, act, mixed, gated, out_part, square_side, cum_rows, step_rows, rows_cot, shared_here, shared_down_here = mixer_forward(
        unit_rows,
        gain_first[None],
        weights,
        out_here,
        conv_kernel,
        conv_bias[None],
        head_cols,
        gain_mixer[None],
        skip_wide,
        out_grad.astype(LOW),
        columns[:, PROJ_HERE:],
        owned[24:],
    )
    shared_here, shared_down_here = shared_here.reshape(D, 2 * SH_HERE), shared_down_here.reshape(SH_HERE, D)
    rows_cot = rows_cot.reshape(SEQ_LEN, D)
    raw_out, squares, up_here, down_here = mixed_scatter(
        out_part.reshape(GROUPS, PIECE, D),
        square_side,
        experts_up.reshape(96, 2 * FF_EXP).astype(LOW),
        experts_down.reshape(32, D).astype(LOW),
    )
    mixer_inverse = lax.rsqrt(jnp.sum(squares[:, 0], axis=0)[:, None] / INNER + NORM_EPSILON)
    middle = inputs + mixer_inverse * raw_out

    second_inverse = inverse_rms(middle)
    normed_two = (middle * second_inverse * gain_second).astype(LOW)
    logits = dot(normed_two, router_full)
    onehot = (routes[0][:, :, None] == jnp.arange(EXPERTS, dtype=jnp.int32)).astype(FULL)
    combine, route_pull = jax.vjp(lambda values: route_combine(values, onehot), logits)
    back_sum, combine_sides, block_part, up_total_grad, down_total_grad, shared_down_total_grad = experts(
        normed_two, combine.T, rows_cot.reshape(GROUPS, PIECE, D), up_here, shared_here, down_here, shared_down_here
    )

    logits_grad = route_pull(combine_sides[:, 0].T)[0].astype(LOW)
    normed_two_grad = back_sum + dot_rhs_t(logits_grad, router_full)
    router_grad = dot_lhs_t(normed_two, logits_grad)
    middle_from_norm, gain_second_grad = norm_back(middle, second_inverse, gain_second, normed_two_grad)
    middle_grad = out_grad + middle_from_norm
    mixer_grad = middle_grad.astype(LOW)
    mixer_inner = jnp.sum(mixer_grad.astype(FULL) * raw_out, axis=1, keepdims=True) / INNER
    mixer_fix = mixer_inverse * mixer_inverse * mixer_inverse * mixer_inner
    rows_mixer, stats, up_sum = middle_gather(
        mixer_grad,
        jnp.pad(jnp.concatenate([mixer_inverse, mixer_fix], axis=1).T, ((0, 6), (0, 0))),
        up_total_grad.reshape(SHARDS, 96, 2 * FF_EXP + 2 * SH_HERE),
    )

    rows_inverse = stats[:, 0].reshape(SEQ_LEN, 1)
    rows_fix = stats[:, 1].reshape(SEQ_LEN, 1)
    gated = gated.astype(FULL)
    gated_normed = (gated * rows_inverse * gain_mixer).astype(LOW)
    out_total_grad = dot_lhs_t(gated_normed, rows_mixer).astype(LOW)
    gated_normed_grad = dot_rhs_t(rows_mixer, out_here)
    gain_mixer_grad = jnp.sum(gated * rows_inverse * gated_normed_grad, axis=0)
    gated_grad = (rows_inverse * gain_mixer * gated_normed_grad - gated * rows_fix).astype(LOW)
    owned_grad = jnp.concatenate(
        [out_total_grad.reshape(SHARDS, 24, D), shared_down_total_grad.reshape(SHARDS, 8, D)], axis=1
    )

    proj_grad, conv_grads, skip_sums, head_sums, block_sum, down_sum, owned_sum = mixer_backward(
        gated_grad,
        projected,
        act,
        mixed,
        cum_rows,
        step_rows,
        conv_kernel,
        conv_bias[None],
        head_cols,
        skip_wide,
        block_part,
        down_total_grad.reshape(SHARDS, 32, D),
        owned_grad,
    )
    owned_sum = lax.ppermute(owned_sum.astype(LOW), both, piece_order(False)).astype(FULL)
    block_out = middle + block_sum
    conv_kernel_grad, conv_bias_grad = conv_grads[:CONV], conv_grads[CONV]
    skip_grad = jnp.sum(skip_sums[0].reshape(HEADS_HERE, HDIM), axis=1)
    bias_grad, log_decay_grad = head_sums[0, :HEADS_HERE, 0], head_sums[1, :HEADS_HERE, 0]
    unit_grad = dot_lhs_t(unit_rows, proj_grad)
    gain_first_grad = jnp.sum(unit_grad * weights.astype(FULL), axis=1)

    place = group_index * INNER_HERE
    kernel_wide = jnp.concatenate([jnp.zeros((CONV, INNER), FULL), conv_kernel_grad[:, INNER_HERE:]], axis=1)
    kernel_wide = lax.dynamic_update_slice_in_dim(kernel_wide, conv_kernel_grad[:, :INNER_HERE], place, 1)
    bias_wide = jnp.concatenate([jnp.zeros((INNER,), FULL), conv_bias_grad[INNER_HERE:]])
    bias_wide = lax.dynamic_update_slice_in_dim(bias_wide, conv_bias_grad[:INNER_HERE], place, 0)
    gain_wide = lax.dynamic_update_slice_in_dim(jnp.zeros((INNER,), FULL), gain_mixer_grad, place, 0)
    small_grad = jnp.concatenate(
        [gain_first_grad, gain_second_grad, gain_wide, bias_wide, kernel_wide.reshape(-1)]
    )
    small_grad = jnp.pad(small_grad.reshape(SHARDS * GROUPS, 178), ((0, 0), (0, 78))).reshape(SHARDS, 16, 128)
    router_rows = jnp.pad(router_grad.reshape(SHARDS, GROUPS, 96), ((0, 0), (0, 0), (0, 32)))
    head_grad = jnp.stack([bias_grad, log_decay_grad, skip_grad])
    head_rows = lax.dynamic_update_slice_in_dim(
        jnp.zeros((3, 128), FULL), head_grad, group_index * HEADS_HERE, 1
    )
    head_rows = jnp.pad(jnp.concatenate(hi_lo(head_rows)), ((0, 2), (0, 0)))
    aux_grad = jnp.concatenate(
        [
            small_grad.astype(LOW),
            router_rows.astype(LOW),
            jnp.broadcast_to(head_rows, (SHARDS, 8, 128)),
        ],
        axis=1,
    )
    normed_grad, column_sum, aux_sum = last_scatter(
        proj_grad, weights, unit_grad.astype(LOW).reshape(SHARDS, 96, PROJ_HERE), aux_grad
    )
    input_from_norm, unused = norm_back(inputs, first_inverse, gain_first, normed_grad)
    hidden_grad = middle_grad + input_from_norm

    shared_back = up_sum[:, 2 * FF_EXP :].astype(LOW).reshape(GROUPS, 12, 2 * SH_HERE)
    aux_side = jnp.concatenate(
        [
            aux_sum[:16].reshape(GROUPS, 2, 128),
            aux_sum[16:24].reshape(GROUPS, 1, 128),
            jnp.broadcast_to(aux_sum[24:27] + aux_sum[27:30], (GROUPS, 3, 128)),
            jnp.zeros((GROUPS, 2, 128), FULL),
        ],
        axis=1,
    )
    dense, shared_back, aux_back = columns_back(
        column_sum.astype(LOW).reshape(GROUPS, 12, PROJ_HERE), shared_back, aux_side
    )
    owner = lax.axis_index("fsdp") * GROUPS + group_index
    own_gain = lax.dynamic_slice_in_dim(gain_first, owner * 12, 12)[:, None]
    small_rows = [values[None] for values in (small_params, small_first, small_second)]
    router_rows = [values.reshape(1, 96) for values in (router_weight, router_first, router_second)]
    news = update(
        (dense, shared_back, aux_back, owned_sum, up_sum, down_sum, own_gain),
        (
            (proj_weight, proj_first, proj_second),
            (shared_up, shared_up_first, shared_up_second),
            (out_weight, out_first, out_second),
            (shared_down, shared_down_first, shared_down_second),
            (experts_up, experts_up_first, experts_up_second),
            (experts_down, experts_down_first, experts_down_second),
            small_rows,
            router_rows,
            (head_params, head_first, head_second),
        ),
    )
    proj_new, shared_up_new, out_new, shared_down_new, up_new, down_new, small_new, router_new, head_new = news
    small_new = [values[0] for values in small_new]
    router_new = [values.reshape(12, EXPERTS) for values in router_new]
    return (
        block_out[None],
        hidden_grad[None],
        *head_new,
        *small_new,
        *proj_new,
        *out_new,
        *router_new,
        *up_new,
        *down_new,
        *shared_up_new,
        *shared_down_new,
    )


def solution(mesh):
    return jax.shard_map(
        local,
        mesh=mesh,
        in_specs=(
            P("fsdp", "seq", None),
            P("fsdp", "seq", None),
            P("fsdp", "seq", None),
            P(),
            P(),
            P(),
            P(("fsdp", "seq")),
            P(("fsdp", "seq")),
            P(("fsdp", "seq")),
            P(("fsdp", "seq"), None),
            P(("fsdp", "seq"), None),
            P(("fsdp", "seq"), None),
            P(("fsdp", "seq"), None),
            P(("fsdp", "seq"), None),
            P(("fsdp", "seq"), None),
            P(("fsdp", "seq"), None),
            P(("fsdp", "seq"), None),
            P(("fsdp", "seq"), None),
            P("fsdp", "seq", None),
            P("fsdp", "seq", None),
            P("fsdp", "seq", None),
            P("fsdp", "seq", None),
            P("fsdp", "seq", None),
            P("fsdp", "seq", None),
            P(("fsdp", "seq"), None),
            P(("fsdp", "seq"), None),
            P(("fsdp", "seq"), None),
            P(("fsdp", "seq"), None),
            P(("fsdp", "seq"), None),
            P(("fsdp", "seq"), None),
        ),
        out_specs=(
            P("fsdp", "seq", None),
            P("fsdp", "seq", None),
            P(),
            P(),
            P(),
            P(("fsdp", "seq")),
            P(("fsdp", "seq")),
            P(("fsdp", "seq")),
            P(("fsdp", "seq"), None),
            P(("fsdp", "seq"), None),
            P(("fsdp", "seq"), None),
            P(("fsdp", "seq"), None),
            P(("fsdp", "seq"), None),
            P(("fsdp", "seq"), None),
            P(("fsdp", "seq"), None),
            P(("fsdp", "seq"), None),
            P(("fsdp", "seq"), None),
            P("fsdp", "seq", None),
            P("fsdp", "seq", None),
            P("fsdp", "seq", None),
            P("fsdp", "seq", None),
            P("fsdp", "seq", None),
            P("fsdp", "seq", None),
            P(("fsdp", "seq"), None),
            P(("fsdp", "seq"), None),
            P(("fsdp", "seq"), None),
            P(("fsdp", "seq"), None),
            P(("fsdp", "seq"), None),
            P(("fsdp", "seq"), None),
        ),
        check_vma=False,
    )
```

time: 4930 us -> 388 us (0.08)
  blocking collectives: 2230 us -> 0 us
  waiting for transfers between devices: 1560 us -> 0.01 us
  starting transfers between devices: 404 us -> 12.8 us
  local copies, waits for them, and re-layouts: 395 us -> 29.6 us
  Pallas kernels: 0 us -> 309 us
  matrix products: 181 us -> 17.8 us
  other arithmetic: 112 us -> 13 us
    unnamed x3 -> x0, blocking collectives: 1790 us -> none
    all_gather x8 -> x0, waiting for transfers between devices: 909 us -> none  [the longest x1 292 us: local(): lax.all_gather(dense_low[5], ('fsdp', 'seq'), axis=0, tiled=True)]
    reduce_scatter x5 -> x0, waiting for transfers between devices: 526 us -> none  [the longest x1 448 us: local(): lax.psum_scatter(out_weight_grad, ('fsdp', 'seq'), scatter_dimension=0, t...]
    unnamed x68 -> x0, starting transfers between devices: 367 us -> none
    all_gather x2 -> x0, blocking collectives: 342 us -> none  [the longest x1 305 us: local(): lax.all_gather(dense_low[3], ('fsdp', 'seq'), axis=0, tiled=True)]
    pallas_call x0 -> x10, Pallas kernels: none -> 309 us  [the longest x1 65.1 us: experts(): pl.pallas_call(experts_kernel, out_shape=(jax.ShapeDtypeStruct((PIECE, D)...]
    unnamed x305 -> x128, local copies, waits for them, and re-layouts: 302 us -> 17.4 us
    dot_general x27 -> x6, matrix products: 181 us -> 17.8 us  [the longest x3 11.4 us: dot_lhs_t(): lax.dot_general(left, right, (((0,), (0,)), ((), ())), preferred_element_...]
  transfers between devices with their start and end apart: 88 -> 2, of which waited for: 23 -> 0; matrix products, arithmetic and copies ran while one was open for 47% -> 3% of each run, Pallas kernels for 0% -> 6%
where the time goes in v1:
time: 388 us; the launch traced here: 385 us
  Pallas kernels  309 us (80%)
  local copies, waits for them, and re-layouts  29.6 us (8%)
  matrix products  17.8 us (5%)
  other arithmetic  13 us (3%)
  starting transfers between devices  12.8 us (3%)
    pallas_call x1, Pallas kernels, experts(): pl.pallas_call(experts_kernel, out_shape=(jax.ShapeDtypeStruct((PIECE, D)...  65.1 us
    pallas_call x1, Pallas kernels, middle_gather(): pl.pallas_call(middle_kernel, out_shape=(jax.ShapeDtypeStruct((GROUPS, ro...  41.7 us
    pallas_call x1, Pallas kernels, mixer_forward(): pl.pallas_call(mixer_forward_kernel, out_shape=(jax.ShapeDtypeStruct((SEQ...  39.6 us
    pallas_call x1, Pallas kernels, mixer_backward(): pl.pallas_call(mixer_backward_kernel, out_shape=(jax.ShapeDtypeStruct((SE...  38.2 us
    pallas_call x1, Pallas kernels, start_gather(): pl.pallas_call(start_kernel, out_shape=(jax.ShapeDtypeStruct((GROUPS, row...  35 us
    pallas_call x1, Pallas kernels, last_scatter(): pl.pallas_call(last_kernel, out_shape=(jax.ShapeDtypeStruct((rows, width)...  32.4 us
    pallas_call x1, Pallas kernels, mixed_scatter(): pl.pallas_call(mixed_kernel, out_shape=(jax.ShapeDtypeStruct((rows, width...  28.5 us
    unnamed x128, local copies, waits for them, and re-layouts  17.4 us
  transfers between devices with their start and end apart: 2, of which 0 were waited for; matrix products, arithmetic and copies ran while one was open for 3% of the time, Pallas kernels for 6%

profile of v1, /device:TPU:1, one launch (start us, length us, event | category | flops | bytes accessed | tf_op | source)
XLA Modules:
  0.0 384.7 jit_solution(4253021293225073912)
XLA Ops:
  0.7 1.0 convert_element_type.113
  1.7 0.8 convert_element_type.114
  2.5 6.2 %collective-permute-start = (bf16[32,1536]{1,0:T(8,128)(2,1)S(1)}, bf16[32,1536]{1,0:T(8,128)(2,1)S(1)}, u32[]{:S(2)}, u32[]{:S(2)}) collective-permute-start(bf16[32,1536]{1,0:T(8,128)(2,1)S(1)} %pad_maximum_fusion.1), channel_id=1, source_target_pairs={{0,0},{1,8},{2,16},{3,24},{4,32},{5,40},{6,48},{7,56},{8,64},{9,72... | collective-permute-start | bytes 294920 | tf_op jit(solution)/shard_map/ppermute | solution.py:1558
  8.7 1.0 convert_element_type.109
  10.5 0.8 concatenate.41
  11.3 10.5 %columns_out.1 = bf16[8,12,1408]{2,1,0:T(8,128)(2,1)} custom-call(bf16[8,12,1408]{2,1,0:T(8,128)(2,1)} %bitcast.126), custom_call_target="tpu_custom_call" | custom-call | flops 30000001024 | bytes 4000000 | tf_op jit(solution)/shard_map/columns_out/pallas_call | solution.py:862
  21.9 1.1 reshape.331
  23.1 0.7 slice.177.rest_0_
  24.1 0.9 fusion.8.x_ref
  25.8 0.6 pad.37.clone
  26.4 0.6 slice.178.rest_1_
  27.0 35.0 %rows_first.1 = (bf16[8,128,1536]{2,1,0:T(8,128)(2,1)}, bf16[16,96,1152]{2,1,0:T(8,128)(2,1)}, bf16[16,24,1536]{2,1,0:T(8,128)(2,1)}) custom-call(bf16[128,1536]{1,0:T(8,128)(2,1)} %fusion.8.x_ref, bf16[96,1152]{1,0:T(8,128)(2,1)} %slice.177.rest_0_, bf16[24,1536]{1,0:T(8,128)(2,1)} %slice.178.rest_1_), custom_call_target="tpu_custom_call" | custom-call | flops 30000001024 | bytes 4000000 | tf_op jit(solution)/shard_map/rows_first/pallas_call | solution.py:314
  62.1 1.2 slice.179
  63.3 0.2 reshape.334
  64.0 0.3 copy-done.43
  64.5 39.6 %mixer_forward.1 = (bf16[1024,1152]{1,0:T(8,128)(2,1)}, bf16[1024,640]{1,0:T(8,128)(2,1)}, f32[1024,384]{1,0:T(8,128)}, bf16[1024,384]{1,0:T(8,128)(2,1)S(1)}, b...) custom-call(bf16[1024,1536]{1,0:T(8,128)(2,1)} %bitcast.150, ...), custom_call_target="tpu_custom_call" | custom-call | flops 30000001024 | bytes 4000000 | tf_op jit(solution)/shard_map/mixer_forward/pallas_call | solution.py:1122
  104.1 0.7 copy-done.29
  104.9 1.9 copy-done.27
  106.7 28.5 %mixer_out.1 = (f32[128,1536]{1,0:T(8,128)S(1)}, f32[8,8,128]{2,1,0:T(8,128)S(1)}, bf16[16,96,1024]{2,1,0:T(8,128)(2,1)S(1)}, bf16[16,32,1536]{2,1,0:T(8,128)(2,1)S(1)}) custom-call(bf16[8,128,1536]{2,1,0:T(8,128)(2,1)S(1)} %bitcast.119, f32[8,8,128]{2,1,0:T(8,128)S(1)} %get-tuple-element.100.side_ref, bf16[96,1024]{1,0:T(8,128)(2,1)S(1)} %bitcast.112, ...), custom_call_target="tpu_custom_call" | custom-call | flops 30000001024 | bytes 4000000 | tf_op jit(solution)/shard_map/mixer_out/pallas_call | solution.py:434
  135.3 1.6 copy-done.26
  136.9 1.2 copy-done.28
  138.1 0.3 multiply_reduce_fusion.4
  138.4 0.9 copy-done.32
  139.4 1.6 fusion.17
  141.2 0.6 select_reduce_fusion.2
  141.8 65.1 %experts.1 = (f32[128,1536]{1,0:T(8,128)}, f32[8,8,128]{2,1,0:T(8,128)}, bf16[8,128,1536]{2,1,0:T(8,128)(2,1)}, bf16[1536,1280]{1,0:T(8,128)(2,1)}, bf16[512,153...) custom-call(bf16[128,1536]{1,0:T(8,128)(2,1)} %copy-done.35, f32[8,128]{1,0:T(8,128)} %bitcast.140, ...), custom_call_target="tpu_custom_call" | custom-call | flops 30000001024 | bytes 4000000 | tf_op jit(solution)/shard_map/experts/pallas_call | solution.py:809
  206.9 0.9 slice.154
  207.9 1.8 multiply_reduce_fusion.1
  209.8 1.3 multiply_reduce_fusion.2
  211.0 41.7 %rows_mixer.1 = (bf16[8,128,1536]{2,1,0:T(8,128)(2,1)S(1)}, f32[8,8,128]{2,1,0:T(8,128)S(1)}, f32[96,1280]{1,0:T(8,128)S(1)}) custom-call(bf16[128,1536]{1,0:T(8,128)(2,1)S(1)} %get-tuple-element.257.x_ref, f32[8,128]{1,0:T(8,128)S(1)} %pad.30.side_ref, bf16[16,96,1280]{2,1,0:T(8,128)(2,1)} %bitcast.149), custom_call_target="tpu_custom_call" | custom-call | flops 30000001024 | bytes 4000000 | tf_op jit(solution)/shard_map/rows_mixer/pallas_call | solution.py:582
  252.8 1.5 convolution_convert_fusion
  254.3 2.9 fusion.3
  257.2 1.3 pad_maximum_fusion.owned_ref
  258.6 38.2 %mixer_backward.1 = (bf16[1024,1152]{1,0:T(8,128)(2,1)}, f32[8,640]{1,0:T(8,128)S(1)}, f32[8,384]{1,0:T(8,128)S(1)}, f32[2,8,128]{2,1,0:T(8,128)S(1)}, f32[128,1...) custom-call(bf16[1024,384]{1,0:T(8,128)(2,1)} %get-tuple-element.264.grad_ref, ...), custom_call_target="tpu_custom_call" | custom-call | flops 30000001024 | bytes 4000000 | tf_op jit(solution)/shard_map/mixer_backward/pallas_call | solution.py:1338
  297.1 9.8 %multiply_reduce_fusion = (bf16[1536]{0:T(1024)(128)(2,1)S(1)}, bf16[1536,1152]{1,0:T(8,128)(2,1)}) fusion(bf16[16,96,1152]{2,1,0:T(8,128)(2,1)} %get-tuple-element.97, bf16[1024,1536]{1,0:T(8,128)(2,1)} %bitcast.151, bf16[1024,1152]{1,0:T(8,128)(2,1)} %get-tuple-element.123.g_ref), kind=kOutput, calls=%fused_computation | convolution fusion | flops 3630955008 | bytes 12585984 | tf_op jit(solution)/shard_map/dot_general | solution.py:1480
  307.0 0.3 dynamic-update-slice
  307.3 0.3 dynamic-update-slice.1
  307.6 0.2 dynamic_update_slice.12
  307.8 0.3 dynamic-update-slice.3
  308.1 0.4 dynamic-update-slice.4
  308.5 0.2 reshape.349
  309.2 0.4 dynamic_update_slice.15
  309.9 0.2 reshape.350
  310.2 2.0 copy-done.6
  312.2 2.0 copy-done.25
  314.2 1.7 copy-done.30
  315.8 32.4 %rows_last.1 = (f32[128,1536]{1,0:T(8,128)S(1)}, f32[96,1152]{1,0:T(8,128)S(1)}, f32[32,128]{1,0:T(8,128)S(1)}) custom-call(bf16[1024,1152]{1,0:T(8,128)(2,1)S(1)} %copy-done.30, bf16[1536,1152]{1,0:T(8,128)(2,1)S(1)} %bitcast.111, bf16[16,96,1152]{2,1,0:T(8,128)(2,1)S(1)} %bitcast.117, bf16[16,32,128]{2,1,0:T(8,128)(2,1)S(1)} %fusion.23.a_ref), custom_call_target="tpu_custom_call" | custom-call | flops 30000001024 | bytes 4000000 | tf_op jit(solution)/shard_map/rows_last/pallas_call | solution.py:537
  348.3 0.8 reshape.351.x_ref
  349.1 0.6 reshape.352.u_ref
  349.8 6.6 %collective-permute-start.1 = (bf16[32,1536]{1,0:T(8,128)(2,1)S(1)}, bf16[32,1536]{1,0:T(8,128)(2,1)S(1)}, u32[]{:S(2)}, u32[]{:S(2)}) collective-permute-start(bf16[32,1536]{1,0:T(8,128)(2,1)S(1)} %convert_element_type.137), channel_id=1, source_target_pairs={{0,0},{8,1},{16,2},{24,3},{32,4},{40,5},{48,6},{56,7},{64,8},{72,9... | collective-permute-start | bytes 294920 | tf_op jit(solution)/shard_map/ppermute | solution.py:1665
  356.6 1.0 add_bitcast_fusion
  357.6 1.1 fusion.12
  358.7 0.7 maximum_maximum_fusion.side_ref
  359.5 12.7 %columns_back.1 = (bf16[8,12,1152]{2,1,0:T(8,128)(2,1)}, bf16[8,12,256]{2,1,0:T(8,128)(2,1)}, f32[8,8,128]{2,1,0:T(8,128)}) custom-call(bf16[8,12,1152]{2,1,0:T(8,128)(2,1)} %reshape.351.x_ref, bf16[8,12,256]{2,1,0:T(8,128)(2,1)} %reshape.352.u_ref, f32[8,8,128]{2,1,0:T(8,128)} %maximum_maximum_fusion.side_ref), custom_call_target="tpu_custom_call" | custom-call | flops 30000001024 | bytes 4000000 | tf_op jit(solution)/shard_map/columns_back/pallas_call | solution.py:886
  372.7 0.8 copy-done.13
  373.5 0.8 copy-done.16
  374.2 5.4 %update.1 = (f32[12,6448]{1,0:T(8,128)}, f32[12,6448]{1,0:T(8,128)}, f32[12,6448]{1,0:T(8,128)}, f32[12,2048]{1,0:T(8,128)}, f32[12,2048]{1,0:T(8,128)}, /*index...) custom-call(bf16[8,12,1152]{2,1,0:T(8,128)(2,1)} %get-tuple-element., ...), custom_call_target="tpu_custom_call" | custom-call | tf_op jit(solution)/shard_map/update/pallas_call | solution.py:1443
  379.7 0.5 broadcast.224
  380.2 0.7 reduce.18
  380.9 0.7 copy.105
  381.6 0.7 reduce.19
  382.4 0.7 copy.106
  383.1 0.7 reduce.20
  383.8 0.7 copy.107
  (225 shorter events, 4.5 us)
Async XLA Ops:
  0.7 9.3 %copy-start.4 = (f32[12,2048]{1,0:T(8,128)S(1)}, f32[12,2048]{1,0:T(8,128)}, u32[]{:S(2)}) copy-start(f32[12,2048]{1,0:T(8,128)} %refs_3_.1) | copy-start | bytes 294916
  0.7 9.4 %copy-start.46 = (f32[12,8]{0,1:T(8,128)S(1)}, f32[12,8]{0,1:T(8,128)}, u32[]{:S(2)}) copy-start(f32[12,8]{0,1:T(8,128)} %param.45) | copy-start | bytes 1156
  0.7 9.5 %copy-start.21 = (f32[178]{0:T(256)S(1)}, f32[178]{0:T(256)}, u32[]{:S(2)}) copy-start(f32[178]{0:T(256)} %param.36) | copy-start | bytes 2140
  2.5 23.9 %collective-permute-start = (bf16[32,1536]{1,0:T(8,128)(2,1)S(1)}, bf16[32,1536]{1,0:T(8,128)(2,1)S(1)}, u32[]{:S(2)}, u32[]{:S(2)}) collective-permute-start(bf16[32,1536]{1,0:T(8,128)(2,1)S(1)} %pad_maximum_fusion.1), channel_id=1, source_target_pairs={{0,0},{1,8},{2,16},{3,24},{4,32},{5,40},{6,48},{7,56},{8,64},{9,72... | collective-permute-start | bytes 294920 | tf_op jit(solution)/shard_map/ppermute | solution.py:1558
  11.3 12.6 %copy-start.31 = (f32[1,128,1536]{2,1,0:T(8,128)S(1)}, f32[1,128,1536]{2,1,0:T(8,128)}, u32[]{:S(2)}) copy-start(f32[1,128,1536]{2,1,0:T(8,128)} %param.30) | copy-start | bytes 2359300
  21.9 3.1 copy-start.17
  21.9 3.3 copy-start.37
  21.9 3.3 copy-start.41
  21.9 3.4 copy-start
  23.1 2.3 copy-start.49
  23.1 2.4 copy-start.47
  23.1 2.5 copy-start.48
  24.0 0.9 copy-start.53
  24.0 0.9 copy-start.50
  63.8 0.6 copy-start.43
  104.1 0.7 copy-start.29
  104.9 1.9 copy-start.27
  135.2 1.7 copy-start.26
  136.9 1.2 copy-start.28
  138.4 0.9 copy-start.32
  139.4 2.4 copy-start.35
  141.8 66.1 %copy-start.33 = (f32[128,1536]{1,0:T(8,128)S(1)}, f32[128,1536]{1,0:T(8,128)}, u32[]{:S(2)}) copy-start(f32[128,1536]{1,0:T(8,128)} %copy-done.32) | copy-start | bytes 2359300
  206.9 2.8 copy-start.38
  206.9 2.8 copy-start.40
  252.8 96.3 %copy-start.2 = (f32[96,1280]{1,0:T(8,128)}, f32[96,1280]{1,0:T(8,128)S(1)}, u32[]{:S(2)}) copy-start(f32[96,1280]{1,0:T(8,128)S(1)} %get-tuple-element.129.up_ref) | copy-start | bytes 1474564
  252.8 1.5 copy-start.55
  254.3 2.9 copy-start.42
  258.6 38.3 %copy-start.36 = (bf16[128,1536]{1,0:T(8,128)(2,1)S(1)}, bf16[128,1536]{1,0:T(8,128)(2,1)}, u32[]{:S(2)}) copy-start(bf16[128,1536]{1,0:T(8,128)(2,1)} %copy-done.35) | copy-start | bytes 1179652
  297.1 10.0 %copy-start.45 = (bf16[22784]{0:T(1024)(128)(2,1)S(1)}, bf16[22784]{0:T(1024)(128)(2,1)}, u32[]{:S(2)}) copy-start(bf16[22784]{0:T(1024)(128)(2,1)} %custom-call) | copy-start | bytes 136708
  310.1 2.0 copy-start.6
  312.2 2.0 copy-start.25
  314.2 1.7 copy-start.30
  315.8 40.6 %copy-start.44 = (f32[1536]{0:T(1024)S(1)}, f32[1536]{0:T(1024)}, u32[]{:S(2)}) copy-start(f32[1536]{0:T(1024)} %copy-done.43) | copy-start | bytes 18436
  348.2 8.3 %copy-start.54 = (f32[128]{0:T(128)S(1)}, f32[128]{0:T(128)}, u32[]{:S(2)}) copy-start(f32[128]{0:T(128)} %copy-done.53) | copy-start | bytes 1540
  348.3 9.3 %copy-start.51 = (f32[128]{0:T(128)S(1)}, f32[128]{0:T(128)}, u32[]{:S(2)}) copy-start(f32[128]{0:T(128)} %copy-done.50) | copy-start | bytes 1540
  349.7 6.8 %copy-start.34 = (f32[128,1536]{1,0:T(8,128)S(1)}, f32[128,1536]{1,0:T(8,128)}, u32[]{:S(2)}) copy-start(f32[128,1536]{1,0:T(8,128)} %copy-done.32) | copy-start | bytes 2359300
  349.8 7.8 %copy-start.39 = (f32[128,1536]{1,0:T(8,128)S(1)}, f32[128,1536]{1,0:T(8,128)}, u32[]{:S(2)}) copy-start(f32[128,1536]{1,0:T(8,128)} %get-tuple-element.258) | copy-start | bytes 2359300
  349.8 22.7 %collective-permute-start.1 = (bf16[32,1536]{1,0:T(8,128)(2,1)S(1)}, bf16[32,1536]{1,0:T(8,128)(2,1)S(1)}, u32[]{:S(2)}, u32[]{:S(2)}) collective-permute-start(bf16[32,1536]{1,0:T(8,128)(2,1)S(1)} %convert_element_type.137), channel_id=1, source_target_pairs={{0,0},{8,1},{16,2},{24,3},{32,4},{40,5},{48,6},{56,7},{64,8},{72,9... | collective-permute-start | bytes 294920 | tf_op jit(solution)/shard_map/ppermute | solution.py:1665
  356.6 2.1 copy-start.52
  359.4 13.1 %copy-start.1 = (f32[32,1,1536]{2,1,0:T(1,128)S(1)}, f32[32,1,1536]{2,1,0:T(1,128)}, u32[]{:S(2)}) copy-start(f32[32,1,1536]{2,1,0:T(1,128)} %refs_15_.1) | copy-start | bytes 589828
  359.4 13.1 %copy-start.3 = (f32[24,1536]{1,0:T(8,128)S(1)}, f32[24,1536]{1,0:T(8,128)}, u32[]{:S(2)}) copy-start(f32[24,1536]{1,0:T(8,128)} %refs_6_.1) | copy-start | bytes 442372
  359.4 13.1 %copy-start.5 = (f32[12,2048]{1,0:T(8,128)S(1)}, f32[12,2048]{1,0:T(8,128)}, u32[]{:S(2)}) copy-start(f32[12,2048]{1,0:T(8,128)} %refs_3_.1) | copy-start | bytes 294916
  359.4 13.1 %copy-start.7 = (f32[8,1536]{1,0:T(8,128)S(1)}, f32[8,1536]{1,0:T(8,128)}, u32[]{:S(2)}) copy-start(f32[8,1536]{1,0:T(8,128)} %refs_9_.1) | copy-start | bytes 147460
  359.4 13.1 %copy-start.8 = (f32[32,1,1536]{2,1,0:T(1,128)S(1)}, f32[32,1,1536]{2,1,0:T(1,128)}, u32[]{:S(2)}) copy-start(f32[32,1,1536]{2,1,0:T(1,128)} %refs_16_.1) | copy-start | bytes 589828
  359.4 13.1 %copy-start.9 = (f32[24,1536]{1,0:T(8,128)S(1)}, f32[24,1536]{1,0:T(8,128)}, u32[]{:S(2)}) copy-start(f32[24,1536]{1,0:T(8,128)} %refs_7_.1) | copy-start | bytes 442372
  359.4 13.1 %copy-start.10 = (f32[24,1536]{1,0:T(8,128)S(1)}, f32[24,1536]{1,0:T(8,128)}, u32[]{:S(2)}) copy-start(f32[24,1536]{1,0:T(8,128)} %refs_8_.1) | copy-start | bytes 442372
  359.4 13.1 %copy-start.11 = (f32[12,2048]{1,0:T(8,128)S(1)}, f32[12,2048]{1,0:T(8,128)}, u32[]{:S(2)}) copy-start(f32[12,2048]{1,0:T(8,128)} %refs_4_.1) | copy-start | bytes 294916
  359.4 13.1 %copy-start.12 = (f32[12,2048]{1,0:T(8,128)S(1)}, f32[12,2048]{1,0:T(8,128)}, u32[]{:S(2)}) copy-start(f32[12,2048]{1,0:T(8,128)} %refs_5_.1) | copy-start | bytes 294916
  359.4 13.1 %copy-start.14 = (f32[8,1536]{1,0:T(8,128)S(1)}, f32[8,1536]{1,0:T(8,128)}, u32[]{:S(2)}) copy-start(f32[8,1536]{1,0:T(8,128)} %refs_10_.1) | copy-start | bytes 147460
  359.5 13.1 %copy-start.15 = (f32[8,1536]{1,0:T(8,128)S(1)}, f32[8,1536]{1,0:T(8,128)}, u32[]{:S(2)}) copy-start(f32[8,1536]{1,0:T(8,128)} %refs_11_.1) | copy-start | bytes 147460
  359.5 13.1 %copy-start.18 = (f32[3,48]{1,0:T(4,128)S(1)}, f32[3,48]{1,0:T(4,128)}, u32[]{:S(2)}) copy-start(f32[3,48]{1,0:T(4,128)} %refs_24_.1) | copy-start | bytes 1732
  359.5 13.1 %copy-start.19 = (f32[3,48]{1,0:T(4,128)S(1)}, f32[3,48]{1,0:T(4,128)}, u32[]{:S(2)}) copy-start(f32[3,48]{1,0:T(4,128)} %refs_25_.1) | copy-start | bytes 1732
  359.5 13.1 %copy-start.20 = (f32[3,48]{1,0:T(4,128)S(1)}, f32[3,48]{1,0:T(4,128)}, u32[]{:S(2)}) copy-start(f32[3,48]{1,0:T(4,128)} %refs_26_.1) | copy-start | bytes 1732
  359.5 13.1 %copy-start.22 = (f32[178]{0:T(256)S(1)}, f32[178]{0:T(256)}, u32[]{:S(2)}) copy-start(f32[178]{0:T(256)} %param.36) | copy-start | bytes 2140
  359.5 13.1 %copy-start.23 = (f32[178]{0:T(256)S(1)}, f32[178]{0:T(256)}, u32[]{:S(2)}) copy-start(f32[178]{0:T(256)} %param.37) | copy-start | bytes 2140
  359.5 13.1 %copy-start.24 = (f32[178]{0:T(256)S(1)}, f32[178]{0:T(256)}, u32[]{:S(2)}) copy-start(f32[178]{0:T(256)} %param.38) | copy-start | bytes 2140
  372.6 0.8 copy-start.13
  373.5 0.8 copy-start.16

commit v2 on v1

--- a/solution.py
+++ b/solution.py
@@ -30,6 +30,7 @@
 CONV_HERE = INNER_HERE + 2 * STATE
 PROJ_HERE = INNER_HERE + CONV_HERE + 128
 SMALL_COLS = 15
+ROUTER_AT = 100
 
 
 NORM_EPSILON = 1e-05
@@ -327,7 +328,20 @@
     ]
 
 
-def ring_scatter(block, slot, device, send, result, buffers):
+def staged(source, target, sem):
+    copies = [pltpu.make_async_copy(source, target, sem)]
+    copies[0].start()
+
+    def ready():
+        if copies:
+            copies.pop().wait()
+        return target
+
+    return ready
+
+
+def ring_scatter(block, slot, device, send, result, buffers, raw=None, near_first=False):
+    raw = raw or block
     in_low, in_high, sum_up, sum_down, land_low, land_high, part_out, part_in = buffers
     rows = part_out.shape[0]
     half = rows // 2
@@ -335,16 +349,22 @@
     everything = pl.ds(0, rows)
     landing = {}
 
-    def begin(turn, other):
-        far = block(2, other)
-        copies = [
+    def begin_far(turn, other):
+        far = raw(2, other)
+        return [
             send(far(first), in_low.at[turn], device(1, False)),
             send(far(second), in_high.at[turn], device(-1, False)),
         ]
+
+    def begin_near(turn, other):
         landing[turn] = [
-            send(block(1, other)(second), land_low.at[turn, second], device(1, False)),
-            send(block(-1, other)(first), land_high.at[turn, first], device(-1, False)),
+            send(raw(1, other)(second), land_low.at[turn, second], device(1, False)),
+            send(raw(-1, other)(first), land_high.at[turn, first], device(-1, False)),
         ]
+
+    def begin(turn, other):
+        copies = begin_far(turn, other)
+        begin_near(turn, other)
         return copies
 
     def middle(turn, other, copies):
@@ -364,7 +384,12 @@
             + land_high[turn].astype(FULL)
         )
 
-    copies = begin(0, True)
+    if near_first:
+        begin_near(0, True)
+        yield True
+        copies = begin_far(0, True)
+    else:
+        copies = begin(0, True)
     yield True
     middle(0, True, copies)
     yield True
@@ -397,15 +422,25 @@
     return block
 
 
+def block_ready(ready, slot):
+    def block(up, other):
+        return lambda cut: ready().at[slot(up, other), cut]
+
+    return block
+
+
 def mixed_kernel(x_ref, side_ref, u_ref, d_ref, out_ref, side_out, u_out, d_out, *rest):
     buffers, (send_sem, recv_sem, s_send, s_recv, s_local) = rest[:8], rest[8:13]
-    u_send, u_recv, d_send, d_recv, keeps = rest[13:]
+    u_send, u_recv, d_send, d_recv, keeps, x_vmem, x_sem = rest[13:]
     me, slot, device = seq_axis()
     core, f_slot, f_device, twin = fsdp_axis()
+    x_ready = staged(x_ref, x_vmem, x_sem)
     meet(all_peers() + ring_peers(f_device) + [twin])
     started, u_started, d_started, crossing = [], [], [], []
     send = sender(send_sem, recv_sem, started)
-    program = ring_scatter(block_of(x_ref, slot), slot, device, send, out_ref, buffers)
+    program = ring_scatter(
+        block_ready(x_ready, slot), slot, device, send, out_ref, buffers, block_of(x_ref, slot)
+    )
     next(program)
     sides = side_start(side_ref, side_out, True, s_send, s_recv, s_local)
     mine = f_slot(0, False) * 2 + core
@@ -439,14 +474,14 @@
             jax.ShapeDtypeStruct((SHARDS, *up_piece.shape), LOW),
             jax.ShapeDtypeStruct((SHARDS, *down_piece.shape), LOW),
         ),
-        in_specs=[vmem_spec(), vmem_spec(), any_spec(), any_spec()],
+        in_specs=[any_spec(), vmem_spec(), any_spec(), any_spec()],
         out_specs=(vmem_spec(), vmem_spec(), any_spec(), any_spec()),
         scratch_shapes=scatter_buffers(rows, width)
         + [dma_sems(13), dma_sems(13), dma_sems(GROUPS), dma_sems(GROUPS), pltpu.SemaphoreType.DMA]
         + [dma_sems(19)] * 4
-        + [dma_sems(2)],
+        + [dma_sems(2), pltpu.VMEM(parts.shape, LOW), pltpu.SemaphoreType.DMA],
         compiler_params=pltpu.CompilerParams(
-            collective_id=4, has_side_effects=True, vmem_limit_bytes=40 << 20
+            collective_id=4, has_side_effects=True, vmem_limit_bytes=52 << 20
         ),
         cost_estimate=BUSY,
         name="mixer_out",
@@ -470,17 +505,17 @@
     core, slot, device, twin = fsdp_axis()
     order = [(2, True), (1, True), (-1, True), (2, False), (1, False), (-1, False), (0, True), (0, False)]
     programs, senders = [], []
-    for pick, target, scratch in arrays:
+    for pick, value, target, scratch in arrays:
         buffers, (core_in, send_sem, recv_sem, c_send, c_recv) = scratch[:8], scratch[8:]
         crossing, copies, arriving = [], [], {}
         started.extend([crossing, copies])
         senders.append((pick, core_in, sender(c_send, c_recv, crossing), arriving))
 
-        def block(up, other, pick=pick, core_in=core_in, arriving=arriving):
+        def block(up, other, value=value, core_in=core_in, arriving=arriving):
             at = slot(up, other)
             if (up, other) in arriving:
                 arriving.pop((up, other)).wait_recv()
-                core_in[at] = (core_in[at].astype(FULL) + pick(at * 2 + core)[...].astype(FULL)).astype(LOW)
+                core_in[at] = (core_in[at].astype(FULL) + value(at * 2 + core)[...].astype(FULL)).astype(LOW)
             return lambda cut: core_in.at[at, cut]
 
         programs.append(ring_scatter(block, slot, device, sender(send_sem, recv_sem, copies), target, buffers))
@@ -495,14 +530,21 @@
     return lambda at: ref.at[at]
 
 
+def ready_blocks(ready):
+    return lambda at: ready().at[at]
+
+
 def shard_peers():
     core, slot, device, twin = fsdp_axis()
     return ring_peers(device) + [twin]
 
 
-def last_kernel(g_ref, p_ref, w_ref, a_ref, x_out, w_out, a_out, x_ref, *rest):
+def last_kernel(g_any, p_any, w_any, a_ref, x_out, w_out, a_out, x_ref, w_ref, g_ref, p_ref, stages, *rest):
     x_buffers, (x_send, x_recv) = rest[:8], rest[8:10]
     me, slot, device = seq_axis()
+    g_ready = staged(g_any, g_ref, stages.at[0])
+    p_ready = staged(p_any, p_ref, stages.at[1])
+    w_ready = staged(w_any, w_ref, stages.at[2])
     done = set()
 
     def part_of(up, other):
@@ -510,6 +552,7 @@
         if (up, other) not in done:
             done.add((up, other))
             here = pl.ds(pl.multiple_of(at * PIECE, PIECE), PIECE)
+            g_ready(), p_ready()
             for part in range(D // 512):
                 cols = slice(part * 512, (part + 1) * 512)
                 x_ref[at, :, cols] = dot_rhs_t(g_ref[here, :], p_ref[cols, :]).astype(LOW)
@@ -520,8 +563,8 @@
     program = ring_scatter(part_of, slot, device, sender(x_send, x_recv, x_started), x_out, x_buffers)
     main, small = shard_scatters(
         [
-            (blocks_of(w_ref), w_out, rest[10 : 10 + SHARD_SCRATCH]),
-            (blocks_of(a_ref), a_out, rest[10 + SHARD_SCRATCH :]),
+            (blocks_of(w_any), ready_blocks(w_ready), w_out, rest[10 : 10 + SHARD_SCRATCH]),
+            (blocks_of(a_ref), blocks_of(a_ref), a_out, rest[10 + SHARD_SCRATCH :]),
         ],
         started,
     )
@@ -541,15 +584,21 @@
             jax.ShapeDtypeStruct(grads.shape[1:], FULL),
             jax.ShapeDtypeStruct(small.shape[1:], FULL),
         ),
-        in_specs=[vmem_spec()] * 4,
+        in_specs=[any_spec(), any_spec(), any_spec(), vmem_spec()],
         out_specs=(vmem_spec(),) * 3,
-        scratch_shapes=[pltpu.VMEM((GROUPS, rows, width), LOW)]
+        scratch_shapes=[
+            pltpu.VMEM((GROUPS, rows, width), LOW),
+            pltpu.VMEM(grads.shape, LOW),
+            pltpu.VMEM(proj_grad.shape, LOW),
+            pltpu.VMEM(weights.shape, LOW),
+            dma_sems(3),
+        ]
         + scatter_buffers(rows, width)
         + [dma_sems(13), dma_sems(13)]
         + shard_scratch(grads)
         + shard_scratch(small),
         compiler_params=pltpu.CompilerParams(
-            collective_id=8, has_side_effects=True, vmem_limit_bytes=40 << 20
+            collective_id=8, has_side_effects=True, vmem_limit_bytes=52 << 20
         ),
         cost_estimate=BUSY,
         name="rows_last",
@@ -564,7 +613,7 @@
     send = sender(x_send, x_recv, x_started)
     program = ring_gather(x_ref, lambda at, cut: x_out.at[(at, *cut)], slot, device, send, nothing)
     next(program)
-    [shard] = shard_scatters([(blocks_of(u_ref), u_out, rest[6:])], started)
+    [shard] = shard_scatters([(blocks_of(u_ref), blocks_of(u_ref), u_out, rest[6:])], started)
     sides = side_start(side_ref, side_out, False, s_send, s_recv, s_local)
     keep = pltpu.make_async_copy(x_ref, x_out.at[me], x_local)
     keep.start()
@@ -598,7 +647,7 @@
         ]
         + shard_scratch(up_grads),
         compiler_params=pltpu.CompilerParams(
-            collective_id=7, has_side_effects=True, vmem_limit_bytes=48 << 20
+            collective_id=7, has_side_effects=True, vmem_limit_bytes=52 << 20
         ),
         cost_estimate=BUSY,
         name="rows_mixer",
@@ -736,6 +785,7 @@
             for index, at in enumerate(slots):
                 parts_ref[at, :, cols] = total[index * PIECE : (index + 1) * PIECE]
 
+    summed = []
     process((0, False))
     next(gather)
     next(gather)
@@ -747,13 +797,19 @@
     next(gather)
     next(gather)
     process((-1, True), (1, True))
+    scatter = ring_scatter(
+        block_of(parts_ref, slot),
+        slot,
+        device,
+        sender(r_send, r_recv, summed),
+        back_out,
+        buffers,
+        near_first=True,
+    )
+    next(scatter)
     take_turns(gather)
     process((2, True))
 
-    summed = []
-    scatter = ring_scatter(
-        block_of(parts_ref, slot), slot, device, sender(r_send, r_recv, summed), back_out, buffers
-    )
     next(scatter)
     backs = side_start(side_send, side_back, True, b_send, b_recv, b_local)
 
@@ -842,7 +898,7 @@
         + [dma_sems(GROUPS), dma_sems(GROUPS), pltpu.SemaphoreType.DMA]
         + [dma_sems(5)],
         compiler_params=pltpu.CompilerParams(
-            collective_id=5, has_side_effects=True, vmem_limit_bytes=56 << 20
+            collective_id=5, has_side_effects=True, vmem_limit_bytes=52 << 20
         ),
         cost_estimate=BUSY,
         name="experts",
@@ -1174,9 +1230,9 @@
     bias_ref,
     head_ref,
     skip_ref,
-    block_ref,
-    down_ref,
-    owned_ref,
+    block_any,
+    down_any,
+    owned_any,
     out_ref,
     conv_ref,
     skip_grad_ref,
@@ -1195,20 +1251,29 @@
     flow_rows,
     row_sums,
     mixed_back,
+    block_ref,
+    down_ref,
+    owned_ref,
+    stages,
     *rest,
 ):
     me, slot, device = seq_axis()
+    block_ready_ref = staged(block_any, block_ref, stages.at[0])
+    downs_ready = staged(down_any, down_ref, stages.at[1])
+    owned_ready = staged(owned_any, owned_ref, stages.at[2])
     meet(ring_peers(device) + shard_peers())
     started = [[]]
     shards = shard_scatters(
         [
-            (blocks_of(down_ref), down_out, rest[10 : 10 + SHARD_SCRATCH]),
-            (blocks_of(owned_ref), owned_out, rest[10 + SHARD_SCRATCH :]),
+            (blocks_of(down_any), ready_blocks(downs_ready), down_out, rest[10 : 10 + SHARD_SCRATCH]),
+            (blocks_of(owned_any), ready_blocks(owned_ready), owned_out, rest[10 + SHARD_SCRATCH :]),
         ],
         started,
     )
     send = sender(rest[8], rest[9], started[0])
-    program = ring_scatter(block_of(block_ref, slot), slot, device, send, block_out, rest[:8])
+    program = ring_scatter(
+        block_ready(block_ready_ref, slot), slot, device, send, block_out, rest[:8], block_of(block_any, slot)
+    )
     next(program)
     scores_and_columns(
         act_ref[:, INNER_HERE : INNER_HERE + STATE],
@@ -1346,7 +1411,7 @@
             jax.ShapeDtypeStruct((32, D), FULL),
             jax.ShapeDtypeStruct((32, D), FULL),
         ),
-        in_specs=[vmem_spec()] * 13,
+        in_specs=[vmem_spec()] * 10 + [any_spec()] * 3,
         out_specs=(vmem_spec(),) * 7,
         scratch_shapes=[
             pltpu.VMEM((SEQ_LEN + 8, 128), FULL),
@@ -1360,6 +1425,10 @@
             pltpu.VMEM((8, SEQ_LEN), FULL),
             pltpu.VMEM((TILE, 128), FULL),
             pltpu.VMEM((128, SEQ_LEN), FULL),
+            pltpu.VMEM(blocks.shape, LOW),
+            pltpu.VMEM(downs.shape, LOW),
+            pltpu.VMEM(owned.shape, LOW),
+            dma_sems(3),
         ]
         + scatter_buffers(PIECE, D)
         + [dma_sems(13), dma_sems(13)]
@@ -1432,9 +1501,9 @@
     aux = aux_ref[0]
     for group in range(1, GROUPS):
         aux = aux + aux_ref[group]
-    small = jnp.concatenate([aux[0:1], aux[1:2]], axis=1)[:, :178]
+    small = jnp.concatenate([aux[0:1, :89], aux[1:2, :89]], axis=1)
     step(6, small, RATE_SMALL, 0.0, (slice(0, 1),))
-    step(7, aux[2:3, :96], RATE_MATRIX, WEIGHT_DECAY, (slice(0, 1),))
+    step(7, aux[:, ROUTER_AT : ROUTER_AT + 12], RATE_MATRIX, WEIGHT_DECAY, (slice(0, 8),))
     step(8, aux[3:6, :HEADS], RATE_HEAD, 0.0, (slice(0, 3),))
 
 
@@ -1445,7 +1514,7 @@
         out_shape=tuple(jax.ShapeDtypeStruct(values.shape, FULL) for values in olds),
         in_specs=[vmem_spec()] * (7 + len(olds)),
         out_specs=(vmem_spec(),) * len(olds),
-        compiler_params=pltpu.CompilerParams(vmem_limit_bytes=52 << 20),
+        compiler_params=pltpu.CompilerParams(vmem_limit_bytes=56 << 20),
         name="update",
     )(*sums, *olds)
     return [news[3 * index : 3 * index + 3] for index in range(len(triples))]
@@ -1623,7 +1692,7 @@
 
     logits_grad = route_pull(combine_sides[:, 0].T)[0].astype(LOW)
     normed_two_grad = back_sum + dot_rhs_t(logits_grad, router_full)
-    router_grad = dot_lhs_t(normed_two, logits_grad)
+    router_grad = dot_lhs_t(logits_grad, normed_two)
     middle_from_norm, gain_second_grad = norm_back(middle, second_inverse, gain_second, normed_two_grad)
     middle_grad = out_grad + middle_from_norm
     mixer_grad = middle_grad.astype(LOW)
@@ -1679,8 +1748,9 @@
     small_grad = jnp.concatenate(
         [gain_first_grad, gain_second_grad, gain_wide, bias_wide, kernel_wide.reshape(-1)]
     )
-    small_grad = jnp.pad(small_grad.reshape(SHARDS * GROUPS, 178), ((0, 0), (0, 78))).reshape(SHARDS, 16, 128)
-    router_rows = jnp.pad(router_grad.reshape(SHARDS, GROUPS, 96), ((0, 0), (0, 0), (0, 32)))
+    small_grad = jnp.pad(small_grad.reshape(SHARDS * GROUPS, 2, 89), ((0, 0), (0, 6), (0, 39)))
+    router_rows = router_grad.reshape(EXPERTS, SHARDS * GROUPS, 12).transpose(1, 0, 2)
+    small_grad = (small_grad + jnp.pad(router_rows, ((0, 0), (0, 0), (ROUTER_AT, 116 - ROUTER_AT)))).astype(LOW)
     head_grad = jnp.stack([bias_grad, log_decay_grad, skip_grad])
     head_rows = lax.dynamic_update_slice_in_dim(
         jnp.zeros((3, 128), FULL), head_grad, group_index * HEADS_HERE, 1
@@ -1688,9 +1758,8 @@
     head_rows = jnp.pad(jnp.concatenate(hi_lo(head_rows)), ((0, 2), (0, 0)))
     aux_grad = jnp.concatenate(
         [
-            small_grad.astype(LOW),
-            router_rows.astype(LOW),
-            jnp.broadcast_to(head_rows, (SHARDS, 8, 128)),
+            small_grad.reshape(SHARDS, 64, 128),
+            jnp.broadcast_to(jnp.pad(head_rows, ((0, 24), (0, 0))), (SHARDS, 32, 128)),
         ],
         axis=1,
     )
@@ -1701,22 +1770,15 @@
     hidden_grad = middle_grad + input_from_norm
 
     shared_back = up_sum[:, 2 * FF_EXP :].astype(LOW).reshape(GROUPS, 12, 2 * SH_HERE)
-    aux_side = jnp.concatenate(
-        [
-            aux_sum[:16].reshape(GROUPS, 2, 128),
-            aux_sum[16:24].reshape(GROUPS, 1, 128),
-            jnp.broadcast_to(aux_sum[24:27] + aux_sum[27:30], (GROUPS, 3, 128)),
-            jnp.zeros((GROUPS, 2, 128), FULL),
-        ],
-        axis=1,
-    )
+    head_side = jnp.pad(aux_sum[64:67] + aux_sum[67:70], ((3, 2), (0, 0)))
+    aux_side = aux_sum[:64].reshape(GROUPS, 8, 128) + head_side
     dense, shared_back, aux_back = columns_back(
         column_sum.astype(LOW).reshape(GROUPS, 12, PROJ_HERE), shared_back, aux_side
     )
     owner = lax.axis_index("fsdp") * GROUPS + group_index
     own_gain = lax.dynamic_slice_in_dim(gain_first, owner * 12, 12)[:, None]
     small_rows = [values[None] for values in (small_params, small_first, small_second)]
-    router_rows = [values.reshape(1, 96) for values in (router_weight, router_first, router_second)]
+    router_rows = [values.T for values in (router_weight, router_first, router_second)]
     news = update(
         (dense, shared_back, aux_back, owned_sum, up_sum, down_sum, own_gain),
         (
@@ -1733,7 +1795,7 @@
     )
     proj_new, shared_up_new, out_new, shared_down_new, up_new, down_new, small_new, router_new, head_new = news
     small_new = [values[0] for values in small_new]
-    router_new = [values.reshape(12, EXPERTS) for values in router_new]
+    router_new = [values.T for values in router_new]
     return (
         block_out[None],
         hidden_grad[None],

time: 388 us -> 368 us (0.948)
  local copies, waits for them, and re-layouts: 29.6 us -> 11.9 us
    unnamed x128 -> x58, local copies, waits for them, and re-layouts: 17.4 us -> 0.62 us
where the time goes in v2:
time: 368 us; the launch traced here: 365 us
  Pallas kernels  306 us (83%)
  matrix products  19.6 us (5%)
  starting transfers between devices  13.1 us (4%)
  other arithmetic  13 us (4%)
  local copies, waits for them, and re-layouts  11.9 us (3%)
    pallas_call x1, Pallas kernels, experts(): pl.pallas_call(experts_kernel, out_shape=(jax.ShapeDtypeStruct((PIECE, D)...  64.1 us
    pallas_call x1, Pallas kernels, middle_gather(): pl.pallas_call(middle_kernel, out_shape=(jax.ShapeDtypeStruct((GROUPS, ro...  40 us
    pallas_call x1, Pallas kernels, mixer_forward(): pl.pallas_call(mixer_forward_kernel, out_shape=(jax.ShapeDtypeStruct((SEQ...  39.6 us
    pallas_call x1, Pallas kernels, mixer_backward(): pl.pallas_call(mixer_backward_kernel, out_shape=(jax.ShapeDtypeStruct((SE...  36.5 us
    pallas_call x1, Pallas kernels, start_gather(): pl.pallas_call(start_kernel, out_shape=(jax.ShapeDtypeStruct((GROUPS, row...  35 us
    pallas_call x1, Pallas kernels, last_scatter(): pl.pallas_call(last_kernel, out_shape=(jax.ShapeDtypeStruct((rows, width)...  31.6 us
    pallas_call x1, Pallas kernels, mixed_scatter(): pl.pallas_call(mixed_kernel, out_shape=(jax.ShapeDtypeStruct((rows, width...  29 us
    dot_general x3, matrix products, dot_lhs_t(): lax.dot_general(left, right, (((0,), (0,)), ((), ())), preferred_element_...  13.6 us
  transfers between devices with their start and end apart: 2, of which 0 were waited for; matrix products, arithmetic and copies ran while one was open for 3% of the time, Pallas kernels for 6%

profile of v2, /device:TPU:1, one launch (start us, length us, event | category | flops | bytes accessed | tf_op | source)
XLA Modules:
  0.0 365.0 jit_solution(7102343351856981989)
XLA Ops:
  0.7 1.0 convert_element_type.119
  1.7 0.8 convert_element_type.120
  2.5 6.2 %collective-permute-start = (bf16[32,1536]{1,0:T(8,128)(2,1)S(1)}, bf16[32,1536]{1,0:T(8,128)(2,1)S(1)}, u32[]{:S(2)}, u32[]{:S(2)}) collective-permute-start(bf16[32,1536]{1,0:T(8,128)(2,1)S(1)} %pad_maximum_fusion.2), channel_id=1, source_target_pairs={{0,0},{1,8},{2,16},{3,24},{4,32},{5,40},{6,48},{7,56},{8,64},{9,72... | collective-permute-start | bytes 294920 | tf_op jit(solution)/shard_map/ppermute | solution.py:1627
  8.7 1.0 convert_element_type.115
  10.0 0.1 reshape.308
  10.1 0.1 copy.84
  10.2 0.1 reshape.309
  10.4 0.1 pad_maximum_fusion.4
  10.5 0.8 concatenate.37
  11.3 10.5 %columns_out.1 = bf16[8,12,1408]{2,1,0:T(8,128)(2,1)} custom-call(bf16[8,12,1408]{2,1,0:T(8,128)(2,1)} %bitcast.133), custom_call_target="tpu_custom_call" | custom-call | flops 30000001024 | bytes 4000000 | tf_op jit(solution)/shard_map/columns_out/pallas_call | solution.py:918
  21.9 1.1 reshape.311
  23.1 0.7 slice.173.rest_0_
  23.8 0.1 fusion.7
  24.0 0.9 fusion.8.x_ref
  24.8 0.1 constant_dynamic-slice_fusion
  25.0 0.1 broadcast_in_dim_reshape.3.skip_ref
  25.3 0.6 slice.174.rest_1_
  25.9 35.0 %rows_first.1 = (bf16[8,128,1536]{2,1,0:T(8,128)(2,1)}, bf16[16,96,1152]{2,1,0:T(8,128)(2,1)}, bf16[16,24,1536]{2,1,0:T(8,128)(2,1)}) custom-call(bf16[128,1536]{1,0:T(8,128)(2,1)} %fusion.8.x_ref, bf16[96,1152]{1,0:T(8,128)(2,1)} %slice.173.rest_0_, bf16[24,1536]{1,0:T(8,128)(2,1)} %slice.174.rest_1_), custom_call_target="tpu_custom_call" | custom-call | flops 30000001024 | bytes 4000000 | tf_op jit(solution)/shard_map/rows_first/pallas_call | solution.py:315
  61.0 1.2 slice.175
  62.1 0.2 reshape.314
  62.4 0.2 reshape.334
  62.7 0.1 dynamic_slice.16
  62.8 0.1 dynamic_slice.18
  62.9 0.3 copy-done.12
  63.3 39.6 %mixer_forward.1 = (bf16[1024,1152]{1,0:T(8,128)(2,1)}, bf16[1024,640]{1,0:T(8,128)(2,1)}, f32[1024,384]{1,0:T(8,128)}, bf16[1024,384]{1,0:T(8,128)(2,1)S(1)}, b...) custom-call(bf16[1024,1536]{1,0:T(8,128)(2,1)} %bitcast.164, ...), custom_call_target="tpu_custom_call" | custom-call | flops 30000001024 | bytes 4000000 | tf_op jit(solution)/shard_map/mixer_forward/pallas_call | solution.py:1178
  103.0 29.0 %mixer_out.1 = (f32[128,1536]{1,0:T(8,128)S(1)}, f32[8,8,128]{2,1,0:T(8,128)S(1)}, bf16[16,96,1024]{2,1,0:T(8,128)(2,1)}, bf16[16,32,1536]{2,1,0:T(8,128)(2,1)}) custom-call(bf16[8,128,1536]{2,1,0:T(8,128)(2,1)} %bitcast.167, f32[8,8,128]{2,1,0:T(8,128)S(1)} %get-tuple-element.100.side_ref, bf16[96,1024]{1,0:T(8,128)(2,1)S(1)} %bitcast.118, ...), custom_call_target="tpu_custom_call" | custom-call | flops 30000001024 | bytes 4000000 | tf_op jit(solution)/shard_map/mixer_out/pallas_call | solution.py:469
  132.1 0.3 multiply_reduce_fusion.4
  132.3 0.1 multiply_convert_fusion.x_ref
  132.5 1.5 fusion.18
  134.1 64.1 %experts.1 = (f32[128,1536]{1,0:T(8,128)S(1)}, f32[8,8,128]{2,1,0:T(8,128)S(1)}, bf16[8,128,1536]{2,1,0:T(8,128)(2,1)}, bf16[1536,1280]{1,0:T(8,128)(2,1)}, bf16...) custom-call(bf16[128,1536]{1,0:T(8,128)(2,1)S(1)} %multiply_convert_fusion.x_ref, f32[8,128]{1,0:T(8,128)S(1)} %bitcast.120, ...), custom_call_target="tpu_custom_call" | custom-call | flops 30000001024 | bytes 4000000 | tf_op jit(solution)/shard_map/experts/pallas_call | solution.py:865
  198.4 1.6 multiply_reduce_fusion.1
  200.0 1.2 multiply_reduce_fusion.2
  201.3 40.0 %rows_mixer.1 = (bf16[8,128,1536]{2,1,0:T(8,128)(2,1)}, f32[8,8,128]{2,1,0:T(8,128)S(1)}, f32[96,1280]{1,0:T(8,128)S(1)}) custom-call(bf16[128,1536]{1,0:T(8,128)(2,1)S(1)} %get-tuple-element.170.x_ref, f32[8,128]{1,0:T(8,128)S(1)} %pad.36.side_ref, bf16[16,96,1280]{2,1,0:T(8,128)(2,1)} %bitcast.162), custom_call_target="tpu_custom_call" | custom-call | flops 30000001024 | bytes 4000000 | tf_op jit(solution)/shard_map/rows_mixer/pallas_call | solution.py:631
  241.3 3.6 convolution_convert_fusion
  244.9 2.9 fusion.3
  247.8 1.3 pad_maximum_fusion.owned_any
  249.1 36.5 %mixer_backward.1 = (bf16[1024,1152]{1,0:T(8,128)(2,1)}, f32[8,640]{1,0:T(8,128)S(1)}, f32[8,384]{1,0:T(8,128)S(1)}, f32[2,8,128]{2,1,0:T(8,128)S(1)}, f32[128,1...) custom-call(bf16[1024,384]{1,0:T(8,128)(2,1)} %get-tuple-element.177.grad_ref, ...), custom_call_target="tpu_custom_call" | custom-call | flops 30000001024 | bytes 4000000 | tf_op jit(solution)/shard_map/mixer_backward/pallas_call | solution.py:1403
  285.7 0.9 fusion.45
  286.7 9.8 %multiply_reduce_fusion = (f32[1536]{0:T(1024)S(1)}, bf16[1536,1152]{1,0:T(8,128)(2,1)}) fusion(bf16[16,96,1152]{2,1,0:T(8,128)(2,1)} %get-tuple-element.97, bf16[1024,1536]{1,0:T(8,128)(2,1)} %bitcast.165, bf16[1024,1152]{1,0:T(8,128)(2,1)} %get-tuple-element.123.g_any), kind=kOutput, calls=%fused_computation | convolution fusion | flops 3630955008 | bytes 12589056 | tf_op jit(solution)/shard_map/dot_general | solution.py:1549
  296.5 0.2 dynamic_update_slice.13
  296.7 0.3 dynamic_update_slice.12
  297.0 0.3 reshape.329
  297.3 0.1 copy.92
  297.4 1.2 copy.93
  298.6 0.1 dot_general.28
  298.7 0.2 convolution_bitcast_fusion
  299.0 0.2 copy.95
  299.3 0.1 reshape_squeeze.2
  299.3 0.1 reduce_sum.170
  299.5 0.1 slice_reduce_fusion.1
  299.6 0.4 dynamic_update_slice.15
  300.2 31.6 %rows_last.1 = (f32[128,1536]{1,0:T(8,128)S(1)}, f32[96,1152]{1,0:T(8,128)S(1)}, f32[96,128]{1,0:T(8,128)S(1)}) custom-call(bf16[1024,1152]{1,0:T(8,128)(2,1)} %get-tuple-element.123.g_any, bf16[1536,1152]{1,0:T(8,128)(2,1)} %bitcast.132, bf16[16,96,1152]{2,1,0:T(8,128)(2,1)} %bitcast.163, bf16[16,96,128]{2,1,0:T(8,128)(2,1)S(1)} %pad_maximum_fusion.1.a_ref), custom_call_target="tpu_custom_call" | custom-call | flops 30000001024 | bytes 4000000 | tf_op jit(solution)/shard_map/rows_last/pallas_call | solution.py:580
  331.8 0.6 bitcast_add_fusion.2.side_ref
  332.5 0.8 reshape.331.x_ref
  333.3 0.6 reshape.332.u_ref
  333.9 6.8 %collective-permute-start.1 = (bf16[32,1536]{1,0:T(8,128)(2,1)S(1)}, bf16[32,1536]{1,0:T(8,128)(2,1)S(1)}, u32[]{:S(2)}, u32[]{:S(2)}) collective-permute-start(bf16[32,1536]{1,0:T(8,128)(2,1)S(1)} %convert_element_type.143), channel_id=1, source_target_pairs={{0,0},{8,1},{16,2},{24,3},{32,4},{40,5},{48,6},{56,7},{64,8},{72,9... | collective-permute-start | bytes 294920 | tf_op jit(solution)/shard_map/ppermute | solution.py:1734
  340.8 1.3 fusion.9
  342.2 1.0 add_bitcast_fusion
  343.1 1.1 fusion.12
  344.2 12.9 %columns_back.1 = (bf16[8,12,1152]{2,1,0:T(8,128)(2,1)}, bf16[8,12,256]{2,1,0:T(8,128)(2,1)}, f32[8,8,128]{2,1,0:T(8,128)}) custom-call(bf16[8,12,1152]{2,1,0:T(8,128)(2,1)} %reshape.331.x_ref, bf16[8,12,256]{2,1,0:T(8,128)(2,1)} %reshape.332.u_ref, f32[8,8,128]{2,1,0:T(8,128)} %bitcast_add_fusion.2.side_ref), custom_call_target="tpu_custom_call" | custom-call | flops 30000001024 | bytes 4000000 | tf_op jit(solution)/shard_map/columns_back/pallas_call | solution.py:942
  357.1 0.1 dynamic-slice_bitcast_fusion
  357.2 0.7 copy.96.gain_ref
  357.9 0.7 convert_element_type.144.owned_ref
  358.6 6.1 %update.1 = (f32[12,6448]{1,0:T(8,128)}, f32[12,6448]{1,0:T(8,128)}, f32[12,6448]{1,0:T(8,128)}, f32[12,2048]{1,0:T(8,128)}, f32[12,2048]{1,0:T(8,128)}, /*index...) custom-call(bf16[8,12,1152]{2,1,0:T(8,128)(2,1)} %get-tuple-element., ...), custom_call_target="tpu_custom_call" | custom-call | tf_op jit(solution)/shard_map/update/pallas_call | solution.py:1512
  (144 shorter events, 1.3 us)
Async XLA Ops:
  0.7 9.3 %copy-start.11 = (f32[12,2048]{1,0:T(8,128)S(1)}, f32[12,2048]{1,0:T(8,128)}, u32[]{:S(2)}) copy-start(f32[12,2048]{1,0:T(8,128)} %refs_3_.1) | copy-start | bytes 294916
  0.7 9.4 %copy-start.15 = (f32[12,8]{0,1:T(8,128)S(1)}, f32[12,8]{0,1:T(8,128)}, u32[]{:S(2)}) copy-start(f32[12,8]{0,1:T(8,128)} %param.45) | copy-start | bytes 1156
  0.7 9.5 %copy-start.20 = (f32[178]{0:T(256)S(1)}, f32[178]{0:T(256)}, u32[]{:S(2)}) copy-start(f32[178]{0:T(256)} %param.36) | copy-start | bytes 2140
  2.5 22.8 %collective-permute-start = (bf16[32,1536]{1,0:T(8,128)(2,1)S(1)}, bf16[32,1536]{1,0:T(8,128)(2,1)S(1)}, u32[]{:S(2)}, u32[]{:S(2)}) collective-permute-start(bf16[32,1536]{1,0:T(8,128)(2,1)S(1)} %pad_maximum_fusion.2), channel_id=1, source_target_pairs={{0,0},{1,8},{2,16},{3,24},{4,32},{5,40},{6,48},{7,56},{8,64},{9,72... | collective-permute-start | bytes 294920 | tf_op jit(solution)/shard_map/ppermute | solution.py:1627
  11.3 12.5 %copy-start.2 = (f32[1,128,1536]{2,1,0:T(8,128)S(1)}, f32[1,128,1536]{2,1,0:T(8,128)}, u32[]{:S(2)}) copy-start(f32[1,128,1536]{2,1,0:T(8,128)} %param.30) | copy-start | bytes 2359300
  21.9 3.0 copy-start.16
  21.9 3.2 copy-start.6
  21.9 3.2 copy-start.9
  21.9 3.3 copy-start.10
  23.1 2.2 copy-start.17
  23.9 0.9 copy-start.21
  23.9 37.0 %copy-start.18 = (f32[128]{0:T(128)}, f32[128]{0:T(128)S(1)}, u32[]{:S(2)}) copy-start(f32[128]{0:T(128)S(1)} %add_rsqrt_fusion.2) | copy-start | bytes 1540
  62.6 0.6 copy-start.12
  103.0 29.1 %copy-start.3 = (f32[1,128,1536]{2,1,0:T(8,128)S(1)}, f32[1,128,1536]{2,1,0:T(8,128)}, u32[]{:S(2)}) copy-start(f32[1,128,1536]{2,1,0:T(8,128)} %param.30) | copy-start | bytes 2359300
  198.3 1.8 copy-start.7
  241.2 92.0 %copy-start = (f32[96,1280]{1,0:T(8,128)}, f32[96,1280]{1,0:T(8,128)S(1)}, u32[]{:S(2)}) copy-start(f32[96,1280]{1,0:T(8,128)S(1)} %get-tuple-element.129.up_ref) | copy-start | bytes 1474564
  241.3 3.6 copy-start.5
  241.3 3.6 copy-start.23
  285.7 10.8 %copy-start.1 = (f32[32,1536]{1,0:T(8,128)}, f32[32,1536]{1,0:T(8,128)S(1)}, u32[]{:S(2)}) copy-start(f32[32,1536]{1,0:T(8,128)S(1)} %get-tuple-element.135.down_ref) | copy-start | bytes 589828
  286.7 10.0 %copy-start.14 = (f32[22784]{0:T(1024)S(1)}, f32[22784]{0:T(1024)}, u32[]{:S(2)}) copy-start(f32[22784]{0:T(1024)} %custom-call) | copy-start | bytes 273412
  300.1 40.7 %copy-start.13 = (f32[1536]{0:T(1024)S(1)}, f32[1536]{0:T(1024)}, u32[]{:S(2)}) copy-start(f32[1536]{0:T(1024)} %copy-done.12) | copy-start | bytes 18436
  331.8 10.3 %copy-start.22 = (f32[128]{0:T(128)S(1)}, f32[128]{0:T(128)}, u32[]{:S(2)}) copy-start(f32[128]{0:T(128)} %copy-done.21) | copy-start | bytes 1540
  332.5 10.6 %copy-start.19 = (f32[128]{0:T(128)S(1)}, f32[128]{0:T(128)}, u32[]{:S(2)}) copy-start(f32[128]{0:T(128)} %copy-done.18) | copy-start | bytes 1540
  333.9 9.2 %copy-start.4 = (f32[1,128,1536]{2,1,0:T(8,128)S(1)}, f32[1,128,1536]{2,1,0:T(8,128)}, u32[]{:S(2)}) copy-start(f32[1,128,1536]{2,1,0:T(8,128)} %param.30) | copy-start | bytes 2359300
  333.9 9.2 %copy-start.8 = (f32[128,1536]{1,0:T(8,128)S(1)}, f32[128,1536]{1,0:T(8,128)}, u32[]{:S(2)}) copy-start(f32[128,1536]{1,0:T(8,128)} %get-tuple-element.171) | copy-start | bytes 2359300
  333.9 23.9 %collective-permute-start.1 = (bf16[32,1536]{1,0:T(8,128)(2,1)S(1)}, bf16[32,1536]{1,0:T(8,128)(2,1)S(1)}, u32[]{:S(2)}, u32[]{:S(2)}) collective-permute-start(bf16[32,1536]{1,0:T(8,128)(2,1)S(1)} %convert_element_type.143), channel_id=1, source_target_pairs={{0,0},{8,1},{16,2},{24,3},{32,4},{40,5},{48,6},{56,7},{64,8},{72,9... | collective-permute-start | bytes 294920 | tf_op jit(solution)/shard_map/ppermute | solution.py:1734

commit v3 on v2

--- a/solution.py
+++ b/solution.py
@@ -1095,7 +1095,7 @@
 
     lax.fori_loop(0, TILES, rows_step, 0)
     move(proj_ref, proj_any)
-    follow("yyyzz", program, shards)
+    follow("yyyzzz", program, shards)
     padded[0:8] = jnp.zeros((8, 128), FULL)
     for part in range(CONV_HERE // 128):
         at = slice(part * 128, (part + 1) * 128)
@@ -1113,7 +1113,7 @@
         columns,
     )
     move(act_ref, act_any)
-    follow("yyz", program, shards)
+    follow("yy", program, shards)
 
     def pair_step(pair, carry):
         at = pl.ds(pl.multiple_of(pair * 128, 128), 128)
@@ -1763,8 +1763,9 @@
         ],
         axis=1,
     )
+    unit_low, owned_sum = lax.optimization_barrier((unit_grad.astype(LOW), owned_sum))
     normed_grad, column_sum, aux_sum = last_scatter(
-        proj_grad, weights, unit_grad.astype(LOW).reshape(SHARDS, 96, PROJ_HERE), aux_grad
+        proj_grad, weights, unit_low.reshape(SHARDS, 96, PROJ_HERE), aux_grad
     )
     input_from_norm, unused = norm_back(inputs, first_inverse, gain_first, normed_grad)
     hidden_grad = middle_grad + input_from_norm

time: 368 us -> 388 us (1.054)
  local copies, waits for them, and re-layouts: 11.9 us -> 25.1 us
    dot_general x2 -> x3, local copies, waits for them, and re-layouts: 1.31 us -> 8.34 us  [dot_lhs_t(): lax.dot_general(left, right, (((0,), (0,)), ((), ())), preferred_element_...]
    optimization_barrier x0 -> x1, local copies, waits for them, and re-layouts: none -> 6 us  [local(): lax.optimization_barrier((unit_grad.astype(LOW), owned_sum))]
    reduce_sum x0 -> x1, other arithmetic: none -> 4.81 us  [local(): gain_first_grad = jnp.sum(unit_grad * weights.astype(FULL), axis=1)]
  transfers between devices with their start and end apart: 2 -> 2, of which waited for: 0 -> 1; matrix products, arithmetic and copies ran while one was open for 3% -> 2% of each run, Pallas kernels for 6% -> 3%
where the time goes in v3:
time: 388 us; the launch traced here: 382 us
  Pallas kernels  304 us (78%)
  local copies, waits for them, and re-layouts  25.1 us (6%)
  matrix products  20.2 us (5%)
  other arithmetic  16 us (4%)
  starting transfers between devices  12.3 us (3%)
    pallas_call x1, Pallas kernels, experts(): pl.pallas_call(experts_kernel, out_shape=(jax.ShapeDtypeStruct((PIECE, D)...  63.6 us
    pallas_call x1, Pallas kernels, middle_gather(): pl.pallas_call(middle_kernel, out_shape=(jax.ShapeDtypeStruct((GROUPS, ro...  40.5 us
    pallas_call x1, Pallas kernels, mixer_forward(): pl.pallas_call(mixer_forward_kernel, out_shape=(jax.ShapeDtypeStruct((SEQ...  39.3 us
    pallas_call x1, Pallas kernels, mixer_backward(): pl.pallas_call(mixer_backward_kernel, out_shape=(jax.ShapeDtypeStruct((SE...  36.8 us
    pallas_call x1, Pallas kernels, start_gather(): pl.pallas_call(start_kernel, out_shape=(jax.ShapeDtypeStruct((GROUPS, row...  35 us
    pallas_call x1, Pallas kernels, last_scatter(): pl.pallas_call(last_kernel, out_shape=(jax.ShapeDtypeStruct((rows, width)...  33.6 us
    pallas_call x1, Pallas kernels, mixed_scatter(): pl.pallas_call(mixed_kernel, out_shape=(jax.ShapeDtypeStruct((rows, width...  29.7 us
    dot_general x3, matrix products, dot_lhs_t(): lax.dot_general(left, right, (((0,), (0,)), ((), ())), preferred_element_...  14.2 us
  transfers between devices with their start and end apart: 2, of which 1 were waited for; matrix products, arithmetic and copies ran while one was open for 2% of the time, Pallas kernels for 3%

profile of v3, /device:TPU:1, one launch (start us, length us, event | category | flops | bytes accessed | tf_op | source)
XLA Modules:
  0.0 382.1 jit_solution(5143229421842161693)
XLA Ops:
  0.7 1.0 convert_element_type.119
  1.7 0.8 convert_element_type.120
  2.5 6.2 %collective-permute-start = (bf16[32,1536]{1,0:T(8,128)(2,1)S(1)}, bf16[32,1536]{1,0:T(8,128)(2,1)S(1)}, u32[]{:S(2)}, u32[]{:S(2)}) collective-permute-start(bf16[32,1536]{1,0:T(8,128)(2,1)S(1)} %pad_maximum_fusion.2), channel_id=1, source_target_pairs={{0,0},{1,8},{2,16},{3,24},{4,32},{5,40},{6,48},{7,56},{8,64},{9,72... | collective-permute-start | bytes 294920 | tf_op jit(solution)/shard_map/ppermute | solution.py:1627
  8.7 1.0 convert_element_type.115
  10.0 0.1 reshape.308
  10.1 0.1 copy.88
  10.2 0.1 reshape.309
  10.4 0.1 pad_maximum_fusion.4
  10.5 0.8 concatenate.37
  11.3 10.5 %columns_out.1 = bf16[8,12,1408]{2,1,0:T(8,128)(2,1)} custom-call(bf16[8,12,1408]{2,1,0:T(8,128)(2,1)} %bitcast.134), custom_call_target="tpu_custom_call" | custom-call | flops 30000001024 | bytes 4000000 | tf_op jit(solution)/shard_map/columns_out/pallas_call | solution.py:918
  21.9 1.1 reshape.311
  23.1 0.7 slice.173.rest_0_
  23.8 0.1 fusion.7
  24.0 0.9 fusion.8.x_ref
  25.0 0.1 broadcast_in_dim_reshape.3.skip_ref
  25.3 0.6 slice.174.rest_1_
  25.9 35.0 %rows_first.1 = (bf16[8,128,1536]{2,1,0:T(8,128)(2,1)}, bf16[16,96,1152]{2,1,0:T(8,128)(2,1)}, bf16[16,24,1536]{2,1,0:T(8,128)(2,1)}) custom-call(bf16[128,1536]{1,0:T(8,128)(2,1)} %fusion.8.x_ref, bf16[96,1152]{1,0:T(8,128)(2,1)} %slice.173.rest_0_, bf16[24,1536]{1,0:T(8,128)(2,1)} %slice.174.rest_1_), custom_call_target="tpu_custom_call" | custom-call | flops 30000001024 | bytes 4000000 | tf_op jit(solution)/shard_map/rows_first/pallas_call | solution.py:315
  61.0 1.2 slice.175
  62.1 0.2 reshape.314
  62.4 0.2 reshape.334
  62.7 0.1 dynamic_slice.16
  63.0 39.3 %mixer_forward.1 = (bf16[1024,1152]{1,0:T(8,128)(2,1)}, bf16[1024,640]{1,0:T(8,128)(2,1)}, f32[1024,384]{1,0:T(8,128)}, bf16[1024,384]{1,0:T(8,128)(2,1)S(1)}, b...) custom-call(bf16[1024,1536]{1,0:T(8,128)(2,1)} %bitcast.164, ...), custom_call_target="tpu_custom_call" | custom-call | flops 30000001024 | bytes 4000000 | tf_op jit(solution)/shard_map/mixer_forward/pallas_call | solution.py:1178
  102.3 29.7 %mixer_out.1 = (f32[128,1536]{1,0:T(8,128)S(1)}, f32[8,8,128]{2,1,0:T(8,128)S(1)}, bf16[16,96,1024]{2,1,0:T(8,128)(2,1)}, bf16[16,32,1536]{2,1,0:T(8,128)(2,1)}) custom-call(bf16[8,128,1536]{2,1,0:T(8,128)(2,1)} %bitcast.167, f32[8,8,128]{2,1,0:T(8,128)S(1)} %get-tuple-element.102.side_ref, bf16[96,1024]{1,0:T(8,128)(2,1)S(1)} %bitcast.118, ...), custom_call_target="tpu_custom_call" | custom-call | flops 30000001024 | bytes 4000000 | tf_op jit(solution)/shard_map/mixer_out/pallas_call | solution.py:469
  132.0 0.3 multiply_reduce_fusion.4
  132.3 0.1 multiply_convert_fusion.x_ref
  132.5 1.5 fusion.18
  134.1 63.6 %experts.1 = (f32[128,1536]{1,0:T(8,128)S(1)}, f32[8,8,128]{2,1,0:T(8,128)S(1)}, bf16[8,128,1536]{2,1,0:T(8,128)(2,1)}, bf16[1536,1280]{1,0:T(8,128)(2,1)}, bf16...) custom-call(bf16[128,1536]{1,0:T(8,128)(2,1)S(1)} %multiply_convert_fusion.x_ref, f32[8,128]{1,0:T(8,128)S(1)} %bitcast.120, ...), custom_call_target="tpu_custom_call" | custom-call | flops 30000001024 | bytes 4000000 | tf_op jit(solution)/shard_map/experts/pallas_call | solution.py:865
  197.8 1.6 multiply_reduce_fusion.1
  199.5 1.2 multiply_reduce_fusion.2
  200.7 40.5 %rows_mixer.1 = (bf16[8,128,1536]{2,1,0:T(8,128)(2,1)}, f32[8,8,128]{2,1,0:T(8,128)S(1)}, f32[96,1280]{1,0:T(8,128)S(1)}) custom-call(bf16[128,1536]{1,0:T(8,128)(2,1)S(1)} %get-tuple-element.174.x_ref, f32[8,128]{1,0:T(8,128)S(1)} %pad.36.side_ref, bf16[16,96,1280]{2,1,0:T(8,128)(2,1)} %bitcast.163), custom_call_target="tpu_custom_call" | custom-call | flops 30000001024 | bytes 4000000 | tf_op jit(solution)/shard_map/rows_mixer/pallas_call | solution.py:631
  241.3 3.6 convolution_convert_fusion
  244.9 2.9 fusion.3
  247.8 1.3 pad_maximum_fusion.owned_any
  249.1 36.8 %mixer_backward.1 = (bf16[1024,1152]{1,0:T(8,128)(2,1)}, f32[8,640]{1,0:T(8,128)S(1)}, f32[8,384]{1,0:T(8,128)S(1)}, f32[2,8,128]{2,1,0:T(8,128)S(1)}, f32[128,1...) custom-call(bf16[1024,384]{1,0:T(8,128)(2,1)} %get-tuple-element.179.grad_ref, ...), custom_call_target="tpu_custom_call" | custom-call | flops 30000001024 | bytes 4000000 | tf_op jit(solution)/shard_map/mixer_backward/pallas_call | solution.py:1403
  285.9 0.7 copy-done.1
  286.6 0.1 fusion.46
  286.8 10.4 %fusion.38 = (bf16[1536,1152]{0,1:T(8,128)(2,1)}, f32[1536,1152]{0,1:T(8,128)}) fusion(bf16[1024,1536]{1,0:T(8,128)(2,1)} %bitcast.165, bf16[1024,1152]{1,0:T(8,128)(2,1)} %get-tuple-element.125.g_any), kind=kOutput, calls=%fused_computation.108 | convolution fusion | flops 3625648128 | bytes 16121856 | tf_op jit(solution)/shard_map/dot_general | solution.py:1549
  297.3 8.0 %copy.97 = f32[1536,1152]{1,0:T(8,128)} copy(f32[1536,1152]{0,1:T(8,128)} %get-tuple-element.195) | data formatting | bytes 14155776 | tf_op jit(solution)/shard_map/dot_general | solution.py:1549
  305.3 4.8 %multiply_reduce_fusion = f32[1536]{0:T(1024)S(1)} fusion(f32[1536,1152]{1,0:T(8,128)} %copy.97, bf16[16,96,1152]{2,1,0:T(8,128)(2,1)} %get-tuple-element.99), kind=kLoop, calls=%fused_computation | loop fusion | flops 5306880 | bytes 10622976 | tf_op jit(solution)/shard_map/reduce_sum | solution.py:1740
  310.1 0.3 dynamic_update_slice.13
  310.4 0.3 dynamic_update_slice.12
  310.7 0.3 reshape.329
  311.0 0.1 copy.98
  311.1 0.2 copy.99
  311.4 0.1 dot_general.28
  311.5 0.2 convolution_bitcast_fusion
  311.7 0.2 copy.101
  312.1 0.1 reduce_sum.170
  312.2 0.1 slice_reduce_fusion.1
  312.4 0.1 dynamic_update_slice.15
  312.6 6.0 %collective-permute-start.1 = (bf16[32,1536]{1,0:T(8,128)(2,1)S(1)}, bf16[32,1536]{1,0:T(8,128)(2,1)S(1)}, u32[]{:S(2)}, u32[]{:S(2)}) collective-permute-start(bf16[32,1536]{1,0:T(8,128)(2,1)S(1)} %convert_element_type.137), channel_id=1, source_target_pairs={{0,0},{8,1},{16,2},{24,3},{32,4},{40,5},{48,6},{56,7},{64,8},{72,9... | collective-permute-start | bytes 294920 | tf_op jit(solution)/shard_map/ppermute | solution.py:1734
  318.7 0.6 reshape.332.u_ref
  319.4 0.7 copy.102.gain_ref
  320.1 1.0 add_bitcast_fusion
  321.1 2.2 collective-permute-done.1
  323.3 0.7 convert_element_type.138.owned_ref
  324.0 6.0 %copy.96 = bf16[1536,1152]{1,0:T(8,128)(2,1)} copy(bf16[1536,1152]{0,1:T(8,128)(2,1)} %get-tuple-element.127) | data formatting | bytes 7077888 | tf_op jit(solution)/shard_map/optimization_barrier | solution.py:1766
  330.0 33.6 %rows_last.1 = (f32[128,1536]{1,0:T(8,128)S(1)}, f32[96,1152]{1,0:T(8,128)S(1)}, f32[96,128]{1,0:T(8,128)S(1)}) custom-call(bf16[1024,1152]{1,0:T(8,128)(2,1)} %get-tuple-element.125.g_any, bf16[1536,1152]{1,0:T(8,128)(2,1)} %bitcast.126, bf16[16,96,1152]{2,1,0:T(8,128)(2,1)} %bitcast.128, bf16[16,96,128]{2,1,0:T(8,128)(2,1)S(1)} %pad_maximum_fusion.1.a_ref), custom_call_target="tpu_custom_call" | custom-call | flops 30000001024 | bytes 4000000 | tf_op jit(solution)/shard_map/rows_last/pallas_call | solution.py:580
  363.7 0.6 bitcast_add_fusion.2.side_ref
  364.3 0.8 reshape.331.x_ref
  365.1 0.2 fusion.9
  365.3 1.1 fusion.12
  366.4 9.1 %columns_back.1 = (bf16[8,12,1152]{2,1,0:T(8,128)(2,1)}, bf16[8,12,256]{2,1,0:T(8,128)(2,1)}, f32[8,8,128]{2,1,0:T(8,128)}) custom-call(bf16[8,12,1152]{2,1,0:T(8,128)(2,1)} %reshape.331.x_ref, bf16[8,12,256]{2,1,0:T(8,128)(2,1)} %reshape.332.u_ref, f32[8,8,128]{2,1,0:T(8,128)} %bitcast_add_fusion.2.side_ref), custom_call_target="tpu_custom_call" | custom-call | flops 30000001024 | bytes 4000000 | tf_op jit(solution)/shard_map/columns_back/pallas_call | solution.py:942
  375.5 6.3 %update.1 = (f32[12,6448]{1,0:T(8,128)}, f32[12,6448]{1,0:T(8,128)}, f32[12,6448]{1,0:T(8,128)}, f32[12,2048]{1,0:T(8,128)}, f32[12,2048]{1,0:T(8,128)}, /*index...) custom-call(bf16[8,12,1152]{2,1,0:T(8,128)(2,1)} %get-tuple-element., ...), custom_call_target="tpu_custom_call" | custom-call | tf_op jit(solution)/shard_map/update/pallas_call | solution.py:1512
  (147 shorter events, 1.6 us)
Async XLA Ops:
  0.7 9.3 %copy-start.11 = (f32[12,2048]{1,0:T(8,128)S(1)}, f32[12,2048]{1,0:T(8,128)}, u32[]{:S(2)}) copy-start(f32[12,2048]{1,0:T(8,128)} %refs_3_.1) | copy-start | bytes 294916
  0.7 9.4 %copy-start.15 = (f32[12,8]{0,1:T(8,128)S(1)}, f32[12,8]{0,1:T(8,128)}, u32[]{:S(2)}) copy-start(f32[12,8]{0,1:T(8,128)} %param.45) | copy-start | bytes 1156
  0.7 9.5 %copy-start.20 = (f32[178]{0:T(256)S(1)}, f32[178]{0:T(256)}, u32[]{:S(2)}) copy-start(f32[178]{0:T(256)} %param.36) | copy-start | bytes 2140
  2.5 22.8 %collective-permute-start = (bf16[32,1536]{1,0:T(8,128)(2,1)S(1)}, bf16[32,1536]{1,0:T(8,128)(2,1)S(1)}, u32[]{:S(2)}, u32[]{:S(2)}) collective-permute-start(bf16[32,1536]{1,0:T(8,128)(2,1)S(1)} %pad_maximum_fusion.2), channel_id=1, source_target_pairs={{0,0},{1,8},{2,16},{3,24},{4,32},{5,40},{6,48},{7,56},{8,64},{9,72... | collective-permute-start | bytes 294920 | tf_op jit(solution)/shard_map/ppermute | solution.py:1627
  11.3 12.5 %copy-start.2 = (f32[1,128,1536]{2,1,0:T(8,128)S(1)}, f32[1,128,1536]{2,1,0:T(8,128)}, u32[]{:S(2)}) copy-start(f32[1,128,1536]{2,1,0:T(8,128)} %param.30) | copy-start | bytes 2359300
  21.9 3.0 copy-start.16
  21.9 3.2 copy-start.6
  21.9 3.2 copy-start.9
  21.9 3.3 copy-start.10
  23.1 2.2 copy-start.17
  23.9 0.9 copy-start.21
  23.9 0.9 copy-start.18
  62.6 39.7 %copy-start.12 = (f32[1536]{0:T(1024)}, f32[1536]{0:T(1024)S(1)}, u32[]{:S(2)}) copy-start(f32[1536]{0:T(1024)S(1)} %get-tuple-element.183) | copy-start | bytes 18436
  102.3 29.7 %copy-start.3 = (f32[1,128,1536]{2,1,0:T(8,128)S(1)}, f32[1,128,1536]{2,1,0:T(8,128)}, u32[]{:S(2)}) copy-start(f32[1,128,1536]{2,1,0:T(8,128)} %param.30) | copy-start | bytes 2359300
  197.7 1.8 copy-start.7
  241.2 77.4 %copy-start = (f32[96,1280]{1,0:T(8,128)}, f32[96,1280]{1,0:T(8,128)S(1)}, u32[]{:S(2)}) copy-start(f32[96,1280]{1,0:T(8,128)S(1)} %get-tuple-element.133.up_ref) | copy-start | bytes 1474564
  241.2 3.6 copy-start.5
  241.3 3.6 copy-start.23
  285.9 0.7 copy-start.1
  305.3 5.1 %copy-start.14 = (f32[22784]{0:T(1024)S(1)}, f32[22784]{0:T(1024)}, u32[]{:S(2)}) copy-start(f32[22784]{0:T(1024)} %custom-call) | copy-start | bytes 273412
  310.1 9.2 %copy-start.13 = (f32[1536]{0:T(1024)S(1)}, f32[1536]{0:T(1024)}, u32[]{:S(2)}) copy-start(f32[1536]{0:T(1024)} %copy-done.12) | copy-start | bytes 18436
  312.6 10.7 %collective-permute-start.1 = (bf16[32,1536]{1,0:T(8,128)(2,1)S(1)}, bf16[32,1536]{1,0:T(8,128)(2,1)S(1)}, u32[]{:S(2)}, u32[]{:S(2)}) collective-permute-start(bf16[32,1536]{1,0:T(8,128)(2,1)S(1)} %convert_element_type.137), channel_id=1, source_target_pairs={{0,0},{8,1},{16,2},{24,3},{32,4},{40,5},{48,6},{56,7},{64,8},{72,9... | collective-permute-start | bytes 294920 | tf_op jit(solution)/shard_map/ppermute | solution.py:1734
  330.0 35.1 %copy-start.4 = (f32[1,128,1536]{2,1,0:T(8,128)S(1)}, f32[1,128,1536]{2,1,0:T(8,128)}, u32[]{:S(2)}) copy-start(f32[1,128,1536]{2,1,0:T(8,128)} %param.30) | copy-start | bytes 2359300
  363.6 1.7 copy-start.22
  363.6 1.7 copy-start.8
  363.6 1.7 copy-start.19
